TPU v7x, 256 devices: a whole 4x4x8 slice. The times are simulated.
256 devices in a mesh: field: 4 (over x), cross: 64 (over y, z, core).
Axes of the slice: x: 4, y: 4, z: 8, core: 2. Of those that a mesh axis runs over, the one named last changes fastest.
Arguments:
- rhs: float32 [4, 64, 8192], P('field', None, 'cross'), may hold values from -12 to 12
- pivot_inverse: bfloat16 [4, 64, 64, 8192], P('field', None, None, 'cross'), as said below
- line_coupling: bfloat16 [4, 64, 64, 8192], P('field', None, None, 'cross'), as said below
- element_block: bfloat16 [4, 64, 64, 8192], P('field', None, None, 'cross'), as said below
- neighbours: int32 [8192, 4], P('cross'), may hold values from 0 to 8191, as said below
- face_type: int32 [8192, 4], P('cross'), may hold values from 0 to 2, as said below
Outputs:
- solution: float32 [4, 64, 8192], P('field', None, 'cross')
- residual: float32 [4, 64, 8192], P('field', None, 'cross')
- precond: float32 [4, 64, 8192], P('field', None, 'cross')
Inputs may be any that keep to these rules, and one draw needn't show every extreme that they name: `neighbours`: the lines form a grid of 256 x 32; the lines of cross index c lie in grid columns c * 4 to (c + 1) * 4 - 1, in a scrambled order within the device, and a line's number is c * 128 + its slot. Faces 0 and 1 name the line one column down and up, faces 2 and 3 one row down and up; a face on the duct's wall names the line itself. Neighbours are mutual. `face_type`: 0 on faces between two lines, 1 (conducting wall) or 2 (insulating wall) on faces of the duct's wall, where neighbours names the line itself. `pivot_inverse`: symmetric with a dominant positive diagonal. `line_coupling`: together with element_block, the operator's line part is symmetric positive definite. `element_block`: symmetric with a dominant positive diagonal.
All inputs are finite; a program needn't handle non-finite values.
Results may differ from a plain program's by a relative error of at most 0.018.
Values may be sent and summed in bfloat16 or wider, within the bound.
No kernel may reach another device: no remote copies, remote signals or barrier semaphores. Data moves between devices by JAX's collectives and lax.ppermute only.
A program may use at most 128 MiB of HBM per device.

v0:
```python
import jax
import jax.numpy as jnp
from jax import lax
from jax.sharding import PartitionSpec as P

ITERS = 2


highest = lax.Precision.HIGHEST
penalty = 2.0


def shortened(shard):

    def short(part):
        return part.astype(jnp.bfloat16) if part.dtype == jnp.float32 else part

    return jax.tree.map(short, shard)


def shifted(value, axis, steps):
    count = lax.axis_size(axis)
    initial, last = (max(0, -steps), min(count, count - steps))
    return lax.ppermute(value, axis, [(source, source + steps) for source in range(initial, last)])


def apply_block(matrix, vector):
    return jnp.einsum("abl,bl->al", matrix.astype(jnp.float32), vector, precision=highest)


def apply_transpose(matrix, vector):
    return jnp.einsum("bal,bl->al", matrix.astype(jnp.float32), vector, precision=highest)


def compose(left, right):
    return jnp.einsum("abl,bcl->acl", left.astype(jnp.float32), right, precision=highest)


def compose_transpose(left, right):
    return jnp.einsum("bal,bcl->acl", left.astype(jnp.float32), right, precision=highest)


def identity_maps(lines):
    return jnp.broadcast_to(jnp.eye(64, dtype=jnp.float32)[:, :, None], (64, 64, lines))


def forward_sweep(residual, pivots, coupling, incoming):
    previous = incoming
    previous = apply_block(pivots[0], residual[0] - apply_block(coupling[0], previous))
    values = [previous]
    return (jnp.stack(values), previous)


def backward_sweep(forward_vals, pivots, coupling, incoming):
    count = forward_vals.shape[0]
    carried = incoming
    values = [None] * count
    for elem in reversed(range(count)):
        value = forward_vals[elem] - apply_block(pivots[elem], carried)
        values[elem] = value
        carried = apply_transpose(coupling[elem], value)
    return (jnp.stack(values), carried)


def segment_responses(pivots, coupling):
    count = pivots.shape[0]
    current = identity_maps(pivots.shape[3])
    current = -compose(pivots[0], compose(coupling[0], current))
    forward_maps = [current]
    backward_maps = [None] * count
    current = -pivots[count - 1].astype(jnp.float32)
    backward_maps[count - 1] = current
    leaving = compose_transpose(coupling[0], current)
    return (forward_maps, backward_maps, leaving)


def operate(vector, blocks, coupling, neighbours, face_type):
    count = vector.shape[0]
    lines = vector.shape[2]
    below = shifted(shortened(vector[count - 1]), "field", 1)
    lifted = apply_transpose(coupling[0], vector[0])
    above = shifted(shortened(lifted), "field", -1)
    total = apply_block(blocks[0], vector[0])
    total = total + apply_block(coupling[0], below)
    rows = [total + above]
    line_part = jnp.stack(rows)
    cube = vector.reshape(count, 4, 4, 4, lines)
    upper_faces = cube[:, 3]
    lower_faces = cube[:, 0]
    from_left = shifted(upper_faces, "cross", 1)
    from_right = shifted(lower_faces, "cross", -1)
    offset = lax.axis_index("cross") * lines
    interior = (face_type == 0).astype(jnp.float32) * penalty
    own_weight = interior + (face_type == 1).astype(jnp.float32) * (2.0 * penalty)
    near0 = jnp.take(
        jnp.concatenate([from_left, upper_faces], axis=3), neighbours[:, 0] - offset + lines, axis=3
    )
    near1 = jnp.take(
        jnp.concatenate([lower_faces, from_right], axis=3), neighbours[:, 1] - offset, axis=3
    )
    near2 = jnp.take(cube[:, :, 3], neighbours[:, 2] - offset, axis=3)
    near3 = jnp.take(cube[:, :, 0], neighbours[:, 3] - offset, axis=3)
    term0 = own_weight[:, 0] * lower_faces - interior[:, 0] * near0
    term1 = own_weight[:, 1] * upper_faces - interior[:, 1] * near1
    term2 = own_weight[:, 2] * cube[:, :, 0] - interior[:, 2] * near2
    term3 = own_weight[:, 3] * cube[:, :, 3] - interior[:, 3] * near3
    faces = jnp.zeros_like(cube)
    faces = faces.at[:, 0].add(term0).at[:, 3].add(term1)
    faces = faces.at[:, :, 0].add(term2).at[:, :, 3].add(term3)
    return line_part + faces.reshape(count, 64, lines)


def inner_product(first, second):
    return lax.psum(jnp.sum(first * second), ("field", "cross"))


def local(rhs, pivot_inverse, line_coupling, element_block, neighbours, face_type):
    lines = rhs.shape[2]
    zeros = jnp.zeros((64, lines), jnp.float32)
    forward_maps, backward_maps, leaving = segment_responses(pivot_inverse, line_coupling)
    crossing = forward_maps[-1]

    def precondition(residual):
        forward_vals, last = forward_sweep(residual, pivot_inverse, line_coupling, zeros)
        entering = zeros
        for turn in range(lax.axis_size("field") - 1):
            entering = shifted(last + apply_block(crossing, entering), "field", 1)
        forward_vals = forward_vals + jnp.stack([apply_block(forward_maps[0], entering)])
        smoothed, carried = backward_sweep(forward_vals, pivot_inverse, line_coupling, zeros)
        entering = zeros
        for turn in range(lax.axis_size("field") - 1):
            entering = shifted(carried + apply_block(leaving, entering), "field", -1)
        return smoothed + jnp.stack([apply_block(backward_maps[0], entering)])

    solution = jnp.zeros_like(rhs)
    residual = rhs
    precond = precondition(residual)
    direction = precond
    rho = inner_product(residual, precond)
    for turn in range(ITERS):
        image = operate(direction, element_block, line_coupling, neighbours, face_type)
        alpha = rho / inner_product(direction, image)
        solution = solution + alpha * direction
        residual = residual - alpha * image
        precond = precondition(residual)
        if turn + 1 < ITERS:
            rho_next = inner_product(residual, precond)
            direction = precond + rho_next / rho * direction
            rho = rho_next
    return (solution, residual, precond)


def solution(mesh):
    placed = (
        P("field", None, "cross"),
        P("field", None, None, "cross"),
        P("field", None, None, "cross"),
        P("field", None, None, "cross"),
        P("cross", None),
        P("cross", None),
    )
    return jax.shard_map(
        local,
        mesh=mesh,
        in_specs=placed,
        out_specs=(P("field", None, "cross"), P("field", None, "cross"), P("field", None, "cross")),
        check_vma=False,
    )
```

profile of v0, /device:TPU:2, one launch (start us, length us, event | category | flops | bytes accessed | tf_op | source)
XLA Modules:
  0.0 511.6 jit_solution(9837103909800287120)
XLA Ops:
  2.3 4.7 copy.157
  7.0 3.8 copy.158
  10.8 5.2 %fusion.30 = f32[128,64,64]{2,1,0:T(8,128)S(1)} fusion(bf16[64,64,128]{1,0,2:T(8,128)(2,1)} %copy.157, f32[64,64]{0,1:T(8,128)S(1)} %fusion.41), kind=kOutput, calls=%fused_computation.58 | convolution fusion | flops 402653184 | bytes 3162112 | tf_op jit(solution)/shard_map/abl,bcl->acl/dot_general | solution.py:36
  16.0 5.0 multiply_reduce_fusion.9
  27.1 5.6 %copy.159 = f32[64,64,128]{0,1,2:T(8,128)} copy(f32[64,64,128]{2,1,0:T(8,128)} %convert_negate_fusion) | data formatting | bytes 4194304 | tf_op jit(solution)/shard_map/neg | solution.py:71
  32.7 5.3 %fusion.81 = f32[128,64,64]{2,1,0:T(8,128)S(1)} fusion(f32[64,64,128]{0,1,2:T(8,128)} %copy.159, bf16[64,64,128]{1,0,2:T(8,128)(2,1)} %copy.157), kind=kOutput, calls=%fused_computation.199 | convolution fusion | flops 402653184 | bytes 5242880 | tf_op jit(solution)/shard_map/bal,bcl->acl/dot_general | solution.py:40
  70.3 3.8 collective-permute-done.3
  74.1 5.4 %fusion.10 = f32[128,1,64]{2,1,0:T(1,128)S(1)} fusion(f32[64,128,1]{0,2,1:T(1,128)S(1)} %bitcast.569, f32[128,64,64]{2,1,0:T(8,128)} %copy-done), kind=kOutput, calls=%fused_computation.18 | convolution fusion | flops 6291456 | bytes 2162688 | tf_op jit(solution)/shard_map/abl,bl->al/dot_general | solution.py:28
  81.5 4.2 collective-permute-done.4
  85.8 3.7 fusion.8
  91.4 4.2 collective-permute-done.5
  95.6 3.7 fusion.82
  132.7 78.7 %all-reduce.2 = (f32[]{:T(128)}, f32[]{:T(128)}) all-reduce(f32[]{:T(128)} %get-tuple-element.115, f32[]{:T(128)} %get-tuple-element.113), channel_id=1, replica_groups=mesh['field'=4,'cross'=64] {'field','cross'}, use_global_device_ids=true, to_apply=%region_1.0 | all-reduce | flops 2 | bytes 16 | tf_op jit(solution)/shard_map/psum | solution.py:114
  249.6 4.2 collective-permute-done.13
  253.8 5.4 %fusion.6 = f32[128,1,64]{2,1,0:T(1,128)S(1)} fusion(f32[64,128,1]{0,2,1:T(1,128)S(1)} %bitcast.573, f32[128,64,64]{2,1,0:T(8,128)} %copy-done), kind=kOutput, calls=%fused_computation.14 | convolution fusion | flops 6291456 | bytes 2162688 | tf_op jit(solution)/shard_map/abl,bl->al/dot_general | solution.py:28
  261.4 4.0 collective-permute-done.14
  265.4 3.7 fusion.4
  271.1 4.2 collective-permute-done.15
  275.3 3.7 fusion.84
  279.7 70.9 %psum.30 = f32[]{:T(128)} all-reduce(f32[]{:T(128)} %fusion.36), channel_id=1, replica_groups=mesh['field'=4,'cross'=64] {'field','cross'}, use_global_device_ids=true, to_apply=%region_5.8 | all-reduce | flops 1 | bytes 8 | tf_op jit(solution)/shard_map/psum | solution.py:114
  371.0 77.2 %psum.31 = f32[]{:T(128)} all-reduce(f32[]{:T(128)} %get-tuple-element.107), channel_id=1, replica_groups=mesh['field'=4,'cross'=64] {'field','cross'}, use_global_device_ids=true, to_apply=%region_7.10 | all-reduce | flops 1 | bytes 8 | tf_op jit(solution)/shard_map/psum | solution.py:114
  481.0 4.2 collective-permute-done.23
  485.3 5.4 %fusion.2 = f32[128,1,64]{2,1,0:T(1,128)S(1)} fusion(f32[64,128,1]{0,2,1:T(1,128)S(1)} %bitcast.576, f32[128,64,64]{2,1,0:T(8,128)} %copy-done), kind=kOutput, calls=%fused_computation.10 | convolution fusion | flops 6291456 | bytes 2162688 | tf_op jit(solution)/shard_map/abl,bl->al/dot_general | solution.py:28
  492.6 4.2 collective-permute-done.24
  (209 shorter events, 185.0 us)
Async XLA Ops:
  21.8 21.8 %collective-permute-start = (f32[64,128]{1,0:T(8,128)S(1)}, f32[64,128]{1,0:T(8,128)S(1)}, u32[]{:S(2)}, u32[]{:S(2)}) collective-permute-start(f32[64,128]{1,0:T(8,128)S(1)} %add_bitcast_fusion.18), channel_id=1, source_target_pairs={{0,64},{64,128},{128,192},{1,65},{65,129},{129,193},{2,66},{66,130... | collective-permute-start | bytes 98312 | tf_op jit(solution)/shard_map/ppermute | solution.py:24
  46.7 5.8 %collective-permute-start.1 = (f32[64,128]{1,0:T(8,128)S(1)}, f32[64,128]{1,0:T(8,128)S(1)}, u32[]{:S(2)}, u32[]{:S(2)}) collective-permute-start(f32[64,128]{1,0:T(8,128)S(1)} %add_bitcast_fusion.17), channel_id=1, source_target_pairs={{0,64},{64,128},{128,192},{1,65},{65,129},{129,193},{2,66},{66,130... | collective-permute-start | bytes 98312 | tf_op jit(solution)/shard_map/ppermute | solution.py:24
  55.5 5.8 %collective-permute-start.2 = (f32[64,128]{1,0:T(8,128)S(1)}, f32[64,128]{1,0:T(8,128)S(1)}, u32[]{:S(2)}, u32[]{:S(2)}) collective-permute-start(f32[64,128]{1,0:T(8,128)S(1)} %add_bitcast_fusion.16), channel_id=1, source_target_pairs={{0,64},{64,128},{128,192},{1,65},{65,129},{129,193},{2,66},{66,130... | collective-permute-start | bytes 98312 | tf_op jit(solution)/shard_map/ppermute | solution.py:24
  68.0 6.2 %collective-permute-start.3 = (f32[64,128]{0,1:T(8,128)S(1)}, f32[64,128]{0,1:T(8,128)S(1)}, u32[]{:S(2)}, u32[]{:S(2)}) collective-permute-start(f32[64,128]{0,1:T(8,128)S(1)} %add_bitcast_fusion.8), channel_id=1, source_target_pairs={{64,0},{128,64},{192,128},{65,1},{129,65},{193,129},{66,2},{130,66... | collective-permute-start | bytes 98312 | tf_op jit(solution)/shard_map/ppermute | solution.py:24
  79.6 6.2 %collective-permute-start.4 = (f32[64,128]{0,1:T(8,128)S(1)}, f32[64,128]{0,1:T(8,128)S(1)}, u32[]{:S(2)}, u32[]{:S(2)}) collective-permute-start(f32[64,128]{0,1:T(8,128)S(1)} %add_bitcast_fusion.7), channel_id=1, source_target_pairs={{64,0},{128,64},{192,128},{65,1},{129,65},{193,129},{66,2},{130,66... | collective-permute-start | bytes 98312 | tf_op jit(solution)/shard_map/ppermute | solution.py:24
  89.5 6.2 %collective-permute-start.5 = (f32[64,128]{0,1:T(8,128)S(1)}, f32[64,128]{0,1:T(8,128)S(1)}, u32[]{:S(2)}, u32[]{:S(2)}) collective-permute-start(f32[64,128]{0,1:T(8,128)S(1)} %add_bitcast_fusion.6), channel_id=1, source_target_pairs={{64,0},{128,64},{192,128},{65,1},{129,65},{193,129},{66,2},{130,66... | collective-permute-start | bytes 98312 | tf_op jit(solution)/shard_map/ppermute | solution.py:24
  100.0 15.3 %collective-permute-start.9 = (f32[1,4,4,128]{3,2,1,0:T(4,128)S(1)}, f32[1,4,4,128]{3,2,1,0:T(4,128)S(1)}, u32[]{:S(2)}, u32[]{:S(2)}) collective-permute-start(f32[1,4,4,128]{3,2,1,0:T(4,128)S(1)} %get-tuple-element.131), channel_id=1, source_target_pairs={{1,0},{2,1},{3,2},{4,3},{5,4},{6,5},{7,6},{8,7},{9,8},{10,9},{11,1... | collective-permute-start | bytes 24584 | tf_op jit(solution)/shard_map/ppermute | solution.py:24
  101.3 18.6 %collective-permute-start.8 = (f32[1,4,4,128]{3,2,1,0:T(4,128)S(1)}, f32[1,4,4,128]{3,2,1,0:T(4,128)S(1)}, u32[]{:S(2)}, u32[]{:S(2)}) collective-permute-start(f32[1,4,4,128]{3,2,1,0:T(4,128)S(1)} %get-tuple-element.132), channel_id=1, source_target_pairs={{0,1},{1,2},{2,3},{3,4},{4,5},{5,6},{6,7},{7,8},{8,9},{9,10},{10,1... | collective-permute-start | bytes 24584 | tf_op jit(solution)/shard_map/ppermute | solution.py:24
  104.4 27.3 %collective-permute-start.6 = (bf16[64,128]{1,0:T(8,128)(2,1)S(1)}, bf16[64,128]{1,0:T(8,128)(2,1)S(1)}, u32[]{:S(2)}, u32[]{:S(2)}) collective-permute-start(bf16[64,128]{1,0:T(8,128)(2,1)S(1)} %convert_element_type.28), channel_id=1, source_target_pairs={{0,64},{64,128},{128,192},{1,65},{65,129},{129,193},{2,66},{66,130... | collective-permute-start | bytes 49160 | tf_op jit(solution)/shard_map/ppermute | solution.py:24
  107.8 24.3 %collective-permute-start.7 = (bf16[64,128]{1,0:T(8,128)(2,1)S(1)}, bf16[64,128]{1,0:T(8,128)(2,1)S(1)}, u32[]{:S(2)}, u32[]{:S(2)}) collective-permute-start(bf16[64,128]{1,0:T(8,128)(2,1)S(1)} %bitcast.587), channel_id=1, source_target_pairs={{64,0},{128,64},{192,128},{65,1},{129,65},{193,129},{66,2},{130,66... | collective-permute-start | bytes 49160 | tf_op jit(solution)/shard_map/ppermute | solution.py:24
  213.1 5.8 %collective-permute-start.10 = (f32[64,128]{1,0:T(8,128)S(1)}, f32[64,128]{1,0:T(8,128)S(1)}, u32[]{:S(2)}, u32[]{:S(2)}) collective-permute-start(f32[64,128]{1,0:T(8,128)S(1)} %add_bitcast_fusion.15), channel_id=1, source_target_pairs={{0,64},{64,128},{128,192},{1,65},{65,129},{129,193},{2,66},{66,130... | collective-permute-start | bytes 98312 | tf_op jit(solution)/shard_map/ppermute | solution.py:24
  223.4 5.8 %collective-permute-start.11 = (f32[64,128]{1,0:T(8,128)S(1)}, f32[64,128]{1,0:T(8,128)S(1)}, u32[]{:S(2)}, u32[]{:S(2)}) collective-permute-start(f32[64,128]{1,0:T(8,128)S(1)} %add_bitcast_fusion.14), channel_id=1, source_target_pairs={{0,64},{64,128},{128,192},{1,65},{65,129},{129,193},{2,66},{66,130... | collective-permute-start | bytes 98312 | tf_op jit(solution)/shard_map/ppermute | solution.py:24
  233.7 5.8 %collective-permute-start.12 = (f32[64,128]{1,0:T(8,128)S(1)}, f32[64,128]{1,0:T(8,128)S(1)}, u32[]{:S(2)}, u32[]{:S(2)}) collective-permute-start(f32[64,128]{1,0:T(8,128)S(1)} %add_bitcast_fusion.13), channel_id=1, source_target_pairs={{0,64},{64,128},{128,192},{1,65},{65,129},{129,193},{2,66},{66,130... | collective-permute-start | bytes 98312 | tf_op jit(solution)/shard_map/ppermute | solution.py:24
  247.6 6.2 %collective-permute-start.13 = (f32[64,128]{0,1:T(8,128)S(1)}, f32[64,128]{0,1:T(8,128)S(1)}, u32[]{:S(2)}, u32[]{:S(2)}) collective-permute-start(f32[64,128]{0,1:T(8,128)S(1)} %add_bitcast_fusion.5), channel_id=1, source_target_pairs={{64,0},{128,64},{192,128},{65,1},{129,65},{193,129},{66,2},{130,66... | collective-permute-start | bytes 98312 | tf_op jit(solution)/shard_map/ppermute | solution.py:24
  259.3 6.2 %collective-permute-start.14 = (f32[64,128]{0,1:T(8,128)S(1)}, f32[64,128]{0,1:T(8,128)S(1)}, u32[]{:S(2)}, u32[]{:S(2)}) collective-permute-start(f32[64,128]{0,1:T(8,128)S(1)} %add_bitcast_fusion.4), channel_id=1, source_target_pairs={{64,0},{128,64},{192,128},{65,1},{129,65},{193,129},{66,2},{130,66... | collective-permute-start | bytes 98312 | tf_op jit(solution)/shard_map/ppermute | solution.py:24
  269.1 6.2 %collective-permute-start.15 = (f32[64,128]{0,1:T(8,128)S(1)}, f32[64,128]{0,1:T(8,128)S(1)}, u32[]{:S(2)}, u32[]{:S(2)}) collective-permute-start(f32[64,128]{0,1:T(8,128)S(1)} %add_bitcast_fusion.3), channel_id=1, source_target_pairs={{64,0},{128,64},{192,128},{65,1},{129,65},{193,129},{66,2},{130,66... | collective-permute-start | bytes 98312 | tf_op jit(solution)/shard_map/ppermute | solution.py:24
  352.0 12.9 %collective-permute-start.19 = (f32[1,4,4,128]{3,2,1,0:T(4,128)S(1)}, f32[1,4,4,128]{3,2,1,0:T(4,128)S(1)}, u32[]{:S(2)}, u32[]{:S(2)}) collective-permute-start(f32[1,4,4,128]{3,2,1,0:T(4,128)S(1)} %get-tuple-element.127), channel_id=1, source_target_pairs={{1,0},{2,1},{3,2},{4,3},{5,4},{6,5},{7,6},{8,7},{9,8},{10,9},{11,1... | collective-permute-start | bytes 24584 | tf_op jit(solution)/shard_map/ppermute | solution.py:24
  353.9 12.2 %collective-permute-start.18 = (f32[1,4,4,128]{3,2,1,0:T(4,128)S(1)}, f32[1,4,4,128]{3,2,1,0:T(4,128)S(1)}, u32[]{:S(2)}, u32[]{:S(2)}) collective-permute-start(f32[1,4,4,128]{3,2,1,0:T(4,128)S(1)} %get-tuple-element.128), channel_id=1, source_target_pairs={{0,1},{1,2},{2,3},{3,4},{4,5},{5,6},{6,7},{7,8},{8,9},{9,10},{10,1... | collective-permute-start | bytes 24584 | tf_op jit(solution)/shard_map/ppermute | solution.py:24
  359.1 10.9 %collective-permute-start.16 = (bf16[64,128]{1,0:T(8,128)(2,1)S(1)}, bf16[64,128]{1,0:T(8,128)(2,1)S(1)}, u32[]{:S(2)}, u32[]{:S(2)}) collective-permute-start(bf16[64,128]{1,0:T(8,128)(2,1)S(1)} %get-tuple-element.109), channel_id=1, source_target_pairs={{0,64},{64,128},{128,192},{1,65},{65,129},{129,193},{2,66},{66,130... | collective-permute-start | bytes 49160 | tf_op jit(solution)/shard_map/ppermute | solution.py:24
  362.7 7.6 %collective-permute-start.17 = (bf16[64,128]{1,0:T(8,128)(2,1)S(1)}, bf16[64,128]{1,0:T(8,128)(2,1)S(1)}, u32[]{:S(2)}, u32[]{:S(2)}) collective-permute-start(bf16[64,128]{1,0:T(8,128)(2,1)S(1)} %bitcast.586), channel_id=1, source_target_pairs={{64,0},{128,64},{192,128},{65,1},{129,65},{193,129},{66,2},{130,66... | collective-permute-start | bytes 49160 | tf_op jit(solution)/shard_map/ppermute | solution.py:24
  450.5 5.8 %collective-permute-start.20 = (f32[64,128]{1,0:T(8,128)S(1)}, f32[64,128]{1,0:T(8,128)S(1)}, u32[]{:S(2)}, u32[]{:S(2)}) collective-permute-start(f32[64,128]{1,0:T(8,128)S(1)} %add_bitcast_fusion.11), channel_id=1, source_target_pairs={{0,64},{64,128},{128,192},{1,65},{65,129},{129,193},{2,66},{66,130... | collective-permute-start | bytes 98312 | tf_op jit(solution)/shard_map/ppermute | solution.py:24
  479.1 6.2 %collective-permute-start.23 = (f32[64,128]{0,1:T(8,128)S(1)}, f32[64,128]{0,1:T(8,128)S(1)}, u32[]{:S(2)}, u32[]{:S(2)}) collective-permute-start(f32[64,128]{0,1:T(8,128)S(1)} %add_bitcast_fusion.2), channel_id=1, source_target_pairs={{64,0},{128,64},{192,128},{65,1},{129,65},{193,129},{66,2},{130,66... | collective-permute-start | bytes 98312 | tf_op jit(solution)/shard_map/ppermute | solution.py:24
  490.7 6.2 %collective-permute-start.24 = (f32[64,128]{0,1:T(8,128)S(1)}, f32[64,128]{0,1:T(8,128)S(1)}, u32[]{:S(2)}, u32[]{:S(2)}) collective-permute-start(f32[64,128]{0,1:T(8,128)S(1)} %add_bitcast_fusion.1), channel_id=1, source_target_pairs={{64,0},{128,64},{192,128},{65,1},{129,65},{193,129},{66,2},{130,66... | collective-permute-start | bytes 98312 | tf_op jit(solution)/shard_map/ppermute | solution.py:24
  500.6 6.2 %collective-permute-start.25 = (f32[64,128]{0,1:T(8,128)S(1)}, f32[64,128]{0,1:T(8,128)S(1)}, u32[]{:S(2)}, u32[]{:S(2)}) collective-permute-start(f32[64,128]{0,1:T(8,128)S(1)} %add_bitcast_fusion), channel_id=1, source_target_pairs={{64,0},{128,64},{192,128},{65,1},{129,65},{193,129},{66,2},{130,66... | collective-permute-start | bytes 98312 | tf_op jit(solution)/shard_map/ppermute | solution.py:24
  (17 other events, 234.1 us)
where the time goes:
time: 519 us; the launch traced here: 512 us
  blocking collectives  227 us (44%)
  matrix products  66.2 us (13%)
  starting transfers between devices  64.4 us (12%)
  waiting for transfers between devices  59.7 us (12%)
  other arithmetic  45.3 us (9%)
  local copies, waits for them, and re-layouts  43.2 us (8%)
  between operations  6.1 us (1%)
    psum x3, blocking collectives, inner_product(): return lax.psum(jnp.sum(first * second), ('field', 'cross'))  227 us
    ppermute x26, starting transfers between devices, shifted(): lax.ppermute(value, axis, [(source, source + steps) for source in range(i...  64.4 us
    ppermute x26, waiting for transfers between devices, shifted(): lax.ppermute(value, axis, [(source, source + steps) for source in range(i...  59.7 us
    dot_general x10, matrix products, apply_block(): jnp.einsum('abl,bl->al', matrix.astype(jnp.float32), vector, precision=hi...  42 us
    unnamed x14, other arithmetic  28.3 us
  transfers between devices with their start and end apart: 26, of which 17 were waited for; matrix products, arithmetic and copies ran while one was open for 9% of the time, Pallas kernels for 0%

commit v1 on v0

v1 whole, which is shorter than its diff:
```python
import functools

import jax
import jax.numpy as jnp
from jax import lax
from jax.experimental import pallas as pl
from jax.experimental.pallas import tpu as pltpu
from jax.sharding import PartitionSpec as P


SEGMENT = 32
BLOCK_ROWS = 1024
COUPLING, PIVOT, DIAGONAL, RESIDUAL = (0, 1024, 2048, 3072)
CHUNK_ROWS = 3072 + 48
VMEM_LIMIT = 48 * 1024 * 1024

f32 = jnp.float32
bf16 = jnp.bfloat16


def params():
    return pltpu.CompilerParams(vmem_limit_bytes=VMEM_LIMIT)


def segment_of(shape):
    return lax.broadcasted_iota(jnp.int32, shape, 1) >> 5


def row_of(shape):
    return lax.broadcasted_iota(jnp.int32, shape, 0)


def matmul(left, right):
    return jnp.dot(left, right, preferred_element_type=f32)


def three_parts(value):
    high = value.astype(bf16)
    rest = value - high.astype(f32)
    middle = rest.astype(bf16)
    low = (rest - middle.astype(f32)).astype(bf16)
    return high, middle, low


def pack_kernel(place, rhs, pivot, coupling, diagonal, neighbours, face_type, out0, out1, out2, out3, weights, order):
    me, cross = place[0], place[1]
    square = (128, 128)
    lane = lax.broadcasted_iota(jnp.int32, square, 1)
    slot = row_of(square)

    def step_down(face):
        near = neighbours[:, face : face + 1] - cross * 128
        return jnp.where((near == lane) & (lane != slot), 1.0, 0.0).astype(bf16)

    ones = jnp.ones(square, bf16)
    across = step_down(0)
    once = matmul(across, ones)
    twice = matmul(across, once.astype(bf16))
    column = once + twice + matmul(across, twice.astype(bf16))
    jump = step_down(2)
    row = matmul(jump, ones)
    for turn in range(5):
        row = row + matmul(jump, row.astype(bf16))
        if turn < 4:
            jump = matmul(jump, jump).astype(bf16)
    owner = jnp.where(cross % 2 == 0, column, 3.0 - column)
    position = (owner * 32.0 + row).astype(jnp.int32)

    segment = lane >> 5
    hits = [position == (((me + d) & 3) * 32 + (lane & 31)) for d in range(4)]
    for q in range(4):
        for d in range(4):
            order[q * 128 : (q + 1) * 128, d * 128 : (d + 1) * 128] = jnp.where(
                hits[d] & (segment == q), 1.0, 0.0
            ).astype(bf16)

    interior = jnp.where(face_type[...] == 0, 2.0, 0.0)
    own = interior + jnp.where(face_type[...] == 1, 4.0, 0.0)
    table = jnp.concatenate([own, interior, jnp.zeros((8, 128), f32)], axis=0).astype(bf16)
    placed = matmul(table, jnp.where(hits[0], 1.0, 0.0).astype(bf16))
    shape = (16, 128)
    seg, m = segment_of(shape), row_of(shape)
    masks = [seg == 0, seg == 3, m < 4, m >= 12]
    total = jnp.zeros(shape, f32)
    for face in range(4):
        total = total + jnp.where(masks[face], placed[face : face + 1], 0.0)
        weights[1 + face] = jnp.where(masks[face], placed[4 + face : 5 + face], 0.0)
    weights[0] = total

    outs = (out0, out1, out2, out3)
    sorting = order[...]

    def send(left, start, rows):
        result = matmul(left, sorting).astype(bf16)
        for d in range(4):
            outs[d][start : start + rows, :] = result[:, d * 128 : (d + 1) * 128]

    parts = []
    for part in three_parts(rhs[...]):
        parts.append(jnp.concatenate([part[16 * q : 16 * q + 16] for q in range(4)], axis=1))
    send(jnp.concatenate(parts, axis=0), RESIDUAL, 48)
    for block, start in ((coupling, COUPLING), (pivot, PIVOT), (diagonal, DIAGONAL)):
        left = jnp.concatenate(
            [block[:, 16 * q : 16 * q + 16, :].reshape(BLOCK_ROWS, 128) for q in range(4)], axis=1
        )
        send(left, start, BLOCK_ROWS)


def pack(place, rhs, pivot, coupling, diagonal, neighbours, face_type):
    chunk = jax.ShapeDtypeStruct((CHUNK_ROWS, 128), bf16)
    vmem = pl.BlockSpec(memory_space=pltpu.VMEM)
    return pl.pallas_call(
        pack_kernel,
        out_shape=[chunk] * 4 + [jax.ShapeDtypeStruct((5, 16, 128), f32), jax.ShapeDtypeStruct((512, 512), bf16)],
        in_specs=[pl.BlockSpec(memory_space=pltpu.SMEM)] + [vmem] * 6,
        out_specs=[vmem] * 6,
        compiler_params=params(),
        name="pack",
    )(place, rhs, pivot, coupling, diagonal, neighbours, face_type)


def to_packed(spread):
    seg = segment_of((16, 128))
    low = jnp.where(seg == 0, spread[0:16], spread[16:32])
    high = jnp.where(seg == 2, spread[32:48], spread[48:64])
    return jnp.where(seg < 2, low, high)


def to_spread(packed):
    seg = segment_of((16, 128))
    parts = []
    for q in range(4):
        part = jnp.where(seg == q, packed, 0.0)
        part = part + pltpu.roll(part, 32, 1)
        parts.append(part + pltpu.roll(part, 64, 1))
    return jnp.concatenate(parts, axis=0)


def transposed_times(blocks, elem, start, spread, row_ref):
    row_ref[...] = spread
    sums = [None] * 4
    for a in range(64):
        block = blocks[elem, start + 16 * a : start + 16 * a + 16, :].astype(f32)
        term = block * row_ref[a : a + 1, :]
        sums[a % 4] = term if sums[a % 4] is None else sums[a % 4] + term
    return (sums[0] + sums[1]) + (sums[2] + sums[3])


def times(blocks, elem, start, packed):
    block = blocks[elem, start : start + BLOCK_ROWS, :].astype(f32).reshape(64, 16, 128)
    total = jnp.sum(block * packed[None], axis=1)
    total = total + pltpu.roll(total, 32, 1)
    return total + pltpu.roll(total, 64, 1)


def fetch(place, received, blocks, sems):
    copies = [
        pltpu.make_async_copy(received[d], blocks.at[(place[0] - d) & 3], sems.at[d]) for d in range(4)
    ]
    for copy in copies:
        copy.start()
    for copy in copies:
        copy.wait()


def line_solve(residual, blocks, row_ref):
    forward = []
    for elem in range(4):
        right = to_spread(residual[elem])
        if elem > 0:
            right = right - times(blocks, elem, COUPLING, forward[-1])
        forward.append(transposed_times(blocks, elem, PIVOT, right, row_ref))
    values = [None] * 4
    carried = None
    for elem in reversed(range(4)):
        value = to_spread(forward[elem])
        if carried is not None:
            value = value - times(blocks, elem, PIVOT, carried)
        values[elem] = value
        if elem > 0:
            carried = transposed_times(blocks, elem, COUPLING, value, row_ref)
    return values


def send_faces(packed, upper, lower):
    seg = segment_of((16, 128))
    to_next, to_before = jnp.zeros((16, 128), f32), jnp.zeros((16, 128), f32)
    for elem in range(4):
        to_next = jnp.where(seg == elem, pltpu.roll(packed[elem], (32 * (elem + 1)) % 128, 1) if elem < 3 else packed[elem], to_next)
        to_before = jnp.where(seg == elem, pltpu.roll(packed[elem], 32 * elem, 1) if elem > 0 else packed[elem], to_before)
    upper[...] = to_next
    lower[...] = to_before


def line_apply(packed, blocks, weights, row_ref):
    spread = [to_spread(v) for v in packed]
    rows = []
    for elem in range(4):
        v = packed[elem]
        total = transposed_times(blocks, elem, DIAGONAL, spread[elem], row_ref)
        if elem > 0:
            total = total + to_packed(times(blocks, elem, COUPLING, packed[elem - 1]))
        if elem < 3:
            total = total + transposed_times(blocks, elem + 1, COUPLING, spread[elem + 1], row_ref)
        below = pltpu.roll(pltpu.roll(v, 4, 0), 1, 1)
        above = pltpu.roll(pltpu.roll(v, 12, 0), 127, 1)
        rows.append(total + weights[0] * v - weights[3] * below - weights[4] * above)
    return rows


def add_faces(partial, before, after, weights):
    rows = []
    for elem in range(4):
        left = before[...] if elem == 0 else pltpu.roll(before[...], 128 - 32 * elem, 1)
        right = after[...] if elem == 3 else pltpu.roll(after[...], 32 * (3 - elem), 1)
        rows.append(partial[elem] - weights[1] * left - weights[2] * right)
    return rows


def product_sum(first, second):
    total = first[0] * second[0]
    for elem in range(1, 4):
        total = total + first[elem] * second[elem]
    return jnp.sum(total, axis=0, keepdims=True)


def solve_kernel(place, r0, r1, r2, r3, residual, values, upper, lower, blocks, row_ref, sems):
    fetch(place, (r0, r1, r2, r3), blocks, sems)
    parts = []
    for elem in range(4):
        part = blocks[elem, RESIDUAL : RESIDUAL + 48, :].astype(f32)
        parts.append((part[0:16] + part[16:32]) + part[32:48])
        residual[elem] = parts[elem]
    packed = [to_packed(v) for v in line_solve(parts, blocks, row_ref)]
    for elem in range(4):
        values[elem] = packed[elem]
    send_faces(packed, upper, lower)


def apply_kernel(place, r0, r1, r2, r3, vector, weights, partial, blocks, row_ref, sems):
    fetch(place, (r0, r1, r2, r3), blocks, sems)
    rows = line_apply([vector[elem] for elem in range(4)], blocks, weights, row_ref)
    for elem in range(4):
        partial[elem] = rows[elem]


def join_solve_kernel(place, r0, r1, r2, r3, partial, before, after, weights, image, values, upper, lower, blocks, row_ref, sems):
    fetch(place, (r0, r1, r2, r3), blocks, sems)
    rows = add_faces(partial, before, after, weights)
    packed = [to_packed(v) for v in line_solve(rows, blocks, row_ref)]
    for elem in range(4):
        image[elem] = rows[elem]
        values[elem] = packed[elem]
    send_faces(packed, upper, lower)


def join_sums_kernel(partial, before, after, weights, r, z, w, s, image, sums):
    rows = add_faces(partial, before, after, weights)
    for elem in range(4):
        image[elem] = rows[elem]

    def values(ref):
        return [ref[elem] for elem in range(4)]

    z_, w_, s_ = values(z), values(w), values(s)
    products = [product_sum(values(r), z_), product_sum(z_, w_), product_sum(w_, s_), product_sum(s_, rows)]
    sums[...] = jnp.concatenate(products + [jnp.zeros((4, 128), f32)], axis=0)


def last_solve_kernel(place, r0, r1, r2, r3, z, w, s, t, back0, back1, back2, back3, blocks, row_ref, last, sems):
    fetch(place, (r0, r1, r2, r3), blocks, sems)
    packed = [to_packed(v) for v in line_solve([t[elem] for elem in range(4)], blocks, row_ref)]
    for elem in range(4):
        last[elem] = packed[elem]
    backs = (back0, back1, back2, back3)
    for d in range(4):
        elem = (place[0] + d) & 3
        for index, ref in enumerate((z, w, s, t, last)):
            backs[d][index] = ref[elem]


def final_kernel(sums, rhs, b0, b1, b2, b3, order, solution, residual, precond):
    vectors = [jnp.concatenate([b[index] for b in (b0, b3, b2, b1)], axis=1) for index in range(5)]
    z, w, s, t, u = vectors
    totals = jnp.sum(sums[...], axis=1, keepdims=True)
    rho, curve, second, third = (totals[k : k + 1, :] for k in range(4))
    alpha = rho / curve
    rho_next = rho - 2.0 * alpha * curve + alpha * alpha * second
    grown = 1.0 + rho_next / rho
    curve_next = grown * grown * curve - 2.0 * alpha * grown * second + alpha * alpha * third
    alpha_next = rho_next / curve_next
    first = alpha + alpha_next * grown
    other = alpha_next * alpha
    combos = [first * z - other * s, other * t - first * w, z - first * s + other * u]
    parts = [part for combo in combos for part in three_parts(combo)]
    moved = lax.dot_general(
        jnp.concatenate(parts, axis=0), order[...], (((1,), (1,)), ((), ())), preferred_element_type=f32
    )
    for index, ref in enumerate((solution, residual, precond)):
        rows = moved[48 * index : 48 * index + 48]
        value = (rows[0:16] + rows[16:32]) + rows[32:48]
        for q in range(4):
            part = value[:, 128 * q : 128 * q + 128]
            if index == 1:
                part = part + rhs[16 * q : 16 * q + 16, :]
            ref[16 * q : 16 * q + 16, :] = part


VMEM = pl.BlockSpec(memory_space=pltpu.VMEM)
SMEM = pl.BlockSpec(memory_space=pltpu.SMEM)
ANY = pl.BlockSpec(memory_space=pl.ANY)
FACE = jax.ShapeDtypeStruct((16, 128), f32)
VECTOR = jax.ShapeDtypeStruct((4, 16, 128), f32)
BASIS = jax.ShapeDtypeStruct((5, 16, 128), f32)


def with_blocks(kernel, place, received, arrays, outs, name, extra=()):
    return pl.pallas_call(
        kernel,
        out_shape=outs,
        in_specs=[SMEM] + [ANY] * 4 + [VMEM] * len(arrays),
        out_specs=[VMEM] * len(outs),
        scratch_shapes=[pltpu.VMEM((4, CHUNK_ROWS, 128), bf16), pltpu.VMEM((64, 128), f32)]
        + list(extra)
        + [pltpu.SemaphoreType.DMA((4,))],
        compiler_params=params(),
        name=name,
    )(place, *received, *arrays)


def plain(kernel, arrays, outs, name):
    return pl.pallas_call(
        kernel,
        out_shape=outs,
        in_specs=[VMEM] * len(arrays),
        out_specs=[VMEM] * len(outs),
        compiler_params=params(),
        name=name,
    )(*arrays)


def around(value, distance):
    count = lax.axis_size("field")
    return lax.ppermute(value, "field", [(i, (i + distance) % count) for i in range(count)])


def column_pairs(step):
    field, cross = lax.axis_size("field"), lax.axis_size("cross")
    device = {}
    for c in range(cross):
        for f in range(field):
            device[field * c + (f if c % 2 == 0 else field - 1 - f)] = f * cross + c
    count = field * cross
    return [(device[g], device[g + step]) for g in range(count) if 0 <= g + step < count]


def exchange(upper, lower):
    before = lax.ppermute(upper, ("field", "cross"), column_pairs(1))
    after = lax.ppermute(lower, ("field", "cross"), column_pairs(-1))
    return before, after


def total_of(value):
    cross = lax.axis_size("cross")
    for masks in ((1,), (2, 4, 6), (8,), (16, 32, 48)):
        moved = [
            lax.ppermute(value, "cross", [(i, i ^ mask) for i in range(cross)]) for mask in masks if mask < cross
        ]
        value = functools.reduce(jnp.add, moved, value)
    return functools.reduce(jnp.add, [around(value, d) for d in (1, 2, 3)], value)


def local(rhs, pivot_inverse, line_coupling, element_block, neighbours, face_type):
    place = jnp.stack([lax.axis_index("field"), lax.axis_index("cross")]).astype(jnp.int32)
    *chunks, weights, order = pack(
        place, rhs[0], pivot_inverse[0], line_coupling[0], element_block[0], neighbours, face_type.T
    )
    received = [chunks[0]] + [around(chunks[d], d) for d in (1, 2, 3)]
    r, z, upper, lower = with_blocks(solve_kernel, place, received, [], [VECTOR, VECTOR, FACE, FACE], "solve_first")
    before, after = exchange(upper, lower)
    (partial,) = with_blocks(apply_kernel, place, received, [z, weights], [VECTOR], "apply_first")
    w, s, upper, lower = with_blocks(
        join_solve_kernel, place, received, [partial, before, after, weights], [VECTOR, VECTOR, FACE, FACE], "solve_second"
    )
    before, after = exchange(upper, lower)
    (partial,) = with_blocks(apply_kernel, place, received, [s, weights], [VECTOR], "apply_second")
    t, sums = plain(
        join_sums_kernel,
        [partial, before, after, weights, r, z, w, s],
        [VECTOR, jax.ShapeDtypeStruct((8, 128), f32)],
        "sums",
    )
    sums = total_of(sums)
    backs = with_blocks(
        last_solve_kernel, place, received, [z, w, s, t], [BASIS] * 4, "solve_last", [pltpu.VMEM((4, 16, 128), f32)]
    )
    returned = [backs[0]] + [around(backs[d], d) for d in (1, 2, 3)]
    shape = jax.ShapeDtypeStruct((64, 128), f32)
    outs = plain(final_kernel, [sums, rhs[0], *returned, order], [shape] * 3, "final")
    return tuple(out[None] for out in outs)


def solution(mesh):
    placed = (
        P("field", None, "cross"),
        P("field", None, None, "cross"),
        P("field", None, None, "cross"),
        P("field", None, None, "cross"),
        P("cross", None),
        P("cross", None),
    )
    return jax.shard_map(
        local,
        mesh=mesh,
        in_specs=placed,
        out_specs=(P("field", None, "cross"), P("field", None, "cross"), P("field", None, "cross")),
        check_vma=False,
    )
```

time: 519 us -> 115 us (0.22)
  the two profiles are of different devices: /device:TPU:2 before, /device:TPU:6 now
where the time goes in v1:
time: 115 us
  waiting for transfers between devices  52.4 us (46%)
  starting transfers between devices  40.4 us (35%)
  Pallas kernels  17.1 us (15%)
  local copies, waits for them, and re-layouts  3.92 us (3%)
    ppermute x9, waiting for transfers between devices, around(): lax.ppermute(value, 'field', [(i, (i + distance) % count) for i in range(...  40.3 us
    ppermute x9, starting transfers between devices, around(): lax.ppermute(value, 'field', [(i, (i + distance) % count) for i in range(...  14.5 us
    ppermute x8, starting transfers between devices, total_of(): lax.ppermute(value, 'cross', [(i, i ^ mask) for i in range(cross)])  14.2 us
    ppermute x8, waiting for transfers between devices, total_of(): lax.ppermute(value, 'cross', [(i, i ^ mask) for i in range(cross)])  12.1 us
    pallas_call x5, Pallas kernels, with_blocks(): pl.pallas_call(kernel, out_shape=outs, in_specs=[SMEM] + [ANY] * 4 + [VME...  11.8 us
    ppermute x2, starting transfers between devices, exchange(): after = lax.ppermute(lower, ('field', 'cross'), column_pairs(-1))  7.84 us
    pallas_call x1, Pallas kernels, pack(): pl.pallas_call(pack_kernel, out_shape=[chunk] * 4 + [jax.ShapeDtypeStruct...  4.21 us
    unnamed x11, local copies, waits for them, and re-layouts  3.92 us
  transfers between devices with their start and end apart: 21, of which 11 were waited for; matrix products, arithmetic and copies ran while one was open for 0% of the time, Pallas kernels for 5%

profile of v1, /device:TPU:6, one launch (start us, length us, event | category | flops | bytes accessed | tf_op | source)
XLA Modules:
  0.0 114.7 jit_solution(7301058597579087587)
XLA Ops:
  4.6 4.2 %pack.1 = (bf16[3120,128]{1,0:T(8,128)(2,1)S(1)}, bf16[3120,128]{1,0:T(8,128)(2,1)S(1)}, bf16[3120,128]{1,0:T(8,128)(2,1)S(1)}, bf16[3120,128]{1,0:T(8,128)(2,1)...) custom-call(s32[2]{0:T(128)S(1)} %pad_add_fusion.place, f32[64,128]{1,0:T(8,128)S(1)} %bitcast.12, ...), custom_call_target="tpu_custom_call" | custom-call | tf_op jit(solution)/shard_map/pack/pallas_call | solution.py:112
  8.9 2.3 %collective-permute-start = (bf16[3120,128]{1,0:T(8,128)(2,1)S(1)}, bf16[3120,128]{1,0:T(8,128)(2,1)S(1)}, u32[]{:S(2)}, u32[]{:S(2)}) collective-permute-start(bf16[3120,128]{1,0:T(8,128)(2,1)S(1)} %get-tuple-element.27), channel_id=1, source_target_pairs={{0,64},{64,128},{128,192},{192,0},{1,65},{65,129},{129,193},{193,1... | collective-permute-start | bytes 2396168 | tf_op jit(solution)/shard_map/ppermute | solution.py:344
  12.1 17.5 %collective-permute-done.r1 = bf16[3120,128]{1,0:T(8,128)(2,1)S(1)} collective-permute-done((bf16[3120,128]{1,0:T(8,128)(2,1)S(1)}, bf16[3120,128]{1,0:T(8,128)(2,1)S(1)}, u32[]{:S(2)}, u32[]{:S(2)}) %collective-permute-start) | collective-permute-done | bytes 798752 | tf_op jit(solution)/shard_map/ppermute | solution.py:344
  29.6 3.8 %collective-permute-done.1.r2 = bf16[3120,128]{1,0:T(8,128)(2,1)S(1)} collective-permute-done((bf16[3120,128]{1,0:T(8,128)(2,1)S(1)}, bf16[3120,128]{1,0:T(8,128)(2,1)S(1)}, u32[]{:S(2)}, u32[]{:S(2)}) %collective-permute-start.1) | collective-permute-done | bytes 798752 | tf_op jit(solution)/shard_map/ppermute | solution.py:344
  33.4 13.8 %collective-permute-done.2.r3 = bf16[3120,128]{1,0:T(8,128)(2,1)S(1)} collective-permute-done((bf16[3120,128]{1,0:T(8,128)(2,1)S(1)}, bf16[3120,128]{1,0:T(8,128)(2,1)S(1)}, u32[]{:S(2)}, u32[]{:S(2)}) %collective-permute-start.2) | collective-permute-done | bytes 798752 | tf_op jit(solution)/shard_map/ppermute | solution.py:344
  47.2 2.8 %solve_first.1 = (f32[4,16,128]{2,1,0:T(8,128)S(1)}, f32[4,16,128]{2,1,0:T(8,128)S(1)}, f32[16,128]{1,0:T(8,128)S(1)}, f32[16,128]{1,0:T(8,128)S(1)}) custom-call(s32[2]{0:T(128)S(1)} %pad_add_fusion.place, bf16[3120,128]{1,0:T(8,128)(2,1)S(1)} %get-tuple-element.26.r0, bf16[3120,128]{1,0:T(8,128)(2,1)S(1)} %collective-permute-done.r1, ...), custom_call_target="tpu_custom_call" | custom-call | tf_op jit(solution)/shard_map/solve_first/pallas_call | solution.py:318
  50.0 1.9 %collective-permute-start.3 = (f32[16,128]{1,0:T(8,128)S(1)}, f32[16,128]{1,0:T(8,128)S(1)}, u32[]{:S(2)}, u32[]{:S(2)}) collective-permute-start(f32[16,128]{1,0:T(8,128)S(1)} %get-tuple-element.32), channel_id=1, source_target_pairs={{0,64},{64,128},{128,192},{192,193},{193,129},{129,65},{65,1},{1,2... | collective-permute-start | bytes 24584 | tf_op jit(solution)/shard_map/ppermute | solution.py:358
  51.9 3.9 %collective-permute-start.4 = (f32[16,128]{1,0:T(8,128)S(1)}, f32[16,128]{1,0:T(8,128)S(1)}, u32[]{:S(2)}, u32[]{:S(2)}) collective-permute-start(f32[16,128]{1,0:T(8,128)S(1)} %get-tuple-element.33), channel_id=1, source_target_pairs={{64,0},{128,64},{192,128},{193,192},{129,193},{65,129},{1,65},{2,1... | collective-permute-start | bytes 24584 | tf_op jit(solution)/shard_map/ppermute | solution.py:359
  55.8 1.7 %apply_first.1.partial = f32[4,16,128]{2,1,0:T(8,128)S(1)} custom-call(s32[2]{0:T(128)S(1)} %pad_add_fusion.place, bf16[3120,128]{1,0:T(8,128)(2,1)S(1)} %get-tuple-element.26.r0, bf16[3120,128]{1,0:T(8,128)(2,1)S(1)} %collective-permute-done.r1, bf16[3120,128]{1,0:T(8,128)(2,1)S(1)} %collective-permute-done.1.r2, ...), custom_call_target="tpu_custom_call" | custom-call | tf_op jit(solution)/shard_map/apply_first/pallas_call | solution.py:318
  57.6 2.8 %solve_second.1 = (f32[4,16,128]{2,1,0:T(8,128)S(1)}, f32[4,16,128]{2,1,0:T(8,128)S(1)}, f32[16,128]{1,0:T(8,128)S(1)}, f32[16,128]{1,0:T(8,128)S(1)}) custom-call(s32[2]{0:T(128)S(1)} %pad_add_fusion.place, bf16[3120,128]{1,0:T(8,128)(2,1)S(1)} %get-tuple-element.26.r0, bf16[3120,128]{1,0:T(8,128)(2,1)S(1)} %collective-permute-done.r1, ...), custom_call_target="tpu_custom_call" | custom-call | tf_op jit(solution)/shard_map/solve_second/pallas_call | solution.py:318
  60.4 1.9 %collective-permute-start.5 = (f32[16,128]{1,0:T(8,128)S(1)}, f32[16,128]{1,0:T(8,128)S(1)}, u32[]{:S(2)}, u32[]{:S(2)}) collective-permute-start(f32[16,128]{1,0:T(8,128)S(1)} %get-tuple-element.35), channel_id=1, source_target_pairs={{0,64},{64,128},{128,192},{192,193},{193,129},{129,65},{65,1},{1,2... | collective-permute-start | bytes 24584 | tf_op jit(solution)/shard_map/ppermute | solution.py:358
  62.4 3.9 %collective-permute-start.6 = (f32[16,128]{1,0:T(8,128)S(1)}, f32[16,128]{1,0:T(8,128)S(1)}, u32[]{:S(2)}, u32[]{:S(2)}) collective-permute-start(f32[16,128]{1,0:T(8,128)S(1)} %get-tuple-element.36), channel_id=1, source_target_pairs={{64,0},{128,64},{192,128},{193,192},{129,193},{65,129},{1,65},{2,1... | collective-permute-start | bytes 24584 | tf_op jit(solution)/shard_map/ppermute | solution.py:359
  69.4 4.7 %collective-permute-start.10 = (f32[8,128]{1,0:T(8,128)S(1)}, f32[8,128]{1,0:T(8,128)S(1)}, u32[]{:S(2)}, u32[]{:S(2)}) collective-permute-start(f32[8,128]{1,0:T(8,128)S(1)} %add.33), channel_id=1, source_target_pairs={{0,6},{1,7},{2,4},{3,5},{4,2},{5,3},{6,0},{7,1},{8,14},{9,15},{10,... | collective-permute-start | bytes 12296 | tf_op jit(solution)/shard_map/ppermute | solution.py:367
  75.7 2.9 %collective-permute-done.9 = f32[8,128]{1,0:T(8,128)S(1)} collective-permute-done((f32[8,128]{1,0:T(8,128)S(1)}, f32[8,128]{1,0:T(8,128)S(1)}, u32[]{:S(2)}, u32[]{:S(2)}) %collective-permute-start.9) | collective-permute-done | bytes 4128 | tf_op jit(solution)/shard_map/ppermute | solution.py:367
  78.7 4.8 %collective-permute-start.11 = (f32[8,128]{1,0:T(8,128)S(1)}, f32[8,128]{1,0:T(8,128)S(1)}, u32[]{:S(2)}, u32[]{:S(2)}) collective-permute-start(f32[8,128]{1,0:T(8,128)S(1)} %add_add_fusion.2), channel_id=1, source_target_pairs={{0,8},{1,9},{2,10},{3,11},{4,12},{5,13},{6,14},{7,15},{8,0},{9,1},... | collective-permute-start | bytes 12296 | tf_op jit(solution)/shard_map/ppermute | solution.py:367
  83.4 3.0 %collective-permute-done.11 = f32[8,128]{1,0:T(8,128)S(1)} collective-permute-done((f32[8,128]{1,0:T(8,128)S(1)}, f32[8,128]{1,0:T(8,128)S(1)}, u32[]{:S(2)}, u32[]{:S(2)}) %collective-permute-start.11) | collective-permute-done | bytes 4128 | tf_op jit(solution)/shard_map/ppermute | solution.py:367
  86.5 3.0 %collective-permute-start.14 = (f32[8,128]{1,0:T(8,128)S(1)}, f32[8,128]{1,0:T(8,128)S(1)}, u32[]{:S(2)}, u32[]{:S(2)}) collective-permute-start(f32[8,128]{1,0:T(8,128)S(1)} %add.37), channel_id=1, source_target_pairs={{0,48},{1,49},{2,50},{3,51},{4,52},{5,53},{6,54},{7,55},{8,56},{9,... | collective-permute-start | bytes 12296 | tf_op jit(solution)/shard_map/ppermute | solution.py:367
  91.3 3.3 %collective-permute-done.13 = f32[8,128]{1,0:T(8,128)S(1)} collective-permute-done((f32[8,128]{1,0:T(8,128)S(1)}, f32[8,128]{1,0:T(8,128)S(1)}, u32[]{:S(2)}, u32[]{:S(2)}) %collective-permute-start.13) | collective-permute-done | bytes 4128 | tf_op jit(solution)/shard_map/ppermute | solution.py:367
  94.6 2.5 %collective-permute-start.17 = (f32[8,128]{1,0:T(8,128)S(1)}, f32[8,128]{1,0:T(8,128)S(1)}, u32[]{:S(2)}, u32[]{:S(2)}) collective-permute-start(f32[8,128]{1,0:T(8,128)S(1)} %add_add_fusion.1), channel_id=1, source_target_pairs={{0,192},{64,0},{128,64},{192,128},{1,193},{65,1},{129,65},{193,129... | collective-permute-start | bytes 12296 | tf_op jit(solution)/shard_map/ppermute | solution.py:344
  97.1 4.5 %collective-permute-start.16 = (f32[8,128]{1,0:T(8,128)S(1)}, f32[8,128]{1,0:T(8,128)S(1)}, u32[]{:S(2)}, u32[]{:S(2)}) collective-permute-start(f32[8,128]{1,0:T(8,128)S(1)} %add_add_fusion.1), channel_id=1, source_target_pairs={{0,128},{64,192},{128,0},{192,64},{1,129},{65,193},{129,1},{193,65... | collective-permute-start | bytes 12296 | tf_op jit(solution)/shard_map/ppermute | solution.py:344
  101.6 2.7 %solve_last.1 = (f32[5,16,128]{2,1,0:T(8,128)S(1)}, f32[5,16,128]{2,1,0:T(8,128)S(1)}, f32[5,16,128]{2,1,0:T(8,128)S(1)}, f32[5,16,128]{2,1,0:T(8,128)S(1)}) custom-call(s32[2]{0:T(128)S(1)} %pad_add_fusion.place, bf16[3120,128]{1,0:T(8,128)(2,1)S(1)} %get-tuple-element.26.r0, bf16[3120,128]{1,0:T(8,128)(2,1)S(1)} %collective-permute-done.r1, ...), custom_call_target="tpu_custom_call" | custom-call | tf_op jit(solution)/shard_map/solve_last/pallas_call | solution.py:318
  105.0 3.5 %collective-permute-start.19 = (f32[5,16,128]{2,1,0:T(8,128)S(1)}, f32[5,16,128]{2,1,0:T(8,128)S(1)}, u32[]{:S(2)}, u32[]{:S(2)}) collective-permute-start(f32[5,16,128]{2,1,0:T(8,128)S(1)} %get-tuple-element.43), channel_id=1, source_target_pairs={{0,128},{64,192},{128,0},{192,64},{1,129},{65,193},{129,1},{193,65... | collective-permute-start | bytes 122888 | tf_op jit(solution)/shard_map/ppermute | solution.py:344
  108.6 1.9 %collective-permute-done.19.b2 = f32[5,16,128]{2,1,0:T(8,128)S(1)} collective-permute-done((f32[5,16,128]{2,1,0:T(8,128)S(1)}, f32[5,16,128]{2,1,0:T(8,128)S(1)}, u32[]{:S(2)}, u32[]{:S(2)}) %collective-permute-start.19) | collective-permute-done | bytes 40992 | tf_op jit(solution)/shard_map/ppermute | solution.py:344
  110.5 3.2 %collective-permute-done.20.b3 = f32[5,16,128]{2,1,0:T(8,128)S(1)} collective-permute-done((f32[5,16,128]{2,1,0:T(8,128)S(1)}, f32[5,16,128]{2,1,0:T(8,128)S(1)}, u32[]{:S(2)}, u32[]{:S(2)}) %collective-permute-start.20) | collective-permute-done | bytes 40992 | tf_op jit(solution)/shard_map/ppermute | solution.py:344
  (43 shorter events, 13.1 us)
Async XLA Ops:
  1.3 0.8 copy-start.2
  2.2 1.2 %copy-start = (bf16[1,64,64,128]{3,2,1,0:T(8,128)(2,1)S(1)}, bf16[1,64,64,128]{3,2,1,0:T(8,128)(2,1)}, u32[]{:S(2)}) copy-start(bf16[1,64,64,128]{3,2,1,0:T(8,128)(2,1)} %param.7) | copy-start | bytes 3145732
  3.4 1.2 %copy-start.1 = (bf16[1,64,64,128]{3,2,1,0:T(8,128)(2,1)S(1)}, bf16[1,64,64,128]{3,2,1,0:T(8,128)(2,1)}, u32[]{:S(2)}) copy-start(bf16[1,64,64,128]{3,2,1,0:T(8,128)(2,1)} %param.8) | copy-start | bytes 3145732
  8.9 20.8 %collective-permute-start = (bf16[3120,128]{1,0:T(8,128)(2,1)S(1)}, bf16[3120,128]{1,0:T(8,128)(2,1)S(1)}, u32[]{:S(2)}, u32[]{:S(2)}) collective-permute-start(bf16[3120,128]{1,0:T(8,128)(2,1)S(1)} %get-tuple-element.27), channel_id=1, source_target_pairs={{0,64},{64,128},{128,192},{192,0},{1,65},{65,129},{129,193},{193,1... | collective-permute-start | bytes 2396168 | tf_op jit(solution)/shard_map/ppermute | solution.py:344
  11.1 22.3 %collective-permute-start.1 = (bf16[3120,128]{1,0:T(8,128)(2,1)S(1)}, bf16[3120,128]{1,0:T(8,128)(2,1)S(1)}, u32[]{:S(2)}, u32[]{:S(2)}) collective-permute-start(bf16[3120,128]{1,0:T(8,128)(2,1)S(1)} %get-tuple-element.28), channel_id=1, source_target_pairs={{0,128},{64,192},{128,0},{192,64},{1,129},{65,193},{129,1},{193,65... | collective-permute-start | bytes 2396168 | tf_op jit(solution)/shard_map/ppermute | solution.py:344
  11.8 35.4 %collective-permute-start.2 = (bf16[3120,128]{1,0:T(8,128)(2,1)S(1)}, bf16[3120,128]{1,0:T(8,128)(2,1)S(1)}, u32[]{:S(2)}, u32[]{:S(2)}) collective-permute-start(bf16[3120,128]{1,0:T(8,128)(2,1)S(1)} %get-tuple-element.29), channel_id=1, source_target_pairs={{0,192},{64,0},{128,64},{192,128},{1,193},{65,1},{129,65},{193,129... | collective-permute-start | bytes 2396168 | tf_op jit(solution)/shard_map/ppermute | solution.py:344
  50.0 7.6 %collective-permute-start.3 = (f32[16,128]{1,0:T(8,128)S(1)}, f32[16,128]{1,0:T(8,128)S(1)}, u32[]{:S(2)}, u32[]{:S(2)}) collective-permute-start(f32[16,128]{1,0:T(8,128)S(1)} %get-tuple-element.32), channel_id=1, source_target_pairs={{0,64},{64,128},{128,192},{192,193},{193,129},{129,65},{65,1},{1,2... | collective-permute-start | bytes 24584 | tf_op jit(solution)/shard_map/ppermute | solution.py:358
  51.9 5.7 %collective-permute-start.4 = (f32[16,128]{1,0:T(8,128)S(1)}, f32[16,128]{1,0:T(8,128)S(1)}, u32[]{:S(2)}, u32[]{:S(2)}) collective-permute-start(f32[16,128]{1,0:T(8,128)S(1)} %get-tuple-element.33), channel_id=1, source_target_pairs={{64,0},{128,64},{192,128},{193,192},{129,193},{65,129},{1,65},{2,1... | collective-permute-start | bytes 24584 | tf_op jit(solution)/shard_map/ppermute | solution.py:359
  60.4 7.6 %collective-permute-start.5 = (f32[16,128]{1,0:T(8,128)S(1)}, f32[16,128]{1,0:T(8,128)S(1)}, u32[]{:S(2)}, u32[]{:S(2)}) collective-permute-start(f32[16,128]{1,0:T(8,128)S(1)} %get-tuple-element.35), channel_id=1, source_target_pairs={{0,64},{64,128},{128,192},{192,193},{193,129},{129,65},{65,1},{1,2... | collective-permute-start | bytes 24584 | tf_op jit(solution)/shard_map/ppermute | solution.py:358
  62.4 5.7 %collective-permute-start.6 = (f32[16,128]{1,0:T(8,128)S(1)}, f32[16,128]{1,0:T(8,128)S(1)}, u32[]{:S(2)}, u32[]{:S(2)}) collective-permute-start(f32[16,128]{1,0:T(8,128)S(1)} %get-tuple-element.36), channel_id=1, source_target_pairs={{64,0},{128,64},{192,128},{193,192},{129,193},{65,129},{1,65},{2,1... | collective-permute-start | bytes 24584 | tf_op jit(solution)/shard_map/ppermute | solution.py:359
  68.2 1.3 %collective-permute-start.7 = (f32[8,128]{1,0:T(8,128)S(1)}, f32[8,128]{1,0:T(8,128)S(1)}, u32[]{:S(2)}, u32[]{:S(2)}) collective-permute-start(f32[8,128]{1,0:T(8,128)S(1)} %get-tuple-element.39), channel_id=1, source_target_pairs={{0,1},{1,0},{2,3},{3,2},{4,5},{5,4},{6,7},{7,6},{8,9},{9,8},{10,11... | collective-permute-start | bytes 12296 | tf_op jit(solution)/shard_map/ppermute | solution.py:367
  69.4 6.3 %collective-permute-start.10 = (f32[8,128]{1,0:T(8,128)S(1)}, f32[8,128]{1,0:T(8,128)S(1)}, u32[]{:S(2)}, u32[]{:S(2)}) collective-permute-start(f32[8,128]{1,0:T(8,128)S(1)} %add.33), channel_id=1, source_target_pairs={{0,6},{1,7},{2,4},{3,5},{4,2},{5,3},{6,0},{7,1},{8,14},{9,15},{10,... | collective-permute-start | bytes 12296 | tf_op jit(solution)/shard_map/ppermute | solution.py:367
  74.2 4.5 %collective-permute-start.9 = (f32[8,128]{1,0:T(8,128)S(1)}, f32[8,128]{1,0:T(8,128)S(1)}, u32[]{:S(2)}, u32[]{:S(2)}) collective-permute-start(f32[8,128]{1,0:T(8,128)S(1)} %add.33), channel_id=1, source_target_pairs={{0,4},{1,5},{2,6},{3,7},{4,0},{5,1},{6,2},{7,3},{8,12},{9,13},{10,... | collective-permute-start | bytes 12296 | tf_op jit(solution)/shard_map/ppermute | solution.py:367
  74.2 4.5 %collective-permute-start.8 = (f32[8,128]{1,0:T(8,128)S(1)}, f32[8,128]{1,0:T(8,128)S(1)}, u32[]{:S(2)}, u32[]{:S(2)}) collective-permute-start(f32[8,128]{1,0:T(8,128)S(1)} %add.33), channel_id=1, source_target_pairs={{0,2},{1,3},{2,0},{3,1},{4,6},{5,7},{6,4},{7,5},{8,10},{9,11},{10,... | collective-permute-start | bytes 12296 | tf_op jit(solution)/shard_map/ppermute | solution.py:367
  78.7 7.8 %collective-permute-start.11 = (f32[8,128]{1,0:T(8,128)S(1)}, f32[8,128]{1,0:T(8,128)S(1)}, u32[]{:S(2)}, u32[]{:S(2)}) collective-permute-start(f32[8,128]{1,0:T(8,128)S(1)} %add_add_fusion.2), channel_id=1, source_target_pairs={{0,8},{1,9},{2,10},{3,11},{4,12},{5,13},{6,14},{7,15},{8,0},{9,1},... | collective-permute-start | bytes 12296 | tf_op jit(solution)/shard_map/ppermute | solution.py:367
  86.5 4.8 %collective-permute-start.14 = (f32[8,128]{1,0:T(8,128)S(1)}, f32[8,128]{1,0:T(8,128)S(1)}, u32[]{:S(2)}, u32[]{:S(2)}) collective-permute-start(f32[8,128]{1,0:T(8,128)S(1)} %add.37), channel_id=1, source_target_pairs={{0,48},{1,49},{2,50},{3,51},{4,52},{5,53},{6,54},{7,55},{8,56},{9,... | collective-permute-start | bytes 12296 | tf_op jit(solution)/shard_map/ppermute | solution.py:367
  89.5 5.1 %collective-permute-start.13 = (f32[8,128]{1,0:T(8,128)S(1)}, f32[8,128]{1,0:T(8,128)S(1)}, u32[]{:S(2)}, u32[]{:S(2)}) collective-permute-start(f32[8,128]{1,0:T(8,128)S(1)} %add.37), channel_id=1, source_target_pairs={{0,32},{1,33},{2,34},{3,35},{4,36},{5,37},{6,38},{7,39},{8,40},{9,... | collective-permute-start | bytes 12296 | tf_op jit(solution)/shard_map/ppermute | solution.py:367
  90.1 4.5 %collective-permute-start.12 = (f32[8,128]{1,0:T(8,128)S(1)}, f32[8,128]{1,0:T(8,128)S(1)}, u32[]{:S(2)}, u32[]{:S(2)}) collective-permute-start(f32[8,128]{1,0:T(8,128)S(1)} %add.37), channel_id=1, source_target_pairs={{0,16},{1,17},{2,18},{3,19},{4,20},{5,21},{6,22},{7,23},{8,24},{9,... | collective-permute-start | bytes 12296 | tf_op jit(solution)/shard_map/ppermute | solution.py:367
  94.6 13.9 %collective-permute-start.17 = (f32[8,128]{1,0:T(8,128)S(1)}, f32[8,128]{1,0:T(8,128)S(1)}, u32[]{:S(2)}, u32[]{:S(2)}) collective-permute-start(f32[8,128]{1,0:T(8,128)S(1)} %add_add_fusion.1), channel_id=1, source_target_pairs={{0,192},{64,0},{128,64},{192,128},{1,193},{65,1},{129,65},{193,129... | collective-permute-start | bytes 12296 | tf_op jit(solution)/shard_map/ppermute | solution.py:344
  97.1 11.4 %collective-permute-start.16 = (f32[8,128]{1,0:T(8,128)S(1)}, f32[8,128]{1,0:T(8,128)S(1)}, u32[]{:S(2)}, u32[]{:S(2)}) collective-permute-start(f32[8,128]{1,0:T(8,128)S(1)} %add_add_fusion.1), channel_id=1, source_target_pairs={{0,128},{64,192},{128,0},{192,64},{1,129},{65,193},{129,1},{193,65... | collective-permute-start | bytes 12296 | tf_op jit(solution)/shard_map/ppermute | solution.py:344
  101.6 6.9 %collective-permute-start.15 = (f32[8,128]{1,0:T(8,128)S(1)}, f32[8,128]{1,0:T(8,128)S(1)}, u32[]{:S(2)}, u32[]{:S(2)}) collective-permute-start(f32[8,128]{1,0:T(8,128)S(1)} %add_add_fusion.1), channel_id=1, source_target_pairs={{0,64},{64,128},{128,192},{192,0},{1,65},{65,129},{129,193},{193,1... | collective-permute-start | bytes 12296 | tf_op jit(solution)/shard_map/ppermute | solution.py:344
  104.3 4.2 %collective-permute-start.18 = (f32[5,16,128]{2,1,0:T(8,128)S(1)}, f32[5,16,128]{2,1,0:T(8,128)S(1)}, u32[]{:S(2)}, u32[]{:S(2)}) collective-permute-start(f32[5,16,128]{2,1,0:T(8,128)S(1)} %get-tuple-element.42), channel_id=1, source_target_pairs={{0,64},{64,128},{128,192},{192,0},{1,65},{65,129},{129,193},{193,1... | collective-permute-start | bytes 122888 | tf_op jit(solution)/shard_map/ppermute | solution.py:344
  105.0 5.5 %collective-permute-start.19 = (f32[5,16,128]{2,1,0:T(8,128)S(1)}, f32[5,16,128]{2,1,0:T(8,128)S(1)}, u32[]{:S(2)}, u32[]{:S(2)}) collective-permute-start(f32[5,16,128]{2,1,0:T(8,128)S(1)} %get-tuple-element.43), channel_id=1, source_target_pairs={{0,128},{64,192},{128,0},{192,64},{1,129},{65,193},{129,1},{193,65... | collective-permute-start | bytes 122888 | tf_op jit(solution)/shard_map/ppermute | solution.py:344
  108.5 5.2 %collective-permute-start.20 = (f32[5,16,128]{2,1,0:T(8,128)S(1)}, f32[5,16,128]{2,1,0:T(8,128)S(1)}, u32[]{:S(2)}, u32[]{:S(2)}) collective-permute-start(f32[5,16,128]{2,1,0:T(8,128)S(1)} %get-tuple-element.44), channel_id=1, source_target_pairs={{0,192},{64,0},{128,64},{192,128},{1,193},{65,1},{129,65},{193,129... | collective-permute-start | bytes 122888 | tf_op jit(solution)/shard_map/ppermute | solution.py:344
  (2 other events, 1.4 us)

commit v2 on v1

v2 whole, which is shorter than its diff:
```python
import jax
import jax.numpy as jnp
from jax import lax
from jax.experimental import pallas as pl
from jax.experimental.pallas import tpu as pltpu
from jax.sharding import PartitionSpec as P


BLOCK_ROWS = 1024
COUPLING, TRIANGLES, TRAIL = (0, 1024, 2048)
CHUNK_ROWS = 2048 + 64
PIVOT, DIAGONAL = (1024, 2048)
ELEMENT_ROWS = 3072
VMEM_LIMIT = 24 * 1024 * 1024

VMEM = pl.BlockSpec(memory_space=pltpu.VMEM)
HBM = pl.BlockSpec(memory_space=pltpu.HBM)

f32 = jnp.float32
bf16 = jnp.bfloat16


def params():
    return pltpu.CompilerParams(vmem_limit_bytes=VMEM_LIMIT)


def segment_of(shape):
    return lax.broadcasted_iota(jnp.int32, shape, 1) >> 5


def row_of(shape):
    return lax.broadcasted_iota(jnp.int32, shape, 0)


def matmul(left, right):
    return jnp.dot(left, right, preferred_element_type=f32)


def matmul_nt(left, right):
    return lax.dot_general(left, right, (((1,), (1,)), ((), ())), preferred_element_type=f32)


def three_parts(value):
    high = value.astype(bf16)
    rest = value - high.astype(f32)
    middle = rest.astype(bf16)
    low = (rest - middle.astype(f32)).astype(bf16)
    return high, middle, low


def pack_kernel(rhs, pivot, coupling, diagonal, neighbours, face_type, out0, out1, out2, out3, weights, order, *scratch):
    *held, sems = scratch
    copies = [
        pltpu.make_async_copy(source, target, sems.at[index])
        for index, (source, target) in enumerate(
            zip((neighbours, face_type, rhs, coupling, pivot, diagonal), held, strict=True)
        )
    ]
    for copy in copies:
        copy.start()
    neighbours, face_type, rhs, coupling, pivot, diagonal = held
    me, cross = lax.axis_index("field"), lax.axis_index("cross")
    square = (128, 128)
    lane = lax.broadcasted_iota(jnp.int32, square, 1)
    sub = row_of(square)
    copies[0].wait()

    def step_down(face):
        near = neighbours[face : face + 1, :] - cross * 128
        return jnp.where((near == sub) & (lane != sub), 1.0, 0.0).astype(bf16)

    ones = jnp.ones((16, 128), bf16)
    across = step_down(0)
    once = matmul(ones, across)
    twice = matmul(once.astype(bf16), across)
    column = once + twice + matmul(twice.astype(bf16), across)
    jump = step_down(2)
    row = matmul(ones, jump)
    for turn in range(5):
        row = row + matmul(row.astype(bf16), jump)
        if turn < 4:
            jump = matmul(jump, jump).astype(bf16)
    owner = jnp.where(cross % 2 == 0, column, 3.0 - column)
    position = (owner * 32.0 + row).astype(jnp.int32)[0:1]

    segment = sub >> 5
    hits = [position == (((me + d) & 3) * 32 + (sub & 31)) for d in range(4)]
    for q in range(4):
        for d in range(4):
            order[d * 128 : (d + 1) * 128, q * 128 : (q + 1) * 128] = jnp.where(
                hits[d] & (segment == q), 1.0, 0.0
            ).astype(bf16)

    outs = (out0, out1, out2, out3)
    sorting = order[...]

    def send(left, start, rows):
        result = matmul_nt(left, sorting).astype(bf16)
        for d in range(4):
            outs[d][start : start + rows, :] = result[:, d * 128 : (d + 1) * 128]

    copies[3].wait()
    left = [coupling[:, 16 * q : 16 * q + 16, :].reshape(BLOCK_ROWS, 128) for q in range(4)]
    send(jnp.concatenate(left, axis=1), COUPLING, BLOCK_ROWS)

    copies[4].wait()
    copies[5].wait()
    corner = (16, 16, 128)
    major, minor = lax.broadcasted_iota(jnp.int32, corner, 0), lax.broadcasted_iota(jnp.int32, corner, 1)
    left, trail = [], []
    for q in range(4):
        here = slice(16 * q, 16 * q + 16)
        own, other = pivot[here, here, :].astype(f32), diagonal[here, here, :].astype(f32)
        mixed = jnp.where(minor <= major, own, other).astype(bf16)
        parts = [mixed]
        if q > 0:
            parts = [diagonal[0 : 16 * q, here, :]] + parts
        if q < 3:
            parts = parts + [pivot[16 * q + 16 : 64, here, :]]
        left.append(jnp.concatenate(parts, axis=0).reshape(BLOCK_ROWS, 128))
        trail.append(jnp.sum(jnp.where(minor == major, other, 0.0), axis=0).astype(bf16))
    send(jnp.concatenate(left, axis=1), TRIANGLES, BLOCK_ROWS)

    copies[2].wait()
    rows = [jnp.concatenate(trail, axis=1)]
    for part in three_parts(rhs[...]):
        rows.append(jnp.concatenate([part[16 * q : 16 * q + 16] for q in range(4)], axis=1))
    send(jnp.concatenate(rows, axis=0), TRAIL, 64)

    copies[1].wait()
    interior = jnp.where(face_type[...] == 0, 2.0, 0.0)
    own = interior + jnp.where(face_type[...] == 1, 4.0, 0.0)
    table = jnp.concatenate([own, interior, jnp.zeros((8, 128), f32)], axis=0).astype(bf16)
    placed = matmul_nt(table, jnp.where(hits[0], 1.0, 0.0).astype(bf16))
    shape = (16, 128)
    seg, m = segment_of(shape), row_of(shape)
    masks = [seg == 0, seg == 3, m < 4, m >= 12]
    total = jnp.zeros(shape, f32)
    for face in range(4):
        total = total + jnp.where(masks[face], placed[face : face + 1], 0.0)
        weights[1 + face] = jnp.where(masks[face], placed[4 + face : 5 + face], 0.0)
    weights[0] = total


def pack(rhs, pivot, coupling, diagonal, neighbours, face_type):
    chunk = jax.ShapeDtypeStruct((CHUNK_ROWS, 128), bf16)
    held = [pltpu.VMEM((4, 128), jnp.int32)] * 2 + [pltpu.VMEM((64, 128), f32)] + [pltpu.VMEM((64, 64, 128), bf16)] * 3
    return pl.pallas_call(
        pack_kernel,
        out_shape=[chunk] * 4 + [jax.ShapeDtypeStruct((5, 16, 128), f32), jax.ShapeDtypeStruct((512, 512), bf16)],
        in_specs=[HBM] * 6,
        out_specs=[VMEM] * 6,
        scratch_shapes=held + [pltpu.SemaphoreType.DMA((6,))],
        compiler_params=params(),
        name="pack",
    )(*(pltpu.with_memory_space_constraint(x, pltpu.HBM) for x in (rhs, pivot, coupling, diagonal, neighbours, face_type)))


def to_packed(spread):
    seg = segment_of((16, 128))
    low = jnp.where(seg == 0, spread[0:16], spread[16:32])
    high = jnp.where(seg == 2, spread[32:48], spread[48:64])
    return jnp.where(seg < 2, low, high)


def to_spread(packed):
    seg = segment_of((16, 128))
    parts = []
    for q in range(4):
        part = jnp.where(seg == q, packed, 0.0)
        part = part + pltpu.roll(part, 32, 1)
        parts.append(part + pltpu.roll(part, 64, 1))
    return jnp.concatenate(parts, axis=0)


def transposed_times(blocks, elem, start, spread, row_ref):
    row_ref[...] = spread
    sums = [None] * 4
    for a in range(64):
        block = blocks[elem, start + 16 * a : start + 16 * a + 16, :].astype(f32)
        term = block * row_ref[a : a + 1, :]
        sums[a % 4] = term if sums[a % 4] is None else sums[a % 4] + term
    return (sums[0] + sums[1]) + (sums[2] + sums[3])


def times(blocks, elem, start, packed):
    block = blocks[elem, start : start + BLOCK_ROWS, :].astype(f32).reshape(64, 16, 128)
    total = jnp.sum(block * packed[None], axis=1)
    total = total + pltpu.roll(total, 32, 1)
    return total + pltpu.roll(total, 64, 1)


def turn_segments(rows):
    seg = segment_of(rows[0].shape)
    rows = list(rows)
    for width, low in ((2, seg < 2), (1, (seg & 1) == 0)):
        for j in range(4):
            if j & width:
                continue
            x, y = rows[j], rows[j + width]
            rows[j] = jnp.where(low, x, pltpu.roll(y, 32 * width, 1))
            rows[j + width] = jnp.where(low, pltpu.roll(x, 128 - 32 * width, 1), y)
    return rows


def unpack_triangles(triangles, trail, blocks, elem):
    shape = (16, 128)
    seg, m = segment_of(shape), row_of(shape)
    turned = []
    for q in range(4):
        block = triangles[256 * q : 256 * q + 256, :].astype(f32).reshape(16, 16, 128)
        turned.append(jnp.swapaxes(block, 0, 1))
    for k in range(16):
        across = turn_segments([turned[q][k] for q in range(4)])
        for q in range(4):
            a = 16 * q + k
            here = triangles[16 * a : 16 * a + 16, :].astype(f32)
            below = (seg < q) | ((seg == q) & (m <= k))
            diagonal = jnp.where((seg == q) & (m == k), trail, jnp.where(below, across[q], here))
            blocks[elem, PIVOT + 16 * a : PIVOT + 16 * a + 16, :] = jnp.where(below, here, across[q]).astype(bf16)
            blocks[elem, DIAGONAL + 16 * a : DIAGONAL + 16 * a + 16, :] = diagonal.astype(bf16)


def line_solve(residual, blocks, row_ref):
    forward = []
    for elem in range(4):
        right = to_spread(residual[elem])
        if elem > 0:
            right = right - times(blocks, elem, COUPLING, forward[-1])
        forward.append(transposed_times(blocks, elem, PIVOT, right, row_ref))
    values = [None] * 4
    carried = None
    for elem in reversed(range(4)):
        value = to_spread(forward[elem])
        if carried is not None:
            value = value - times(blocks, elem, PIVOT, carried)
        values[elem] = value
        if elem > 0:
            carried = transposed_times(blocks, elem, COUPLING, value, row_ref)
    return values


def send_faces(packed, upper, lower):
    seg = segment_of((16, 128))
    to_next, to_before = jnp.zeros((16, 128), f32), jnp.zeros((16, 128), f32)
    for elem in range(4):
        to_next = jnp.where(seg == elem, pltpu.roll(packed[elem], (32 * (elem + 1)) % 128, 1) if elem < 3 else packed[elem], to_next)
        to_before = jnp.where(seg == elem, pltpu.roll(packed[elem], 32 * elem, 1) if elem > 0 else packed[elem], to_before)
    upper[...] = to_next
    lower[...] = to_before


def line_apply(packed, blocks, weights, row_ref):
    spread = [to_spread(v) for v in packed]
    rows = []
    for elem in range(4):
        v = packed[elem]
        total = transposed_times(blocks, elem, DIAGONAL, spread[elem], row_ref)
        if elem > 0:
            total = total + to_packed(times(blocks, elem, COUPLING, packed[elem - 1]))
        if elem < 3:
            total = total + transposed_times(blocks, elem + 1, COUPLING, spread[elem + 1], row_ref)
        below = pltpu.roll(pltpu.roll(v, 4, 0), 1, 1)
        above = pltpu.roll(pltpu.roll(v, 12, 0), 127, 1)
        rows.append(total + weights[0] * v - weights[3] * below - weights[4] * above)
    return rows


def add_faces(partial, before, after, weights):
    rows = []
    for elem in range(4):
        left = before[...] if elem == 0 else pltpu.roll(before[...], 128 - 32 * elem, 1)
        right = after[...] if elem == 3 else pltpu.roll(after[...], 32 * (3 - elem), 1)
        rows.append(partial[elem] - weights[1] * left - weights[2] * right)
    return rows


def product_sum(first, second):
    total = first[0] * second[0]
    for elem in range(1, 4):
        total = total + first[elem] * second[elem]
    return jnp.sum(total, axis=0, keepdims=True)


def solve_kernel(c0, c1, c2, c3, blocks, residual, values, upper, lower, triangles, row_ref, sems):
    me = lax.axis_index("field")
    copies = []
    for d, source in enumerate((c0, c1, c2, c3)):
        elem = (me - d) & 3
        pairs = (
            (source.at[TRIANGLES:CHUNK_ROWS, :], triangles.at[elem]),
            (source.at[0:BLOCK_ROWS, :], blocks.at[elem, 0:BLOCK_ROWS, :]),
        )
        copies.append([pltpu.make_async_copy(*pair, sems.at[2 * d + k]) for k, pair in enumerate(pairs)])
    for group in copies:
        for copy in group:
            copy.start()
    for group in copies:
        for copy in group:
            copy.wait()
    parts = []
    for elem in range(4):
        trail = triangles[elem, BLOCK_ROWS : BLOCK_ROWS + 64, :].astype(f32)
        parts.append((trail[16:32] + trail[32:48]) + trail[48:64])
        residual[elem] = parts[elem]
        unpack_triangles(triangles.at[elem], trail[0:16], blocks, elem)
    packed = [to_packed(v) for v in line_solve(parts, blocks, row_ref)]
    for elem in range(4):
        values[elem] = packed[elem]
    send_faces(packed, upper, lower)


def apply_kernel(blocks, vector, weights, partial, row_ref):
    rows = line_apply([vector[elem] for elem in range(4)], blocks, weights, row_ref)
    for elem in range(4):
        partial[elem] = rows[elem]


def join_solve_kernel(blocks, partial, before, after, weights, image, values, upper, lower, row_ref):
    rows = add_faces(partial, before, after, weights)
    packed = [to_packed(v) for v in line_solve(rows, blocks, row_ref)]
    for elem in range(4):
        image[elem] = rows[elem]
        values[elem] = packed[elem]
    send_faces(packed, upper, lower)


def last_solve_kernel(blocks, partial, before, after, weights, r, z, w, s, back0, back1, back2, back3, row_ref, t, u):
    rows = add_faces(partial, before, after, weights)
    packed = [to_packed(v) for v in line_solve(rows, blocks, row_ref)]
    for elem in range(4):
        t[elem] = rows[elem]
        u[elem] = packed[elem]

    def values(ref):
        return [ref[elem] for elem in range(4)]

    z_, w_, s_ = values(z), values(w), values(s)
    seg = segment_of((1, 128))
    sums = jnp.zeros((1, 128), f32)
    for index, pair in enumerate(((values(r), z_), (z_, w_), (w_, s_), (s_, rows))):
        total = product_sum(*pair)
        total = total + pltpu.roll(total, 32, 1)
        total = total + pltpu.roll(total, 64, 1)
        sums = jnp.where(seg == index, total, sums)
    me = lax.axis_index("field")
    for d, back in enumerate((back0, back1, back2, back3)):
        elem = (me + d) & 3
        for index, ref in enumerate((z, w, s, t, u)):
            back[16 * index : 16 * index + 16, :] = ref[elem]
        back[80:88, :] = jnp.broadcast_to(sums, (8, 128))


def final_kernel(sums, rhs, b0, b1, b2, b3, order, solution, residual, precond):
    backs = (b0, b3, b2, b1)
    z, w, s, t, u = (
        jnp.concatenate([b[16 * index : 16 * index + 16, :] for b in backs], axis=1) for index in range(5)
    )
    total = jnp.sum(sums[...], axis=0)
    totals = [jnp.sum(total[:, 32 * k : 32 * k + 32], axis=1, keepdims=True) for k in range(4)]
    rho, curve, second, third = totals
    alpha = rho / curve
    rho_next = rho - 2.0 * alpha * curve + alpha * alpha * second
    grown = 1.0 + rho_next / rho
    curve_next = grown * grown * curve - 2.0 * alpha * grown * second + alpha * alpha * third
    alpha_next = rho_next / curve_next
    first = alpha + alpha_next * grown
    other = alpha_next * alpha
    combos = [first * z - other * s, other * t - first * w, z - first * s + other * u]
    parts = [part for combo in combos for part in three_parts(combo)]
    moved = matmul(jnp.concatenate(parts, axis=0), order[...])
    for index, ref in enumerate((solution, residual, precond)):
        rows = moved[48 * index : 48 * index + 48]
        value = (rows[0:16] + rows[16:32]) + rows[32:48]
        for q in range(4):
            part = value[:, 128 * q : 128 * q + 128]
            if index == 1:
                part = part + rhs[16 * q : 16 * q + 16, :]
            ref[16 * q : 16 * q + 16, :] = part


FACE = jax.ShapeDtypeStruct((16, 128), f32)
VECTOR = jax.ShapeDtypeStruct((4, 16, 128), f32)
BACK = jax.ShapeDtypeStruct((88, 128), f32)
BLOCKS = jax.ShapeDtypeStruct((4, ELEMENT_ROWS, 128), bf16)


def kernel(body, arrays, outs, name, spec=VMEM, scratch=()):
    return pl.pallas_call(
        body,
        out_shape=outs,
        in_specs=[spec] * len(arrays),
        out_specs=[VMEM] * len(outs),
        scratch_shapes=list(scratch),
        compiler_params=params(),
        name=name,
    )(*arrays)


def around(value, distance):
    count = lax.axis_size("field")
    return lax.ppermute(value, "field", [(i, (i + distance) % count) for i in range(count)])


def column_pairs(step):
    field, cross = lax.axis_size("field"), lax.axis_size("cross")
    device = {}
    for c in range(cross):
        for f in range(field):
            device[field * c + (f if c % 2 == 0 else field - 1 - f)] = f * cross + c
    count = field * cross
    return [(device[g], device[g + step]) for g in range(count) if 0 <= g + step < count]


def exchange(upper, lower):
    before = lax.ppermute(upper, ("field", "cross"), column_pairs(1))
    after = lax.ppermute(lower, ("field", "cross"), column_pairs(-1))
    return before, after


def local(rhs, pivot_inverse, line_coupling, element_block, neighbours, face_type):
    *chunks, weights, order = pack(
        rhs[0], pivot_inverse[0], line_coupling[0], element_block[0], neighbours.T, face_type.T
    )
    received = [chunks[0]] + [around(chunks[d], d) for d in (1, 2, 3)]
    spread = pltpu.VMEM((64, 128), f32)
    triangles = pltpu.VMEM((4, CHUNK_ROWS - TRIANGLES, 128), bf16)
    blocks, r, z, upper, lower = kernel(
        solve_kernel,
        received,
        [BLOCKS, VECTOR, VECTOR, FACE, FACE],
        "solve_first",
        pl.BlockSpec(memory_space=pl.ANY),
        [triangles, spread, pltpu.SemaphoreType.DMA((8,))],
    )
    before, after = exchange(upper, lower)
    (partial,) = kernel(apply_kernel, [blocks, z, weights], [VECTOR], "apply_first", scratch=[spread])
    w, s, upper, lower = kernel(
        join_solve_kernel,
        [blocks, partial, before, after, weights],
        [VECTOR, VECTOR, FACE, FACE],
        "solve_second",
        scratch=[spread],
    )
    before, after = exchange(upper, lower)
    (partial,) = kernel(apply_kernel, [blocks, s, weights], [VECTOR], "apply_second", scratch=[spread])
    backs = kernel(
        last_solve_kernel,
        [blocks, partial, before, after, weights, r, z, w, s],
        [BACK] * 4,
        "solve_last",
        scratch=[spread, pltpu.VMEM((4, 16, 128), f32), pltpu.VMEM((4, 16, 128), f32)],
    )
    returned = [backs[0]] + [around(backs[d], d) for d in (1, 2, 3)]
    row = (returned[0][80:81] + returned[1][80:81]) + (returned[2][80:81] + returned[3][80:81])
    rows = jnp.broadcast_to(row[None], (lax.axis_size("cross"), 1, 128))
    sums = lax.all_to_all(rows, "cross", 0, 0)
    shape = jax.ShapeDtypeStruct((64, 128), f32)
    outs = kernel(final_kernel, [sums, rhs[0], *returned, order], [shape] * 3, "final")
    return tuple(out[None] for out in outs)


def solution(mesh):
    placed = (
        P("field", None, "cross"),
        P("field", None, None, "cross"),
        P("field", None, None, "cross"),
        P("field", None, None, "cross"),
        P("cross", None),
        P("cross", None),
    )
    return jax.shard_map(
        local,
        mesh=mesh,
        in_specs=placed,
        out_specs=(P("field", None, "cross"), P("field", None, "cross"), P("field", None, "cross")),
        check_vma=False,
    )
```

time: 115 us -> 88.9 us (0.77)
  the two profiles are of different devices: /device:TPU:6 before, /device:TPU:1 now
where the time goes in v2:
time: 88.9 us; the launch traced here: 88.6 us
  waiting for transfers between devices  29.3 us (33%)
  blocking collectives  22.2 us (25%)
  starting transfers between devices  21.3 us (24%)
  Pallas kernels  15.1 us (17%)
    ppermute x6, waiting for transfers between devices, around(): lax.ppermute(value, 'field', [(i, (i + distance) % count) for i in range(...  24.9 us
    all_to_all x1, blocking collectives, local(): sums = lax.all_to_all(rows, 'cross', 0, 0)  22.2 us
    pallas_call x6, Pallas kernels, kernel(): pl.pallas_call(body, out_shape=outs, in_specs=[spec] * len(arrays), out_s...  11.4 us
    ppermute x2, starting transfers between devices, exchange(): before = lax.ppermute(upper, ('field', 'cross'), column_pairs(1))  8.77 us
    ppermute x6, starting transfers between devices, around(): lax.ppermute(value, 'field', [(i, (i + distance) % count) for i in range(...  8.64 us
    ppermute x2, waiting for transfers between devices, exchange(): after = lax.ppermute(lower, ('field', 'cross'), column_pairs(-1))  4.39 us
    ppermute x2, starting transfers between devices, exchange(): after = lax.ppermute(lower, ('field', 'cross'), column_pairs(-1))  3.84 us
    pallas_call x1, Pallas kernels, pack(): pl.pallas_call(pack_kernel, out_shape=[chunk] * 4 + [jax.ShapeDtypeStruct...  3.64 us
  transfers between devices with their start and end apart: 10, of which 7 were waited for; matrix products, arithmetic and copies ran while one was open for 0% of the time, Pallas kernels for 2%

profile of v2, /device:TPU:1, one launch (start us, length us, event | category | flops | bytes accessed | tf_op | source)
XLA Modules:
  0.0 88.6 jit_solution(10676034912524104532)
XLA Ops:
  0.6 3.6 %pack.1 = (bf16[2112,128]{1,0:T(8,128)(2,1)S(1)}, bf16[2112,128]{1,0:T(8,128)(2,1)S(1)}, bf16[2112,128]{1,0:T(8,128)(2,1)S(1)}, bf16[2112,128]{1,0:T(8,128)(2,1)...) custom-call(f32[64,128]{1,0:T(8,128)} %bitcast.11, bf16[64,64,128]{2,1,0:T(8,128)(2,1)} %bitcast.13, ...), custom_call_target="tpu_custom_call" | custom-call | tf_op jit(solution)/shard_map/pack/pallas_call | solution.py:148
  4.3 2.1 %collective-permute-start = (bf16[2112,128]{1,0:T(8,128)(2,1)S(1)}, bf16[2112,128]{1,0:T(8,128)(2,1)S(1)}, u32[]{:S(2)}, u32[]{:S(2)}) collective-permute-start(bf16[2112,128]{1,0:T(8,128)(2,1)S(1)} %get-tuple-element.26), channel_id=1, source_target_pairs={{0,64},{64,128},{128,192},{192,0},{1,65},{65,129},{129,193},{193,1... | collective-permute-start | bytes 1622024 | tf_op jit(solution)/shard_map/ppermute | solution.py:402
  6.4 2.5 %collective-permute-start.1 = (bf16[2112,128]{1,0:T(8,128)(2,1)S(1)}, bf16[2112,128]{1,0:T(8,128)(2,1)S(1)}, u32[]{:S(2)}, u32[]{:S(2)}) collective-permute-start(bf16[2112,128]{1,0:T(8,128)(2,1)S(1)} %get-tuple-element.27), channel_id=1, source_target_pairs={{0,128},{64,192},{128,0},{192,64},{1,129},{65,193},{129,1},{193,65... | collective-permute-start | bytes 1622024 | tf_op jit(solution)/shard_map/ppermute | solution.py:402
  8.9 1.1 %collective-permute-start.2 = (bf16[2112,128]{1,0:T(8,128)(2,1)S(1)}, bf16[2112,128]{1,0:T(8,128)(2,1)S(1)}, u32[]{:S(2)}, u32[]{:S(2)}) collective-permute-start(bf16[2112,128]{1,0:T(8,128)(2,1)S(1)} %get-tuple-element.28), channel_id=1, source_target_pairs={{0,192},{64,0},{128,64},{192,128},{1,193},{65,1},{129,65},{193,129... | collective-permute-start | bytes 1622024 | tf_op jit(solution)/shard_map/ppermute | solution.py:402
  10.0 7.4 %collective-permute-done.c1 = bf16[2112,128]{1,0:T(8,128)(2,1)S(1)} collective-permute-done((bf16[2112,128]{1,0:T(8,128)(2,1)S(1)}, bf16[2112,128]{1,0:T(8,128)(2,1)S(1)}, u32[]{:S(2)}, u32[]{:S(2)}) %collective-permute-start) | collective-permute-done | bytes 540704 | tf_op jit(solution)/shard_map/ppermute | solution.py:402
  17.4 14.7 %collective-permute-done.1.c2 = bf16[2112,128]{1,0:T(8,128)(2,1)S(1)} collective-permute-done((bf16[2112,128]{1,0:T(8,128)(2,1)S(1)}, bf16[2112,128]{1,0:T(8,128)(2,1)S(1)}, u32[]{:S(2)}, u32[]{:S(2)}) %collective-permute-start.1) | collective-permute-done | bytes 540704 | tf_op jit(solution)/shard_map/ppermute | solution.py:402
  32.1 4.6 %solve_first.1 = (bf16[4,3072,128]{2,1,0:T(8,128)(2,1)S(1)}, f32[4,16,128]{2,1,0:T(8,128)S(1)}, f32[4,16,128]{2,1,0:T(8,128)S(1)}, f32[16,128]{1,0:T(8,128)S(1)}, f32[16,128]{1,0:T(8,128)S(1)}) custom-call(bf16[2112,128]{1,0:T(8,128)(2,1)S(1)} %get-tuple-element.25.c0, bf16[2112,128]{1,0:T(8,128)(2,1)S(1)} %collective-permute-done.c1, ...), custom_call_target="tpu_custom_call" | custom-call | tf_op jit(solution)/shard_map/solve_first/pallas_call | solution.py:389
  36.8 5.0 %collective-permute-start.3 = (f32[16,128]{1,0:T(8,128)S(1)}, f32[16,128]{1,0:T(8,128)S(1)}, u32[]{:S(2)}, u32[]{:S(2)}) collective-permute-start(f32[16,128]{1,0:T(8,128)S(1)} %get-tuple-element.32), channel_id=1, source_target_pairs={{0,64},{64,128},{128,192},{192,193},{193,129},{129,65},{65,1},{1,2... | collective-permute-start | bytes 24584 | tf_op jit(solution)/shard_map/ppermute | solution.py:416
  41.7 1.9 %collective-permute-start.4 = (f32[16,128]{1,0:T(8,128)S(1)}, f32[16,128]{1,0:T(8,128)S(1)}, u32[]{:S(2)}, u32[]{:S(2)}) collective-permute-start(f32[16,128]{1,0:T(8,128)S(1)} %get-tuple-element.33), channel_id=1, source_target_pairs={{64,0},{128,64},{192,128},{193,192},{129,193},{65,129},{1,65},{2,1... | collective-permute-start | bytes 24584 | tf_op jit(solution)/shard_map/ppermute | solution.py:417
  43.7 0.8 apply_first.1.partial
  44.5 2.2 %collective-permute-done.4.after = f32[16,128]{1,0:T(8,128)S(1)} collective-permute-done((f32[16,128]{1,0:T(8,128)S(1)}, f32[16,128]{1,0:T(8,128)S(1)}, u32[]{:S(2)}, u32[]{:S(2)}) %collective-permute-start.4) | collective-permute-done | bytes 8224 | tf_op jit(solution)/shard_map/ppermute | solution.py:417
  46.7 2.1 %solve_second.1 = (f32[4,16,128]{2,1,0:T(8,128)S(1)}, f32[4,16,128]{2,1,0:T(8,128)S(1)}, f32[16,128]{1,0:T(8,128)S(1)}, f32[16,128]{1,0:T(8,128)S(1)}) custom-call(bf16[4,3072,128]{2,1,0:T(8,128)(2,1)S(1)} %get-tuple-element.29.blocks, f32[4,16,128]{2,1,0:T(8,128)S(1)} %apply_first.1.partial, f32[16,128]{1,0:T(8,128)S(1)} %collective-permute-done.3.before, ...), custom_call_target="tpu_custom_call" | custom-call | tf_op jit(solution)/shard_map/solve_second/pallas_call | solution.py:389
  48.8 3.8 %collective-permute-start.5 = (f32[16,128]{1,0:T(8,128)S(1)}, f32[16,128]{1,0:T(8,128)S(1)}, u32[]{:S(2)}, u32[]{:S(2)}) collective-permute-start(f32[16,128]{1,0:T(8,128)S(1)} %get-tuple-element.35), channel_id=1, source_target_pairs={{0,64},{64,128},{128,192},{192,193},{193,129},{129,65},{65,1},{1,2... | collective-permute-start | bytes 24584 | tf_op jit(solution)/shard_map/ppermute | solution.py:416
  52.6 1.9 %collective-permute-start.6 = (f32[16,128]{1,0:T(8,128)S(1)}, f32[16,128]{1,0:T(8,128)S(1)}, u32[]{:S(2)}, u32[]{:S(2)}) collective-permute-start(f32[16,128]{1,0:T(8,128)S(1)} %get-tuple-element.36), channel_id=1, source_target_pairs={{64,0},{128,64},{192,128},{193,192},{129,193},{65,129},{1,65},{2,1... | collective-permute-start | bytes 24584 | tf_op jit(solution)/shard_map/ppermute | solution.py:417
  54.5 0.8 apply_second.1.partial
  55.4 2.2 %collective-permute-done.6.after = f32[16,128]{1,0:T(8,128)S(1)} collective-permute-done((f32[16,128]{1,0:T(8,128)S(1)}, f32[16,128]{1,0:T(8,128)S(1)}, u32[]{:S(2)}, u32[]{:S(2)}) %collective-permute-start.6) | collective-permute-done | bytes 8224 | tf_op jit(solution)/shard_map/ppermute | solution.py:417
  57.6 2.0 %solve_last.1 = (f32[88,128]{1,0:T(8,128)S(1)}, f32[88,128]{1,0:T(8,128)S(1)}, f32[88,128]{1,0:T(8,128)S(1)}, f32[88,128]{1,0:T(8,128)S(1)}) custom-call(bf16[4,3072,128]{2,1,0:T(8,128)(2,1)S(1)} %get-tuple-element.29.blocks, f32[4,16,128]{2,1,0:T(8,128)S(1)} %apply_second.1.partial, f32[16,128]{1,0:T(8,128)S(1)} %collective-permute-done.5.before, ...), custom_call_target="tpu_custom_call" | custom-call | tf_op jit(solution)/shard_map/solve_last/pallas_call | solution.py:389
  59.6 0.3 collective-permute-start.7
  59.9 2.6 %collective-permute-start.9 = (f32[88,128]{1,0:T(8,128)S(1)}, f32[88,128]{1,0:T(8,128)S(1)}, u32[]{:S(2)}, u32[]{:S(2)}) collective-permute-start(f32[88,128]{1,0:T(8,128)S(1)} %get-tuple-element.42), channel_id=1, source_target_pairs={{0,192},{64,0},{128,64},{192,128},{1,193},{65,1},{129,65},{193,129... | collective-permute-start | bytes 135176 | tf_op jit(solution)/shard_map/ppermute | solution.py:402
  62.5 1.4 %collective-permute-done.7.b1 = f32[88,128]{1,0:T(8,128)S(1)} collective-permute-done((f32[88,128]{1,0:T(8,128)S(1)}, f32[88,128]{1,0:T(8,128)S(1)}, u32[]{:S(2)}, u32[]{:S(2)}) %collective-permute-start.7) | collective-permute-done | bytes 45088 | tf_op jit(solution)/shard_map/ppermute | solution.py:402
  63.9 0.5 collective-permute-done.8.b2
  64.4 0.9 collective-permute-done.9.b3
  65.3 22.2 %all_to_all.5.sums = f32[64,1,128]{2,1,0:T(1,128)S(1)} all-to-all(f32[64,1,128]{2,1,0:T(1,128)S(1)} %broadcast_in_dim.18), channel_id=1, replica_groups=mesh['field'=4,'cross'=64] {'cross'}, dimensions={0} | all-to-all | bytes 65536 | tf_op jit(solution)/shard_map/all_to_all | solution.py:457
  87.5 1.1 %final.1 = (f32[64,128]{1,0:T(8,128)}, f32[64,128]{1,0:T(8,128)}, f32[64,128]{1,0:T(8,128)}) custom-call(f32[64,1,128]{2,1,0:T(1,128)S(1)} %all_to_all.5.sums, f32[64,128]{1,0:T(8,128)S(1)} %bitcast.12, f32[88,128]{1,0:T(8,128)S(1)} %get-tuple-element.39.b0, f32[88,128]{1,0:T(8,128)S(1)} %collective-permute-done.7.b1, ...), custom_call_target="tpu_custom_call" | custom-call | tf_op jit(solution)/shard_map/final/pallas_call | solution.py:389
  (8 shorter events, 0.1 us)
Async XLA Ops:
  4.3 13.1 %collective-permute-start = (bf16[2112,128]{1,0:T(8,128)(2,1)S(1)}, bf16[2112,128]{1,0:T(8,128)(2,1)S(1)}, u32[]{:S(2)}, u32[]{:S(2)}) collective-permute-start(bf16[2112,128]{1,0:T(8,128)(2,1)S(1)} %get-tuple-element.26), channel_id=1, source_target_pairs={{0,64},{64,128},{128,192},{192,0},{1,65},{65,129},{129,193},{193,1... | collective-permute-start | bytes 1622024 | tf_op jit(solution)/shard_map/ppermute | solution.py:402
  6.4 25.7 %collective-permute-start.1 = (bf16[2112,128]{1,0:T(8,128)(2,1)S(1)}, bf16[2112,128]{1,0:T(8,128)(2,1)S(1)}, u32[]{:S(2)}, u32[]{:S(2)}) collective-permute-start(bf16[2112,128]{1,0:T(8,128)(2,1)S(1)} %get-tuple-element.27), channel_id=1, source_target_pairs={{0,128},{64,192},{128,0},{192,64},{1,129},{65,193},{129,1},{193,65... | collective-permute-start | bytes 1622024 | tf_op jit(solution)/shard_map/ppermute | solution.py:402
  8.9 23.3 %collective-permute-start.2 = (bf16[2112,128]{1,0:T(8,128)(2,1)S(1)}, bf16[2112,128]{1,0:T(8,128)(2,1)S(1)}, u32[]{:S(2)}, u32[]{:S(2)}) collective-permute-start(bf16[2112,128]{1,0:T(8,128)(2,1)S(1)} %get-tuple-element.28), channel_id=1, source_target_pairs={{0,192},{64,0},{128,64},{192,128},{1,193},{65,1},{129,65},{193,129... | collective-permute-start | bytes 1622024 | tf_op jit(solution)/shard_map/ppermute | solution.py:402
  36.8 7.7 %collective-permute-start.3 = (f32[16,128]{1,0:T(8,128)S(1)}, f32[16,128]{1,0:T(8,128)S(1)}, u32[]{:S(2)}, u32[]{:S(2)}) collective-permute-start(f32[16,128]{1,0:T(8,128)S(1)} %get-tuple-element.32), channel_id=1, source_target_pairs={{0,64},{64,128},{128,192},{192,193},{193,129},{129,65},{65,1},{1,2... | collective-permute-start | bytes 24584 | tf_op jit(solution)/shard_map/ppermute | solution.py:416
  41.7 5.0 %collective-permute-start.4 = (f32[16,128]{1,0:T(8,128)S(1)}, f32[16,128]{1,0:T(8,128)S(1)}, u32[]{:S(2)}, u32[]{:S(2)}) collective-permute-start(f32[16,128]{1,0:T(8,128)S(1)} %get-tuple-element.33), channel_id=1, source_target_pairs={{64,0},{128,64},{192,128},{193,192},{129,193},{65,129},{1,65},{2,1... | collective-permute-start | bytes 24584 | tf_op jit(solution)/shard_map/ppermute | solution.py:417
  48.8 6.6 %collective-permute-start.5 = (f32[16,128]{1,0:T(8,128)S(1)}, f32[16,128]{1,0:T(8,128)S(1)}, u32[]{:S(2)}, u32[]{:S(2)}) collective-permute-start(f32[16,128]{1,0:T(8,128)S(1)} %get-tuple-element.35), channel_id=1, source_target_pairs={{0,64},{64,128},{128,192},{192,193},{193,129},{129,65},{65,1},{1,2... | collective-permute-start | bytes 24584 | tf_op jit(solution)/shard_map/ppermute | solution.py:416
  52.6 5.0 %collective-permute-start.6 = (f32[16,128]{1,0:T(8,128)S(1)}, f32[16,128]{1,0:T(8,128)S(1)}, u32[]{:S(2)}, u32[]{:S(2)}) collective-permute-start(f32[16,128]{1,0:T(8,128)S(1)} %get-tuple-element.36), channel_id=1, source_target_pairs={{64,0},{128,64},{192,128},{193,192},{129,193},{65,129},{1,65},{2,1... | collective-permute-start | bytes 24584 | tf_op jit(solution)/shard_map/ppermute | solution.py:417
  54.5 33.0 %copy-start = (f32[1,64,128]{2,1,0:T(8,128)S(1)}, f32[1,64,128]{2,1,0:T(8,128)}, u32[]{:S(2)}) copy-start(f32[1,64,128]{2,1,0:T(8,128)} %param.6) | copy-start | bytes 98308
  59.6 4.4 %collective-permute-start.7 = (f32[88,128]{1,0:T(8,128)S(1)}, f32[88,128]{1,0:T(8,128)S(1)}, u32[]{:S(2)}, u32[]{:S(2)}) collective-permute-start(f32[88,128]{1,0:T(8,128)S(1)} %get-tuple-element.40), channel_id=1, source_target_pairs={{0,64},{64,128},{128,192},{192,0},{1,65},{65,129},{129,193},{193,1... | collective-permute-start | bytes 135176 | tf_op jit(solution)/shard_map/ppermute | solution.py:402
  59.8 4.6 %collective-permute-start.8 = (f32[88,128]{1,0:T(8,128)S(1)}, f32[88,128]{1,0:T(8,128)S(1)}, u32[]{:S(2)}, u32[]{:S(2)}) collective-permute-start(f32[88,128]{1,0:T(8,128)S(1)} %get-tuple-element.41), channel_id=1, source_target_pairs={{0,128},{64,192},{128,0},{192,64},{1,129},{65,193},{129,1},{193,65... | collective-permute-start | bytes 135176 | tf_op jit(solution)/shard_map/ppermute | solution.py:402
  59.9 5.3 %collective-permute-start.9 = (f32[88,128]{1,0:T(8,128)S(1)}, f32[88,128]{1,0:T(8,128)S(1)}, u32[]{:S(2)}, u32[]{:S(2)}) collective-permute-start(f32[88,128]{1,0:T(8,128)S(1)} %get-tuple-element.42), channel_id=1, source_target_pairs={{0,192},{64,0},{128,64},{192,128},{1,193},{65,1},{129,65},{193,129... | collective-permute-start | bytes 135176 | tf_op jit(solution)/shard_map/ppermute | solution.py:402

commit v3 on v2

--- a/solution.py
+++ b/solution.py
@@ -1,3 +1,5 @@
+import functools
+
 import jax
 import jax.numpy as jnp
 from jax import lax
@@ -48,16 +50,22 @@
     return high, middle, low
 
 
-def pack_kernel(rhs, pivot, coupling, diagonal, neighbours, face_type, out0, out1, out2, out3, weights, order, *scratch):
-    *held, sems = scratch
-    copies = [
-        pltpu.make_async_copy(source, target, sems.at[index])
-        for index, (source, target) in enumerate(
-            zip((neighbours, face_type, rhs, coupling, pivot, diagonal), held, strict=True)
-        )
-    ]
+def start_fetch(sources, targets, sems):
+    copies = [pltpu.make_async_copy(*pair, sems.at[i]) for i, pair in enumerate(zip(sources, targets, strict=True))]
     for copy in copies:
         copy.start()
+    return copies
+
+
+def send(left, sorting, outs, start, rows):
+    result = matmul_nt(left, sorting).astype(bf16)
+    for d in range(4):
+        outs[d][start : start + rows, :] = result[:, d * 128 : (d + 1) * 128]
+
+
+def pack_kernel(neighbours, face_type, rhs, coupling, pivot, diagonal, out0, out1, out2, out3, weights, order, *scratch):
+    *held, sems = scratch
+    copies = start_fetch((neighbours, face_type, rhs, coupling, pivot, diagonal), held, sems)
     neighbours, face_type, rhs, coupling, pivot, diagonal = held
     me, cross = lax.axis_index("field"), lax.axis_index("cross")
     square = (128, 128)
@@ -91,41 +99,31 @@
                 hits[d] & (segment == q), 1.0, 0.0
             ).astype(bf16)
 
-    outs = (out0, out1, out2, out3)
-    sorting = order[...]
-
-    def send(left, start, rows):
-        result = matmul_nt(left, sorting).astype(bf16)
-        for d in range(4):
-            outs[d][start : start + rows, :] = result[:, d * 128 : (d + 1) * 128]
-
+    outs, sorting = (out0, out1, out2, out3), order[...]
     copies[3].wait()
     left = [coupling[:, 16 * q : 16 * q + 16, :].reshape(BLOCK_ROWS, 128) for q in range(4)]
-    send(jnp.concatenate(left, axis=1), COUPLING, BLOCK_ROWS)
-
-    copies[4].wait()
-    copies[5].wait()
+    send(jnp.concatenate(left, axis=1), sorting, outs, COUPLING, BLOCK_ROWS)
+
+    for copy in (copies[2], copies[4], copies[5]):
+        copy.wait()
     corner = (16, 16, 128)
     major, minor = lax.broadcasted_iota(jnp.int32, corner, 0), lax.broadcasted_iota(jnp.int32, corner, 1)
     left, trail = [], []
     for q in range(4):
         here = slice(16 * q, 16 * q + 16)
         own, other = pivot[here, here, :].astype(f32), diagonal[here, here, :].astype(f32)
-        mixed = jnp.where(minor <= major, own, other).astype(bf16)
-        parts = [mixed]
+        parts = [jnp.where(minor <= major, own, other).astype(bf16)]
         if q > 0:
             parts = [diagonal[0 : 16 * q, here, :]] + parts
         if q < 3:
             parts = parts + [pivot[16 * q + 16 : 64, here, :]]
         left.append(jnp.concatenate(parts, axis=0).reshape(BLOCK_ROWS, 128))
         trail.append(jnp.sum(jnp.where(minor == major, other, 0.0), axis=0).astype(bf16))
-    send(jnp.concatenate(left, axis=1), TRIANGLES, BLOCK_ROWS)
-
-    copies[2].wait()
+    send(jnp.concatenate(left, axis=1), sorting, outs, TRIANGLES, BLOCK_ROWS)
     rows = [jnp.concatenate(trail, axis=1)]
     for part in three_parts(rhs[...]):
         rows.append(jnp.concatenate([part[16 * q : 16 * q + 16] for q in range(4)], axis=1))
-    send(jnp.concatenate(rows, axis=0), TRAIL, 64)
+    send(jnp.concatenate(rows, axis=0), sorting, outs, TRAIL, 64)
 
     copies[1].wait()
     interior = jnp.where(face_type[...] == 0, 2.0, 0.0)
@@ -142,18 +140,8 @@
     weights[0] = total
 
 
-def pack(rhs, pivot, coupling, diagonal, neighbours, face_type):
-    chunk = jax.ShapeDtypeStruct((CHUNK_ROWS, 128), bf16)
-    held = [pltpu.VMEM((4, 128), jnp.int32)] * 2 + [pltpu.VMEM((64, 128), f32)] + [pltpu.VMEM((64, 64, 128), bf16)] * 3
-    return pl.pallas_call(
-        pack_kernel,
-        out_shape=[chunk] * 4 + [jax.ShapeDtypeStruct((5, 16, 128), f32), jax.ShapeDtypeStruct((512, 512), bf16)],
-        in_specs=[HBM] * 6,
-        out_specs=[VMEM] * 6,
-        scratch_shapes=held + [pltpu.SemaphoreType.DMA((6,))],
-        compiler_params=params(),
-        name="pack",
-    )(*(pltpu.with_memory_space_constraint(x, pltpu.HBM) for x in (rhs, pivot, coupling, diagonal, neighbours, face_type)))
+def in_hbm(*arrays):
+    return [pltpu.with_memory_space_constraint(array, pltpu.HBM) for array in arrays]
 
 
 def to_packed(spread):
@@ -165,29 +153,31 @@
 
 def to_spread(packed):
     seg = segment_of((16, 128))
+    rolled = [packed] + [pltpu.roll(packed, 32 * k, 1) for k in (1, 2, 3)]
     parts = []
     for q in range(4):
-        part = jnp.where(seg == q, packed, 0.0)
-        part = part + pltpu.roll(part, 32, 1)
-        parts.append(part + pltpu.roll(part, 64, 1))
+        low = jnp.where(seg == 0, rolled[-q % 4], rolled[(1 - q) % 4])
+        high = jnp.where(seg == 2, rolled[(2 - q) % 4], rolled[(3 - q) % 4])
+        parts.append(jnp.where(seg < 2, low, high))
     return jnp.concatenate(parts, axis=0)
+
+
+def over_segments(value):
+    return (value + pltpu.roll(value, 32, 1)) + (pltpu.roll(value, 64, 1) + pltpu.roll(value, 96, 1))
 
 
 def transposed_times(blocks, elem, start, spread, row_ref):
     row_ref[...] = spread
     sums = [None] * 4
     for a in range(64):
-        block = blocks[elem, start + 16 * a : start + 16 * a + 16, :].astype(f32)
-        term = block * row_ref[a : a + 1, :]
+        term = blocks[elem, start + 16 * a : start + 16 * a + 16, :].astype(f32) * row_ref[a : a + 1, :]
         sums[a % 4] = term if sums[a % 4] is None else sums[a % 4] + term
     return (sums[0] + sums[1]) + (sums[2] + sums[3])
 
 
 def times(blocks, elem, start, packed):
     block = blocks[elem, start : start + BLOCK_ROWS, :].astype(f32).reshape(64, 16, 128)
-    total = jnp.sum(block * packed[None], axis=1)
-    total = total + pltpu.roll(total, 32, 1)
-    return total + pltpu.roll(total, 64, 1)
+    return over_segments(jnp.sum(block * packed[None], axis=1))
 
 
 def turn_segments(rows):
@@ -203,20 +193,20 @@
     return rows
 
 
-def unpack_triangles(triangles, trail, blocks, elem):
+def unpack(chunk, blocks, residual, elem, wide):
     shape = (16, 128)
     seg, m = segment_of(shape), row_of(shape)
-    turned = []
-    for q in range(4):
-        block = triangles[256 * q : 256 * q + 256, :].astype(f32).reshape(16, 16, 128)
-        turned.append(jnp.swapaxes(block, 0, 1))
+    blocks[elem, 0:BLOCK_ROWS, :] = chunk[COUPLING : COUPLING + BLOCK_ROWS, :]
+    wide[...] = chunk[TRIANGLES : TRIANGLES + BLOCK_ROWS, :].astype(f32)
+    trail = chunk[TRAIL : TRAIL + 64, :].astype(f32)
+    residual[elem] = (trail[16:32] + trail[32:48]) + trail[48:64]
     for k in range(16):
-        across = turn_segments([turned[q][k] for q in range(4)])
+        across = turn_segments([wide[pl.ds(256 * q + k, 16, stride=16), :] for q in range(4)])
         for q in range(4):
             a = 16 * q + k
-            here = triangles[16 * a : 16 * a + 16, :].astype(f32)
+            here = wide[16 * a : 16 * a + 16, :]
             below = (seg < q) | ((seg == q) & (m <= k))
-            diagonal = jnp.where((seg == q) & (m == k), trail, jnp.where(below, across[q], here))
+            diagonal = jnp.where((seg == q) & (m == k), trail[0:16], jnp.where(below, across[q], here))
             blocks[elem, PIVOT + 16 * a : PIVOT + 16 * a + 16, :] = jnp.where(below, here, across[q]).astype(bf16)
             blocks[elem, DIAGONAL + 16 * a : DIAGONAL + 16 * a + 16, :] = diagonal.astype(bf16)
 
@@ -282,29 +272,14 @@
     return jnp.sum(total, axis=0, keepdims=True)
 
 
-def solve_kernel(c0, c1, c2, c3, blocks, residual, values, upper, lower, triangles, row_ref, sems):
-    me = lax.axis_index("field")
-    copies = []
-    for d, source in enumerate((c0, c1, c2, c3)):
-        elem = (me - d) & 3
-        pairs = (
-            (source.at[TRIANGLES:CHUNK_ROWS, :], triangles.at[elem]),
-            (source.at[0:BLOCK_ROWS, :], blocks.at[elem, 0:BLOCK_ROWS, :]),
-        )
-        copies.append([pltpu.make_async_copy(*pair, sems.at[2 * d + k]) for k, pair in enumerate(pairs)])
-    for group in copies:
-        for copy in group:
-            copy.start()
-    for group in copies:
-        for copy in group:
-            copy.wait()
-    parts = []
-    for elem in range(4):
-        trail = triangles[elem, BLOCK_ROWS : BLOCK_ROWS + 64, :].astype(f32)
-        parts.append((trail[16:32] + trail[32:48]) + trail[48:64])
-        residual[elem] = parts[elem]
-        unpack_triangles(triangles.at[elem], trail[0:16], blocks, elem)
-    packed = [to_packed(v) for v in line_solve(parts, blocks, row_ref)]
+def unpack_kernel(distance, *refs):
+    *_, chunk, blocks, residual, wide = refs
+    unpack(chunk, blocks, residual, (lax.axis_index("field") - distance) & 3, wide)
+
+
+def solve_kernel(blocks_before, residual_before, chunk, blocks, residual, values, upper, lower, row_ref, wide):
+    unpack(chunk, blocks, residual, (lax.axis_index("field") - 2) & 3, wide)
+    packed = [to_packed(v) for v in line_solve([residual[elem] for elem in range(4)], blocks, row_ref)]
     for elem in range(4):
         values[elem] = packed[elem]
     send_faces(packed, upper, lower)
@@ -385,13 +360,14 @@
 BLOCKS = jax.ShapeDtypeStruct((4, ELEMENT_ROWS, 128), bf16)
 
 
-def kernel(body, arrays, outs, name, spec=VMEM, scratch=()):
+def kernel(body, arrays, outs, name, spec=VMEM, scratch=(), aliases=None):
     return pl.pallas_call(
         body,
         out_shape=outs,
-        in_specs=[spec] * len(arrays),
+        in_specs=spec if isinstance(spec, list) else [spec] * len(arrays),
         out_specs=[VMEM] * len(outs),
         scratch_shapes=list(scratch),
+        input_output_aliases=aliases or {},
         compiler_params=params(),
         name=name,
     )(*arrays)
@@ -419,19 +395,35 @@
 
 
 def local(rhs, pivot_inverse, line_coupling, element_block, neighbours, face_type):
-    *chunks, weights, order = pack(
-        rhs[0], pivot_inverse[0], line_coupling[0], element_block[0], neighbours.T, face_type.T
-    )
-    received = [chunks[0]] + [around(chunks[d], d) for d in (1, 2, 3)]
-    spread = pltpu.VMEM((64, 128), f32)
-    triangles = pltpu.VMEM((4, CHUNK_ROWS - TRIANGLES, 128), bf16)
+    matrix, small = pltpu.VMEM((64, 64, 128), bf16), pltpu.VMEM((4, 128), jnp.int32)
+    spread, wide = pltpu.VMEM((64, 128), f32), pltpu.VMEM((BLOCK_ROWS, 128), f32)
+    *chunks, weights, order = kernel(
+        pack_kernel,
+        in_hbm(neighbours.T, face_type.T, rhs[0], line_coupling[0], pivot_inverse[0], element_block[0]),
+        [jax.ShapeDtypeStruct((CHUNK_ROWS, 128), bf16)] * 4
+        + [jax.ShapeDtypeStruct((5, 16, 128), f32), jax.ShapeDtypeStruct((512, 512), bf16)],
+        "pack",
+        HBM,
+        [small, small, pltpu.VMEM((64, 128), f32), matrix, matrix, matrix, pltpu.SemaphoreType.DMA((6,))],
+    )
+    held = []
+    arrived = {d: around(chunks[d], d) if d else chunks[0] for d in (0, 1, 3, 2)}
+    for d in (0, 1, 3):
+        held = kernel(
+            functools.partial(unpack_kernel, d),
+            [*held, arrived[d]],
+            [BLOCKS, VECTOR],
+            f"unpack_{d}",
+            scratch=[wide],
+            aliases={0: 0, 1: 1} if held else None,
+        )
     blocks, r, z, upper, lower = kernel(
         solve_kernel,
-        received,
+        [*held, arrived[2]],
         [BLOCKS, VECTOR, VECTOR, FACE, FACE],
         "solve_first",
-        pl.BlockSpec(memory_space=pl.ANY),
-        [triangles, spread, pltpu.SemaphoreType.DMA((8,))],
+        scratch=[spread, wide],
+        aliases={0: 0, 1: 1},
     )
     before, after = exchange(upper, lower)
     (partial,) = kernel(apply_kernel, [blocks, z, weights], [VECTOR], "apply_first", scratch=[spread])

time: 88.9 us -> 85 us (0.956)
  Pallas kernels: 15.1 us -> 12.8 us
  starting transfers between devices: 21.3 us -> 20.3 us
    pallas_call x7 -> x10, Pallas kernels: 15.1 us -> 12.8 us  [kernel(): pl.pallas_call(body, out_shape=outs, in_specs=spec if isinstance(spec, li...]
  transfers between devices with their start and end apart: 10 -> 10, of which waited for: 7 -> 7; matrix products, arithmetic and copies ran while one was open for 0% -> 0% of each run, Pallas kernels for 2% -> 4%
where the time goes in v3:
time: 85 us; the launch traced here: 84.8 us
  waiting for transfers between devices  28.7 us (34%)
  blocking collectives  22.2 us (26%)
  starting transfers between devices  20.3 us (24%)
  Pallas kernels  12.8 us (15%)
    ppermute x6, waiting for transfers between devices, around(): lax.ppermute(value, 'field', [(i, (i + distance) % count) for i in range(...  24.2 us
    all_to_all x1, blocking collectives, local(): sums = lax.all_to_all(rows, 'cross', 0, 0)  22.2 us
    pallas_call x10, Pallas kernels, kernel(): pl.pallas_call(body, out_shape=outs, in_specs=spec if isinstance(spec, li...  12.8 us
    ppermute x2, starting transfers between devices, exchange(): before = lax.ppermute(upper, ('field', 'cross'), column_pairs(1))  8.59 us
    ppermute x6, starting transfers between devices, around(): lax.ppermute(value, 'field', [(i, (i + distance) % count) for i in range(...  7.86 us
    ppermute x2, waiting for transfers between devices, exchange(): after = lax.ppermute(lower, ('field', 'cross'), column_pairs(-1))  4.52 us
    ppermute x2, starting transfers between devices, exchange(): after = lax.ppermute(lower, ('field', 'cross'), column_pairs(-1))  3.84 us
  transfers between devices with their start and end apart: 10, of which 7 were waited for; matrix products, arithmetic and copies ran while one was open for 0% of the time, Pallas kernels for 4%

profile of v3, /device:TPU:1, one launch (start us, length us, event | category | flops | bytes accessed | tf_op | source)
XLA Modules:
  0.0 84.8 jit_solution(1678180718445861683)
XLA Ops:
  0.6 3.5 %pack.1 = (bf16[2112,128]{1,0:T(8,128)(2,1)S(1)}, bf16[2112,128]{1,0:T(8,128)(2,1)S(1)}, bf16[2112,128]{1,0:T(8,128)(2,1)S(1)}, bf16[2112,128]{1,0:T(8,128)(2,1)...) custom-call(s32[4,128]{1,0:T(4,128)} %bitcast.16, s32[4,128]{1,0:T(4,128)} %bitcast.17, ...), custom_call_target="tpu_custom_call" | custom-call | tf_op jit(solution)/shard_map/pack/pallas_call | solution.py:364
  4.1 2.1 %collective-permute-start = (bf16[2112,128]{1,0:T(8,128)(2,1)S(1)}, bf16[2112,128]{1,0:T(8,128)(2,1)S(1)}, u32[]{:S(2)}, u32[]{:S(2)}) collective-permute-start(bf16[2112,128]{1,0:T(8,128)(2,1)S(1)} %get-tuple-element.34), channel_id=1, source_target_pairs={{0,64},{64,128},{128,192},{192,0},{1,65},{65,129},{129,193},{193,1... | collective-permute-start | bytes 1622024 | tf_op jit(solution)/shard_map/ppermute | solution.py:378
  6.2 1.4 %collective-permute-start.1 = (bf16[2112,128]{1,0:T(8,128)(2,1)S(1)}, bf16[2112,128]{1,0:T(8,128)(2,1)S(1)}, u32[]{:S(2)}, u32[]{:S(2)}) collective-permute-start(bf16[2112,128]{1,0:T(8,128)(2,1)S(1)} %get-tuple-element.37), channel_id=1, source_target_pairs={{0,192},{64,0},{128,64},{192,128},{1,193},{65,1},{129,65},{193,129... | collective-permute-start | bytes 1622024 | tf_op jit(solution)/shard_map/ppermute | solution.py:378
  7.6 1.6 %collective-permute-start.2 = (bf16[2112,128]{1,0:T(8,128)(2,1)S(1)}, bf16[2112,128]{1,0:T(8,128)(2,1)S(1)}, u32[]{:S(2)}, u32[]{:S(2)}) collective-permute-start(bf16[2112,128]{1,0:T(8,128)(2,1)S(1)} %get-tuple-element.40), channel_id=1, source_target_pairs={{0,128},{64,192},{128,0},{192,64},{1,129},{65,193},{129,1},{193,65... | collective-permute-start | bytes 1622024 | tf_op jit(solution)/shard_map/ppermute | solution.py:378
  9.8 7.4 %collective-permute-done.refs_2_ = bf16[2112,128]{1,0:T(8,128)(2,1)S(1)} collective-permute-done((bf16[2112,128]{1,0:T(8,128)(2,1)S(1)}, bf16[2112,128]{1,0:T(8,128)(2,1)S(1)}, u32[]{:S(2)}, u32[]{:S(2)}) %collective-permute-start) | collective-permute-done | bytes 540704 | tf_op jit(solution)/shard_map/ppermute | solution.py:378
  17.2 0.6 unpack_1.1
  17.8 0.9 %collective-permute-done.1.refs_2_ = bf16[2112,128]{1,0:T(8,128)(2,1)S(1)} collective-permute-done((bf16[2112,128]{1,0:T(8,128)(2,1)S(1)}, bf16[2112,128]{1,0:T(8,128)(2,1)S(1)}, u32[]{:S(2)}, u32[]{:S(2)}) %collective-permute-start.1) | collective-permute-done | bytes 540704 | tf_op jit(solution)/shard_map/ppermute | solution.py:378
  19.3 12.6 %collective-permute-done.2.chunk = bf16[2112,128]{1,0:T(8,128)(2,1)S(1)} collective-permute-done((bf16[2112,128]{1,0:T(8,128)(2,1)S(1)}, bf16[2112,128]{1,0:T(8,128)(2,1)S(1)}, u32[]{:S(2)}, u32[]{:S(2)}) %collective-permute-start.2) | collective-permute-done | bytes 540704 | tf_op jit(solution)/shard_map/ppermute | solution.py:378
  31.9 1.9 %solve_first.1 = (bf16[4,3072,128]{2,1,0:T(8,128)(2,1)S(1)}, f32[4,16,128]{2,1,0:T(8,128)S(1)}, f32[4,16,128]{2,1,0:T(8,128)S(1)}, f32[16,128]{1,0:T(8,128)S(1)}, f32[16,128]{1,0:T(8,128)S(1)}) custom-call(bf16[4,3072,128]{2,1,0:T(8,128)(2,1)S(1)} %get-tuple-element.38.blocks_before, ...), custom_call_target="tpu_custom_call", output_to_operand_aliasing={{0}: (0, {}), {1}: (1, {})} | custom-call | tf_op jit(solution)/shard_map/solve_first/pallas_call | solution.py:364
  33.8 5.0 %collective-permute-start.3 = (f32[16,128]{1,0:T(8,128)S(1)}, f32[16,128]{1,0:T(8,128)S(1)}, u32[]{:S(2)}, u32[]{:S(2)}) collective-permute-start(f32[16,128]{1,0:T(8,128)S(1)} %get-tuple-element.44), channel_id=1, source_target_pairs={{0,64},{64,128},{128,192},{192,193},{193,129},{129,65},{65,1},{1,2... | collective-permute-start | bytes 24584 | tf_op jit(solution)/shard_map/ppermute | solution.py:392
  38.8 1.9 %collective-permute-start.4 = (f32[16,128]{1,0:T(8,128)S(1)}, f32[16,128]{1,0:T(8,128)S(1)}, u32[]{:S(2)}, u32[]{:S(2)}) collective-permute-start(f32[16,128]{1,0:T(8,128)S(1)} %get-tuple-element.45), channel_id=1, source_target_pairs={{64,0},{128,64},{192,128},{193,192},{129,193},{65,129},{1,65},{2,1... | collective-permute-start | bytes 24584 | tf_op jit(solution)/shard_map/ppermute | solution.py:393
  40.7 0.8 apply_first.1.partial
  41.5 2.3 %collective-permute-done.4.after = f32[16,128]{1,0:T(8,128)S(1)} collective-permute-done((f32[16,128]{1,0:T(8,128)S(1)}, f32[16,128]{1,0:T(8,128)S(1)}, u32[]{:S(2)}, u32[]{:S(2)}) %collective-permute-start.4) | collective-permute-done | bytes 8224 | tf_op jit(solution)/shard_map/ppermute | solution.py:393
  43.7 1.5 %solve_second.1 = (f32[4,16,128]{2,1,0:T(8,128)S(1)}, f32[4,16,128]{2,1,0:T(8,128)S(1)}, f32[16,128]{1,0:T(8,128)S(1)}, f32[16,128]{1,0:T(8,128)S(1)}) custom-call(bf16[4,3072,128]{2,1,0:T(8,128)(2,1)S(1)} %get-tuple-element.41.blocks, f32[4,16,128]{2,1,0:T(8,128)S(1)} %apply_first.1.partial, f32[16,128]{1,0:T(8,128)S(1)} %collective-permute-done.3.before, ...), custom_call_target="tpu_custom_call" | custom-call | tf_op jit(solution)/shard_map/solve_second/pallas_call | solution.py:364
  45.3 3.6 %collective-permute-start.5 = (f32[16,128]{1,0:T(8,128)S(1)}, f32[16,128]{1,0:T(8,128)S(1)}, u32[]{:S(2)}, u32[]{:S(2)}) collective-permute-start(f32[16,128]{1,0:T(8,128)S(1)} %get-tuple-element.47), channel_id=1, source_target_pairs={{0,64},{64,128},{128,192},{192,193},{193,129},{129,65},{65,1},{1,2... | collective-permute-start | bytes 24584 | tf_op jit(solution)/shard_map/ppermute | solution.py:392
  48.9 1.9 %collective-permute-start.6 = (f32[16,128]{1,0:T(8,128)S(1)}, f32[16,128]{1,0:T(8,128)S(1)}, u32[]{:S(2)}, u32[]{:S(2)}) collective-permute-start(f32[16,128]{1,0:T(8,128)S(1)} %get-tuple-element.48), channel_id=1, source_target_pairs={{64,0},{128,64},{192,128},{193,192},{129,193},{65,129},{1,65},{2,1... | collective-permute-start | bytes 24584 | tf_op jit(solution)/shard_map/ppermute | solution.py:393
  50.8 0.8 apply_second.1.partial
  51.6 2.3 %collective-permute-done.6.after = f32[16,128]{1,0:T(8,128)S(1)} collective-permute-done((f32[16,128]{1,0:T(8,128)S(1)}, f32[16,128]{1,0:T(8,128)S(1)}, u32[]{:S(2)}, u32[]{:S(2)}) %collective-permute-start.6) | collective-permute-done | bytes 8224 | tf_op jit(solution)/shard_map/ppermute | solution.py:393
  53.9 1.5 %solve_last.1 = (f32[88,128]{1,0:T(8,128)S(1)}, f32[88,128]{1,0:T(8,128)S(1)}, f32[88,128]{1,0:T(8,128)S(1)}, f32[88,128]{1,0:T(8,128)S(1)}) custom-call(bf16[4,3072,128]{2,1,0:T(8,128)(2,1)S(1)} %get-tuple-element.41.blocks, f32[4,16,128]{2,1,0:T(8,128)S(1)} %apply_second.1.partial, f32[16,128]{1,0:T(8,128)S(1)} %collective-permute-done.5.before, ...), custom_call_target="tpu_custom_call" | custom-call | tf_op jit(solution)/shard_map/solve_last/pallas_call | solution.py:364
  55.5 2.6 %collective-permute-start.9 = (f32[88,128]{1,0:T(8,128)S(1)}, f32[88,128]{1,0:T(8,128)S(1)}, u32[]{:S(2)}, u32[]{:S(2)}) collective-permute-start(f32[88,128]{1,0:T(8,128)S(1)} %get-tuple-element.54), channel_id=1, source_target_pairs={{0,192},{64,0},{128,64},{192,128},{1,193},{65,1},{129,65},{193,129... | collective-permute-start | bytes 135176 | tf_op jit(solution)/shard_map/ppermute | solution.py:378
  58.1 2.4 %collective-permute-done.7.b1 = f32[88,128]{1,0:T(8,128)S(1)} collective-permute-done((f32[88,128]{1,0:T(8,128)S(1)}, f32[88,128]{1,0:T(8,128)S(1)}, u32[]{:S(2)}, u32[]{:S(2)}) %collective-permute-start.7) | collective-permute-done | bytes 45088 | tf_op jit(solution)/shard_map/ppermute | solution.py:378
  60.5 0.9 %collective-permute-done.9.b3 = f32[88,128]{1,0:T(8,128)S(1)} collective-permute-done((f32[88,128]{1,0:T(8,128)S(1)}, f32[88,128]{1,0:T(8,128)S(1)}, u32[]{:S(2)}, u32[]{:S(2)}) %collective-permute-start.9) | collective-permute-done | bytes 45088 | tf_op jit(solution)/shard_map/ppermute | solution.py:378
  61.4 22.2 %all_to_all.5.sums = f32[64,1,128]{2,1,0:T(1,128)S(1)} all-to-all(f32[64,1,128]{2,1,0:T(1,128)S(1)} %broadcast_in_dim.18), channel_id=1, replica_groups=mesh['field'=4,'cross'=64] {'cross'}, dimensions={0} | all-to-all | bytes 65536 | tf_op jit(solution)/shard_map/all_to_all | solution.py:449
  83.7 1.1 %final.1 = (f32[64,128]{1,0:T(8,128)}, f32[64,128]{1,0:T(8,128)}, f32[64,128]{1,0:T(8,128)}) custom-call(f32[64,1,128]{2,1,0:T(1,128)S(1)} %all_to_all.5.sums, f32[64,128]{1,0:T(8,128)S(1)} %bitcast.12, f32[88,128]{1,0:T(8,128)S(1)} %get-tuple-element.51.b0, f32[88,128]{1,0:T(8,128)S(1)} %collective-permute-done.7.b1, ...), custom_call_target="tpu_custom_call" | custom-call | tf_op jit(solution)/shard_map/final/pallas_call | solution.py:364
  (11 shorter events, 1.4 us)
Async XLA Ops:
  4.1 13.1 %collective-permute-start = (bf16[2112,128]{1,0:T(8,128)(2,1)S(1)}, bf16[2112,128]{1,0:T(8,128)(2,1)S(1)}, u32[]{:S(2)}, u32[]{:S(2)}) collective-permute-start(bf16[2112,128]{1,0:T(8,128)(2,1)S(1)} %get-tuple-element.34), channel_id=1, source_target_pairs={{0,64},{64,128},{128,192},{192,0},{1,65},{65,129},{129,193},{193,1... | collective-permute-start | bytes 1622024 | tf_op jit(solution)/shard_map/ppermute | solution.py:378
  6.2 12.5 %collective-permute-start.1 = (bf16[2112,128]{1,0:T(8,128)(2,1)S(1)}, bf16[2112,128]{1,0:T(8,128)(2,1)S(1)}, u32[]{:S(2)}, u32[]{:S(2)}) collective-permute-start(bf16[2112,128]{1,0:T(8,128)(2,1)S(1)} %get-tuple-element.37), channel_id=1, source_target_pairs={{0,192},{64,0},{128,64},{192,128},{1,193},{65,1},{129,65},{193,129... | collective-permute-start | bytes 1622024 | tf_op jit(solution)/shard_map/ppermute | solution.py:378
  7.6 24.4 %collective-permute-start.2 = (bf16[2112,128]{1,0:T(8,128)(2,1)S(1)}, bf16[2112,128]{1,0:T(8,128)(2,1)S(1)}, u32[]{:S(2)}, u32[]{:S(2)}) collective-permute-start(bf16[2112,128]{1,0:T(8,128)(2,1)S(1)} %get-tuple-element.40), channel_id=1, source_target_pairs={{0,128},{64,192},{128,0},{192,64},{1,129},{65,193},{129,1},{193,65... | collective-permute-start | bytes 1622024 | tf_op jit(solution)/shard_map/ppermute | solution.py:378
  33.8 7.7 %collective-permute-start.3 = (f32[16,128]{1,0:T(8,128)S(1)}, f32[16,128]{1,0:T(8,128)S(1)}, u32[]{:S(2)}, u32[]{:S(2)}) collective-permute-start(f32[16,128]{1,0:T(8,128)S(1)} %get-tuple-element.44), channel_id=1, source_target_pairs={{0,64},{64,128},{128,192},{192,193},{193,129},{129,65},{65,1},{1,2... | collective-permute-start | bytes 24584 | tf_op jit(solution)/shard_map/ppermute | solution.py:392
  38.8 5.0 %collective-permute-start.4 = (f32[16,128]{1,0:T(8,128)S(1)}, f32[16,128]{1,0:T(8,128)S(1)}, u32[]{:S(2)}, u32[]{:S(2)}) collective-permute-start(f32[16,128]{1,0:T(8,128)S(1)} %get-tuple-element.45), channel_id=1, source_target_pairs={{64,0},{128,64},{192,128},{193,192},{129,193},{65,129},{1,65},{2,1... | collective-permute-start | bytes 24584 | tf_op jit(solution)/shard_map/ppermute | solution.py:393
  45.3 6.3 %collective-permute-start.5 = (f32[16,128]{1,0:T(8,128)S(1)}, f32[16,128]{1,0:T(8,128)S(1)}, u32[]{:S(2)}, u32[]{:S(2)}) collective-permute-start(f32[16,128]{1,0:T(8,128)S(1)} %get-tuple-element.47), channel_id=1, source_target_pairs={{0,64},{64,128},{128,192},{192,193},{193,129},{129,65},{65,1},{1,2... | collective-permute-start | bytes 24584 | tf_op jit(solution)/shard_map/ppermute | solution.py:392
  48.9 5.0 %collective-permute-start.6 = (f32[16,128]{1,0:T(8,128)S(1)}, f32[16,128]{1,0:T(8,128)S(1)}, u32[]{:S(2)}, u32[]{:S(2)}) collective-permute-start(f32[16,128]{1,0:T(8,128)S(1)} %get-tuple-element.48), channel_id=1, source_target_pairs={{64,0},{128,64},{192,128},{193,192},{129,193},{65,129},{1,65},{2,1... | collective-permute-start | bytes 24584 | tf_op jit(solution)/shard_map/ppermute | solution.py:393
  50.8 32.9 %copy-start = (f32[1,64,128]{2,1,0:T(8,128)S(1)}, f32[1,64,128]{2,1,0:T(8,128)}, u32[]{:S(2)}) copy-start(f32[1,64,128]{2,1,0:T(8,128)} %param.6) | copy-start | bytes 98308
  55.4 5.2 %collective-permute-start.7 = (f32[88,128]{1,0:T(8,128)S(1)}, f32[88,128]{1,0:T(8,128)S(1)}, u32[]{:S(2)}, u32[]{:S(2)}) collective-permute-start(f32[88,128]{1,0:T(8,128)S(1)} %get-tuple-element.52), channel_id=1, source_target_pairs={{0,64},{64,128},{128,192},{192,0},{1,65},{65,129},{129,193},{193,1... | collective-permute-start | bytes 135176 | tf_op jit(solution)/shard_map/ppermute | solution.py:378
  55.4 5.1 %collective-permute-start.8 = (f32[88,128]{1,0:T(8,128)S(1)}, f32[88,128]{1,0:T(8,128)S(1)}, u32[]{:S(2)}, u32[]{:S(2)}) collective-permute-start(f32[88,128]{1,0:T(8,128)S(1)} %get-tuple-element.53), channel_id=1, source_target_pairs={{0,128},{64,192},{128,0},{192,64},{1,129},{65,193},{129,1},{193,65... | collective-permute-start | bytes 135176 | tf_op jit(solution)/shard_map/ppermute | solution.py:378
  55.5 5.9 %collective-permute-start.9 = (f32[88,128]{1,0:T(8,128)S(1)}, f32[88,128]{1,0:T(8,128)S(1)}, u32[]{:S(2)}, u32[]{:S(2)}) collective-permute-start(f32[88,128]{1,0:T(8,128)S(1)} %get-tuple-element.54), channel_id=1, source_target_pairs={{0,192},{64,0},{128,64},{192,128},{1,193},{65,1},{129,65},{193,129... | collective-permute-start | bytes 135176 | tf_op jit(solution)/shard_map/ppermute | solution.py:378

commit v4 on v3

--- a/solution.py
+++ b/solution.py
@@ -9,10 +9,12 @@
 
 
 BLOCK_ROWS = 1024
-COUPLING, TRIANGLES, TRAIL = (0, 1024, 2048)
-CHUNK_ROWS = 2048 + 64
-PIVOT, DIAGONAL = (1024, 2048)
-ELEMENT_ROWS = 3072
+COUPLING, WIDE, SHORT, CORNER, RESIDUAL = (0, 1024, 1280, 1408, 1664)
+FIRST_ROWS = 1664 + 48
+SECOND_WIDE, SECOND_SHORT, SECOND_DIAGONAL = (0, 256, 384)
+SECOND_ROWS = 384 + 16
+PIVOT = 1024
+ELEMENT_ROWS = 2048
 VMEM_LIMIT = 24 * 1024 * 1024
 
 VMEM = pl.BlockSpec(memory_space=pltpu.VMEM)
@@ -63,10 +65,33 @@
         outs[d][start : start + rows, :] = result[:, d * 128 : (d + 1) * 128]
 
 
-def pack_kernel(neighbours, face_type, rhs, coupling, pivot, diagonal, out0, out1, out2, out3, weights, order, *scratch):
+def parts_below(block):
+    def part(rows, column):
+        return block[rows, 16 * column : 16 * column + 16, :].reshape(-1, 128)
+
+    last, upper, lower = slice(48, 64), slice(32, 40), slice(40, 48)
+    wide = [part(last, 0), part(last, 1), part(last, 2), part(slice(16, 32), 0)]
+    short = [part(upper, 0), part(upper, 1), part(lower, 0), part(lower, 1)]
+    return [jnp.concatenate(wide, axis=1), jnp.concatenate(short, axis=1)]
+
+
+def corner_orders():
+    shape = (16, 16, 128)
+    return lax.broadcasted_iota(jnp.int32, shape, 0), lax.broadcasted_iota(jnp.int32, shape, 1)
+
+
+def pack_first_kernel(
+    neighbours, face_type, rhs, coupling, pivot, diagonal, out0, out1, out2, out3, weights, order, *scratch
+):
     *held, sems = scratch
-    copies = start_fetch((neighbours, face_type, rhs, coupling, pivot, diagonal), held, sems)
-    neighbours, face_type, rhs, coupling, pivot, diagonal = held
+    sources = [neighbours, face_type, rhs, coupling, pivot]
+    targets = list(held[:5])
+    for q in range(4):
+        here = slice(16 * q, 16 * q + 16)
+        sources.append(diagonal.at[here, here, :])
+        targets.append(held[5].at[q])
+    copies = start_fetch(sources, targets, sems)
+    neighbours, face_type, rhs, coupling, pivot, corners = held
     me, cross = lax.axis_index("field"), lax.axis_index("cross")
     square = (128, 128)
     lane = lax.broadcasted_iota(jnp.int32, square, 1)
@@ -104,26 +129,18 @@
     left = [coupling[:, 16 * q : 16 * q + 16, :].reshape(BLOCK_ROWS, 128) for q in range(4)]
     send(jnp.concatenate(left, axis=1), sorting, outs, COUPLING, BLOCK_ROWS)
 
-    for copy in (copies[2], copies[4], copies[5]):
+    for copy in (copies[2], *copies[4:]):
         copy.wait()
-    corner = (16, 16, 128)
-    major, minor = lax.broadcasted_iota(jnp.int32, corner, 0), lax.broadcasted_iota(jnp.int32, corner, 1)
-    left, trail = [], []
+    major, minor = corner_orders()
+    shared = []
     for q in range(4):
         here = slice(16 * q, 16 * q + 16)
-        own, other = pivot[here, here, :].astype(f32), diagonal[here, here, :].astype(f32)
-        parts = [jnp.where(minor <= major, own, other).astype(bf16)]
-        if q > 0:
-            parts = [diagonal[0 : 16 * q, here, :]] + parts
-        if q < 3:
-            parts = parts + [pivot[16 * q + 16 : 64, here, :]]
-        left.append(jnp.concatenate(parts, axis=0).reshape(BLOCK_ROWS, 128))
-        trail.append(jnp.sum(jnp.where(minor == major, other, 0.0), axis=0).astype(bf16))
-    send(jnp.concatenate(left, axis=1), sorting, outs, TRIANGLES, BLOCK_ROWS)
-    rows = [jnp.concatenate(trail, axis=1)]
+        own, other = pivot[here, here, :].astype(f32), corners[q].astype(f32)
+        shared.append(jnp.where(minor <= major, own, other).astype(bf16).reshape(256, 128))
+    rows = parts_below(pivot) + [jnp.concatenate(shared, axis=1)]
     for part in three_parts(rhs[...]):
         rows.append(jnp.concatenate([part[16 * q : 16 * q + 16] for q in range(4)], axis=1))
-    send(jnp.concatenate(rows, axis=0), sorting, outs, TRAIL, 64)
+    send(jnp.concatenate(rows, axis=0), sorting, outs, WIDE, FIRST_ROWS - WIDE)
 
     copies[1].wait()
     interior = jnp.where(face_type[...] == 0, 2.0, 0.0)
@@ -140,6 +157,18 @@
     weights[0] = total
 
 
+def pack_second_kernel(diagonal, order, after, out0, out1, out2, out3, held, sems):
+    (copy,) = start_fetch([diagonal], [held], sems)
+    copy.wait()
+    major, minor = corner_orders()
+    trail = []
+    for q in range(4):
+        here = slice(16 * q, 16 * q + 16)
+        trail.append(jnp.sum(jnp.where(minor == major, held[here, here, :].astype(f32), 0.0), axis=0).astype(bf16))
+    rows = parts_below(held) + [jnp.concatenate(trail, axis=1)]
+    send(jnp.concatenate(rows, axis=0), order[...], (out0, out1, out2, out3), 0, SECOND_ROWS)
+
+
 def in_hbm(*arrays):
     return [pltpu.with_memory_space_constraint(array, pltpu.HBM) for array in arrays]
 
@@ -193,22 +222,49 @@
     return rows
 
 
-def unpack(chunk, blocks, residual, elem, wide):
+def spread_parts(wide, parts, corner):
+    seg = segment_of((16, 128))
+    for k in range(16):
+        diagonal = corner[16 * k : 16 * k + 16, :].astype(f32)
+        last = parts[16 * k : 16 * k + 16, :].astype(f32)
+        third = parts[256 + 16 * (k % 8) : 272 + 16 * (k % 8), :].astype(f32)
+        if k >= 8:
+            third = pltpu.roll(third, 64, 1)
+        wide[16 * k : 16 * k + 16, :] = diagonal
+        wide[256 + 16 * k : 272 + 16 * k, :] = jnp.where(seg == 0, pltpu.roll(last, 32, 1), diagonal)
+        wide[512 + 16 * k : 528 + 16 * k, :] = jnp.where(seg == 2, diagonal, third)
+        wide[768 + 16 * k : 784 + 16 * k, :] = jnp.where(seg == 3, diagonal, last)
+
+
+def unpack_pivot(chunk, blocks, residual, elem, wide):
     shape = (16, 128)
     seg, m = segment_of(shape), row_of(shape)
     blocks[elem, 0:BLOCK_ROWS, :] = chunk[COUPLING : COUPLING + BLOCK_ROWS, :]
-    wide[...] = chunk[TRIANGLES : TRIANGLES + BLOCK_ROWS, :].astype(f32)
-    trail = chunk[TRAIL : TRAIL + 64, :].astype(f32)
-    residual[elem] = (trail[16:32] + trail[32:48]) + trail[48:64]
+    part = chunk[RESIDUAL : RESIDUAL + 48, :].astype(f32)
+    residual[elem] = (part[0:16] + part[16:32]) + part[32:48]
+    spread_parts(wide, chunk.at[WIDE:CORNER, :], chunk.at[CORNER:RESIDUAL, :])
     for k in range(16):
         across = turn_segments([wide[pl.ds(256 * q + k, 16, stride=16), :] for q in range(4)])
         for q in range(4):
             a = 16 * q + k
-            here = wide[16 * a : 16 * a + 16, :]
             below = (seg < q) | ((seg == q) & (m <= k))
-            diagonal = jnp.where((seg == q) & (m == k), trail[0:16], jnp.where(below, across[q], here))
-            blocks[elem, PIVOT + 16 * a : PIVOT + 16 * a + 16, :] = jnp.where(below, here, across[q]).astype(bf16)
-            blocks[elem, DIAGONAL + 16 * a : DIAGONAL + 16 * a + 16, :] = diagonal.astype(bf16)
+            value = jnp.where(below, wide[16 * a : 16 * a + 16, :], across[q])
+            blocks[elem, PIVOT + 16 * a : PIVOT + 16 * a + 16, :] = value.astype(bf16)
+
+
+def unpack_diagonal(first, second, diagonals, elem, wide):
+    shape = (16, 128)
+    seg, m = segment_of(shape), row_of(shape)
+    trail = second[SECOND_DIAGONAL:SECOND_ROWS, :].astype(f32)
+    spread_parts(wide, second.at[0:SECOND_DIAGONAL, :], first.at[CORNER:RESIDUAL, :])
+    for k in range(16):
+        across = turn_segments([wide[pl.ds(256 * q + k, 16, stride=16), :] for q in range(4)])
+        for q in range(4):
+            a = 16 * q + k
+            here = (seg < q) | ((seg == q) & (m > k))
+            value = jnp.where(here, wide[16 * a : 16 * a + 16, :], across[q])
+            value = jnp.where((seg == q) & (m == k), trail, value)
+            diagonals[elem, 16 * a : 16 * a + 16, :] = value.astype(bf16)
 
 
 def line_solve(residual, blocks, row_ref):
@@ -230,22 +286,27 @@
     return values
 
 
-def send_faces(packed, upper, lower):
+def is_even_column():
+    return (lax.axis_index("field") + lax.axis_index("cross")) % 2 == 0
+
+
+def send_faces(packed, inner, outer):
     seg = segment_of((16, 128))
-    to_next, to_before = jnp.zeros((16, 128), f32), jnp.zeros((16, 128), f32)
-    for elem in range(4):
-        to_next = jnp.where(seg == elem, pltpu.roll(packed[elem], (32 * (elem + 1)) % 128, 1) if elem < 3 else packed[elem], to_next)
-        to_before = jnp.where(seg == elem, pltpu.roll(packed[elem], 32 * elem, 1) if elem > 0 else packed[elem], to_before)
-    upper[...] = to_next
-    lower[...] = to_before
-
-
-def line_apply(packed, blocks, weights, row_ref):
+    to_next, to_before = packed[3], packed[0]
+    for elem in range(3):
+        to_next = jnp.where(seg == elem, pltpu.roll(packed[elem], 32 * (elem + 1), 1), to_next)
+        to_before = jnp.where(seg == elem + 1, pltpu.roll(packed[elem + 1], 32 * (elem + 1), 1), to_before)
+    even = is_even_column()
+    inner[...] = jnp.where(even, to_next, to_before)
+    outer[...] = jnp.where(even, to_before, to_next)
+
+
+def line_apply(packed, blocks, diagonals, weights, row_ref):
     spread = [to_spread(v) for v in packed]
     rows = []
     for elem in range(4):
         v = packed[elem]
-        total = transposed_times(blocks, elem, DIAGONAL, spread[elem], row_ref)
+        total = transposed_times(diagonals, elem, 0, spread[elem], row_ref)
         if elem > 0:
             total = total + to_packed(times(blocks, elem, COUPLING, packed[elem - 1]))
         if elem < 3:
@@ -256,11 +317,14 @@
     return rows
 
 
-def add_faces(partial, before, after, weights):
+def add_faces(partial, inner, outer, weights):
+    even = is_even_column()
+    before = jnp.where(even, outer[...], inner[...])
+    after = jnp.where(even, inner[...], outer[...])
     rows = []
     for elem in range(4):
-        left = before[...] if elem == 0 else pltpu.roll(before[...], 128 - 32 * elem, 1)
-        right = after[...] if elem == 3 else pltpu.roll(after[...], 32 * (3 - elem), 1)
+        left = before if elem == 0 else pltpu.roll(before, 128 - 32 * elem, 1)
+        right = after if elem == 3 else pltpu.roll(after, 32 * (3 - elem), 1)
         rows.append(partial[elem] - weights[1] * left - weights[2] * right)
     return rows
 
@@ -274,34 +338,39 @@
 
 def unpack_kernel(distance, *refs):
     *_, chunk, blocks, residual, wide = refs
-    unpack(chunk, blocks, residual, (lax.axis_index("field") - distance) & 3, wide)
-
-
-def solve_kernel(blocks_before, residual_before, chunk, blocks, residual, values, upper, lower, row_ref, wide):
-    unpack(chunk, blocks, residual, (lax.axis_index("field") - 2) & 3, wide)
+    unpack_pivot(chunk, blocks, residual, (lax.axis_index("field") - distance) & 3, wide)
+
+
+def solve_kernel(blocks_before, residual_before, chunk, blocks, residual, values, inner_out, outer_out, row_ref, wide):
+    unpack_pivot(chunk, blocks, residual, (lax.axis_index("field") - 2) & 3, wide)
     packed = [to_packed(v) for v in line_solve([residual[elem] for elem in range(4)], blocks, row_ref)]
     for elem in range(4):
         values[elem] = packed[elem]
-    send_faces(packed, upper, lower)
-
-
-def apply_kernel(blocks, vector, weights, partial, row_ref):
-    rows = line_apply([vector[elem] for elem in range(4)], blocks, weights, row_ref)
+    send_faces(packed, inner_out, outer_out)
+
+
+def unpack_second_kernel(distance, *refs):
+    *_, first, second, diagonals, wide = refs
+    unpack_diagonal(first, second, diagonals, (lax.axis_index("field") - distance) & 3, wide)
+
+
+def apply_kernel(blocks, diagonals, vector, weights, partial, row_ref):
+    rows = line_apply([vector[elem] for elem in range(4)], blocks, diagonals, weights, row_ref)
     for elem in range(4):
         partial[elem] = rows[elem]
 
 
-def join_solve_kernel(blocks, partial, before, after, weights, image, values, upper, lower, row_ref):
-    rows = add_faces(partial, before, after, weights)
+def join_solve_kernel(blocks, partial, inner, outer, weights, image, values, inner_out, outer_out, row_ref):
+    rows = add_faces(partial, inner, outer, weights)
     packed = [to_packed(v) for v in line_solve(rows, blocks, row_ref)]
     for elem in range(4):
         image[elem] = rows[elem]
         values[elem] = packed[elem]
-    send_faces(packed, upper, lower)
-
-
-def last_solve_kernel(blocks, partial, before, after, weights, r, z, w, s, back0, back1, back2, back3, row_ref, t, u):
-    rows = add_faces(partial, before, after, weights)
+    send_faces(packed, inner_out, outer_out)
+
+
+def last_solve_kernel(blocks, partial, inner, outer, weights, r, z, w, s, back0, back1, back2, back3, row_ref, t, u):
+    rows = add_faces(partial, inner, outer, weights)
     packed = [to_packed(v) for v in line_solve(rows, blocks, row_ref)]
     for elem in range(4):
         t[elem] = rows[elem]
@@ -358,6 +427,7 @@
 VECTOR = jax.ShapeDtypeStruct((4, 16, 128), f32)
 BACK = jax.ShapeDtypeStruct((88, 128), f32)
 BLOCKS = jax.ShapeDtypeStruct((4, ELEMENT_ROWS, 128), bf16)
+DIAGONALS = jax.ShapeDtypeStruct((4, BLOCK_ROWS, 128), bf16)
 
 
 def kernel(body, arrays, outs, name, spec=VMEM, scratch=(), aliases=None):
@@ -378,67 +448,89 @@
     return lax.ppermute(value, "field", [(i, (i + distance) % count) for i in range(count)])
 
 
-def column_pairs(step):
+def column_swaps(first):
     field, cross = lax.axis_size("field"), lax.axis_size("cross")
     device = {}
     for c in range(cross):
         for f in range(field):
             device[field * c + (f if c % 2 == 0 else field - 1 - f)] = f * cross + c
-    count = field * cross
-    return [(device[g], device[g + step]) for g in range(count) if 0 <= g + step < count]
-
-
-def exchange(upper, lower):
-    before = lax.ppermute(upper, ("field", "cross"), column_pairs(1))
-    after = lax.ppermute(lower, ("field", "cross"), column_pairs(-1))
-    return before, after
+    pairs = [(device[g], device[g + 1]) for g in range(first, field * cross - 1, 2)]
+    return pairs + [(b, a) for a, b in pairs]
+
+
+def exchange(inner, outer):
+    return [lax.ppermute(faces, ("field", "cross"), column_swaps(first)) for first, faces in enumerate((inner, outer))]
 
 
 def local(rhs, pivot_inverse, line_coupling, element_block, neighbours, face_type):
     matrix, small = pltpu.VMEM((64, 64, 128), bf16), pltpu.VMEM((4, 128), jnp.int32)
     spread, wide = pltpu.VMEM((64, 128), f32), pltpu.VMEM((BLOCK_ROWS, 128), f32)
+    fetches = 9
     *chunks, weights, order = kernel(
-        pack_kernel,
+        pack_first_kernel,
         in_hbm(neighbours.T, face_type.T, rhs[0], line_coupling[0], pivot_inverse[0], element_block[0]),
-        [jax.ShapeDtypeStruct((CHUNK_ROWS, 128), bf16)] * 4
+        [jax.ShapeDtypeStruct((FIRST_ROWS, 128), bf16)] * 4
         + [jax.ShapeDtypeStruct((5, 16, 128), f32), jax.ShapeDtypeStruct((512, 512), bf16)],
-        "pack",
+        "pack_first",
         HBM,
-        [small, small, pltpu.VMEM((64, 128), f32), matrix, matrix, matrix, pltpu.SemaphoreType.DMA((6,))],
+        [small, small, pltpu.VMEM((64, 128), f32), matrix, matrix, pltpu.VMEM((4, 16, 16, 128), bf16)]
+        + [pltpu.SemaphoreType.DMA((fetches,))],
     )
     held = []
-    arrived = {d: around(chunks[d], d) if d else chunks[0] for d in (0, 1, 3, 2)}
+    first = {d: around(chunks[d], d) if d else chunks[0] for d in (0, 1, 3, 2)}
     for d in (0, 1, 3):
         held = kernel(
             functools.partial(unpack_kernel, d),
-            [*held, arrived[d]],
+            [*held, *(diagonals if d == 3 else []), first[d]],
             [BLOCKS, VECTOR],
             f"unpack_{d}",
             scratch=[wide],
             aliases={0: 0, 1: 1} if held else None,
         )
-    blocks, r, z, upper, lower = kernel(
+        if d == 1:
+            chunks = kernel(
+                pack_second_kernel,
+                in_hbm(element_block[0]) + [order, held[1]],
+                [jax.ShapeDtypeStruct((SECOND_ROWS, 128), bf16)] * 4,
+                "pack_second",
+                [HBM, VMEM, VMEM],
+                [matrix, pltpu.SemaphoreType.DMA((1,))],
+            )
+            second = {d: around(chunks[d], d) if d else chunks[0] for d in (0, 1, 3, 2)}
+            diagonals = kernel(
+                functools.partial(unpack_second_kernel, 0), [first[0], second[0]], [DIAGONALS], "unpack_second_0", scratch=[wide]
+            )
+    blocks, r, z, inner, outer = kernel(
         solve_kernel,
-        [*held, arrived[2]],
+        [*held, first[2]],
         [BLOCKS, VECTOR, VECTOR, FACE, FACE],
         "solve_first",
         scratch=[spread, wide],
         aliases={0: 0, 1: 1},
     )
-    before, after = exchange(upper, lower)
-    (partial,) = kernel(apply_kernel, [blocks, z, weights], [VECTOR], "apply_first", scratch=[spread])
-    w, s, upper, lower = kernel(
+    inner, outer = exchange(inner, outer)
+    for d in (1, 3, 2):
+        diagonals = kernel(
+            functools.partial(unpack_second_kernel, d),
+            [*diagonals, first[d], second[d]],
+            [DIAGONALS],
+            f"unpack_second_{d}",
+            scratch=[wide],
+            aliases={0: 0},
+        )
+    (partial,) = kernel(apply_kernel, [blocks, *diagonals, z, weights], [VECTOR], "apply_first", scratch=[spread])
+    w, s, inner, outer = kernel(
         join_solve_kernel,
-        [blocks, partial, before, after, weights],
+        [blocks, partial, inner, outer, weights],
         [VECTOR, VECTOR, FACE, FACE],
         "solve_second",
         scratch=[spread],
     )
-    before, after = exchange(upper, lower)
-    (partial,) = kernel(apply_kernel, [blocks, s, weights], [VECTOR], "apply_second", scratch=[spread])
+    inner, outer = exchange(inner, outer)
+    (partial,) = kernel(apply_kernel, [blocks, *diagonals, s, weights], [VECTOR], "apply_second", scratch=[spread])
     backs = kernel(
         last_solve_kernel,
-        [blocks, partial, before, after, weights, r, z, w, s],
+        [blocks, partial, inner, outer, weights, r, z, w, s],
         [BACK] * 4,
         "solve_last",
         scratch=[spread, pltpu.VMEM((4, 16, 128), f32), pltpu.VMEM((4, 16, 128), f32)],

time: 85 us -> 78.1 us (0.919)
  waiting for transfers between devices: 28.7 us -> 11.8 us
  starting transfers between devices: 20.3 us -> 25.6 us
  Pallas kernels: 12.8 us -> 16.5 us
  blocking collectives: 22.2 us -> 23.1 us
    ppermute x6 -> x9, waiting for transfers between devices: 24.2 us -> 11.4 us  [around(): lax.ppermute(value, 'field', [(i, (i + distance) % count) for i in range(...]
    ppermute x6 -> x9, starting transfers between devices: 7.86 us -> 13.9 us  [around(): lax.ppermute(value, 'field', [(i, (i + distance) % count) for i in range(...]
    ppermute x4, waiting for transfers between devices: 4.52 us -> 0.45 us  [exchange(): lax.ppermute(faces, ('field', 'cross'), column_swaps(first))]
    pallas_call x10 -> x15, Pallas kernels: 12.8 us -> 16.5 us  [kernel(): pl.pallas_call(body, out_shape=outs, in_specs=spec if isinstance(spec, li...]
    all_to_all x1, blocking collectives: 22.2 us -> 23.1 us  [local(): sums = lax.all_to_all(rows, 'cross', 0, 0)]
  transfers between devices with their start and end apart: 10 -> 13, of which waited for: 7 -> 6; matrix products, arithmetic and copies ran while one was open for 0% -> 0% of each run, Pallas kernels for 4% -> 12%
where the time goes in v4:
time: 78.1 us; the launch traced here: 77.9 us
  starting transfers between devices  25.6 us (33%)
  blocking collectives  23.1 us (30%)
  Pallas kernels  16.5 us (21%)
  waiting for transfers between devices  11.8 us (15%)
  between operations  0.8 us (1%)
    all_to_all x1, blocking collectives, local(): sums = lax.all_to_all(rows, 'cross', 0, 0)  23.1 us
    pallas_call x15, Pallas kernels, kernel(): pl.pallas_call(body, out_shape=outs, in_specs=spec if isinstance(spec, li...  16.5 us
    ppermute x9, starting transfers between devices, around(): lax.ppermute(value, 'field', [(i, (i + distance) % count) for i in range(...  13.9 us
    ppermute x4, starting transfers between devices, exchange(): lax.ppermute(faces, ('field', 'cross'), column_swaps(first))  11.8 us
    ppermute x9, waiting for transfers between devices, around(): lax.ppermute(value, 'field', [(i, (i + distance) % count) for i in range(...  11.4 us
  transfers between devices with their start and end apart: 13, of which 6 were waited for; matrix products, arithmetic and copies ran while one was open for 0% of the time, Pallas kernels for 12%

profile of v4, /device:TPU:1, one launch (start us, length us, event | category | flops | bytes accessed | tf_op | source)
XLA Modules:
  0.0 77.9 jit_solution(8461850047304583889)
XLA Ops:
  0.6 3.2 %pack_first.1 = (bf16[1712,128]{1,0:T(8,128)(2,1)S(1)}, bf16[1712,128]{1,0:T(8,128)(2,1)S(1)}, bf16[1712,128]{1,0:T(8,128)(2,1)S(1)}, bf16[1712,128]{1,0:T(8,128...) custom-call(s32[4,128]{1,0:T(4,128)} %bitcast.17, s32[4,128]{1,0:T(4,128)} %bitcast.18, ...), custom_call_target="tpu_custom_call" | custom-call | tf_op jit(solution)/shard_map/pack_first/pallas_call | solution.py:434
  3.8 2.1 %collective-permute-start = (bf16[1712,128]{1,0:T(8,128)(2,1)S(1)}, bf16[1712,128]{1,0:T(8,128)(2,1)S(1)}, u32[]{:S(2)}, u32[]{:S(2)}) collective-permute-start(bf16[1712,128]{1,0:T(8,128)(2,1)S(1)} %get-tuple-element.38), channel_id=1, source_target_pairs={{0,64},{64,128},{128,192},{192,0},{1,65},{65,129},{129,193},{193,1... | collective-permute-start | bytes 1314824 | tf_op jit(solution)/shard_map/ppermute | solution.py:448
  6.0 1.4 %collective-permute-start.1 = (bf16[1712,128]{1,0:T(8,128)(2,1)S(1)}, bf16[1712,128]{1,0:T(8,128)(2,1)S(1)}, u32[]{:S(2)}, u32[]{:S(2)}) collective-permute-start(bf16[1712,128]{1,0:T(8,128)(2,1)S(1)} %get-tuple-element.43), channel_id=1, source_target_pairs={{0,192},{64,0},{128,64},{192,128},{1,193},{65,1},{129,65},{193,129... | collective-permute-start | bytes 1314824 | tf_op jit(solution)/shard_map/ppermute | solution.py:448
  7.3 1.6 %collective-permute-start.2 = (bf16[1712,128]{1,0:T(8,128)(2,1)S(1)}, bf16[1712,128]{1,0:T(8,128)(2,1)S(1)}, u32[]{:S(2)}, u32[]{:S(2)}) collective-permute-start(bf16[1712,128]{1,0:T(8,128)(2,1)S(1)} %get-tuple-element.46), channel_id=1, source_target_pairs={{0,128},{64,192},{128,0},{192,64},{1,129},{65,193},{129,1},{193,65... | collective-permute-start | bytes 1314824 | tf_op jit(solution)/shard_map/ppermute | solution.py:448
  9.5 5.2 %collective-permute-done.refs_2_.refs_1_ = bf16[1712,128]{1,0:T(8,128)(2,1)S(1)} collective-permute-done((bf16[1712,128]{1,0:T(8,128)(2,1)S(1)}, bf16[1712,128]{1,0:T(8,128)(2,1)S(1)}, u32[]{:S(2)}, u32[]{:S(2)}) %collective-permute-start) | collective-permute-done | bytes 438304 | tf_op jit(solution)/shard_map/ppermute | solution.py:448
  15.3 1.6 %pack_second.1 = (bf16[400,128]{1,0:T(8,128)(2,1)S(1)}, bf16[400,128]{1,0:T(8,128)(2,1)S(1)}, bf16[400,128]{1,0:T(8,128)(2,1)S(1)}, bf16[400,128]{1,0:T(8,128)(2,1)S(1)}) custom-call(bf16[64,64,128]{2,1,0:T(8,128)(2,1)} %bitcast.14, bf16[512,512]{1,0:T(8,128)(2,1)S(1)} %get-tuple-element.41.order, f32[4,16,128]{2,1,0:T(8,128)S(1)} %get-tuple-element.40.after.refs_1_), custom_call_target="tpu_custom_call" | custom-call | tf_op jit(solution)/shard_map/pack_second/pallas_call | solution.py:434
  17.0 2.0 %collective-permute-start.3 = (bf16[400,128]{1,0:T(8,128)(2,1)S(1)}, bf16[400,128]{1,0:T(8,128)(2,1)S(1)}, u32[]{:S(2)}, u32[]{:S(2)}) collective-permute-start(bf16[400,128]{1,0:T(8,128)(2,1)S(1)} %get-tuple-element.48), channel_id=1, source_target_pairs={{0,64},{64,128},{128,192},{192,0},{1,65},{65,129},{129,193},{193,1... | collective-permute-start | bytes 307208 | tf_op jit(solution)/shard_map/ppermute | solution.py:448
  18.9 1.6 %collective-permute-start.4 = (bf16[400,128]{1,0:T(8,128)(2,1)S(1)}, bf16[400,128]{1,0:T(8,128)(2,1)S(1)}, u32[]{:S(2)}, u32[]{:S(2)}) collective-permute-start(bf16[400,128]{1,0:T(8,128)(2,1)S(1)} %get-tuple-element.49), channel_id=1, source_target_pairs={{0,192},{64,0},{128,64},{192,128},{1,193},{65,1},{129,65},{193,129... | collective-permute-start | bytes 307208 | tf_op jit(solution)/shard_map/ppermute | solution.py:448
  20.6 1.9 %collective-permute-start.5 = (bf16[400,128]{1,0:T(8,128)(2,1)S(1)}, bf16[400,128]{1,0:T(8,128)(2,1)S(1)}, u32[]{:S(2)}, u32[]{:S(2)}) collective-permute-start(bf16[400,128]{1,0:T(8,128)(2,1)S(1)} %get-tuple-element.50), channel_id=1, source_target_pairs={{0,128},{64,192},{128,0},{192,64},{1,129},{65,193},{129,1},{193,65... | collective-permute-start | bytes 307208 | tf_op jit(solution)/shard_map/ppermute | solution.py:448
  23.6 3.7 %collective-permute-done.2.chunk.refs_1_ = bf16[1712,128]{1,0:T(8,128)(2,1)S(1)} collective-permute-done((bf16[1712,128]{1,0:T(8,128)(2,1)S(1)}, bf16[1712,128]{1,0:T(8,128)(2,1)S(1)}, u32[]{:S(2)}, u32[]{:S(2)}) %collective-permute-start.2) | collective-permute-done | bytes 438304 | tf_op jit(solution)/shard_map/ppermute | solution.py:448
  27.3 1.8 %solve_first.1 = (bf16[4,2048,128]{2,1,0:T(8,128)(2,1)S(1)}, f32[4,16,128]{2,1,0:T(8,128)S(1)}, f32[4,16,128]{2,1,0:T(8,128)S(1)}, f32[16,128]{1,0:T(8,128)S(1)}, f32[16,128]{1,0:T(8,128)S(1)}) custom-call(bf16[4,2048,128]{2,1,0:T(8,128)(2,1)S(1)} %get-tuple-element.44.blocks_before, ...), custom_call_target="tpu_custom_call", output_to_operand_aliasing={{0}: (0, {}), {1}: (1, {})} | custom-call | tf_op jit(solution)/shard_map/solve_first/pallas_call | solution.py:434
  29.5 7.5 %collective-permute-start.7 = (f32[16,128]{1,0:T(8,128)S(1)}, f32[16,128]{1,0:T(8,128)S(1)}, u32[]{:S(2)}, u32[]{:S(2)}) collective-permute-start(f32[16,128]{1,0:T(8,128)S(1)} %get-tuple-element.54), channel_id=1, source_target_pairs={{64,128},{192,193},{129,65},{1,2},{66,130},{194,195},{131,67},{3,4... | collective-permute-start | bytes 24584 | tf_op jit(solution)/shard_map/ppermute | solution.py:462
  38.7 0.9 %apply_first.1.partial = f32[4,16,128]{2,1,0:T(8,128)S(1)} custom-call(bf16[4,2048,128]{2,1,0:T(8,128)(2,1)S(1)} %get-tuple-element.47.blocks, bf16[4,1024,128]{2,1,0:T(8,128)(2,1)S(1)} %unpack_second_2.1.diagonals, f32[4,16,128]{2,1,0:T(8,128)S(1)} %get-tuple-element.51.vector.z, f32[5,16,128]{2,1,0:T(8,128)S(1)} %get-tuple-element.52.weights), custom_call_target="tpu_custom_call" | custom-call | tf_op jit(solution)/shard_map/apply_first/pallas_call | solution.py:434
  39.6 1.6 %solve_second.1 = (f32[4,16,128]{2,1,0:T(8,128)S(1)}, f32[4,16,128]{2,1,0:T(8,128)S(1)}, f32[16,128]{1,0:T(8,128)S(1)}, f32[16,128]{1,0:T(8,128)S(1)}) custom-call(bf16[4,2048,128]{2,1,0:T(8,128)(2,1)S(1)} %get-tuple-element.47.blocks, f32[4,16,128]{2,1,0:T(8,128)S(1)} %apply_first.1.partial, f32[16,128]{1,0:T(8,128)S(1)} %collective-permute-done.6.inner, ...), custom_call_target="tpu_custom_call" | custom-call | tf_op jit(solution)/shard_map/solve_second/pallas_call | solution.py:434
  41.3 3.9 %collective-permute-start.9 = (f32[16,128]{1,0:T(8,128)S(1)}, f32[16,128]{1,0:T(8,128)S(1)}, u32[]{:S(2)}, u32[]{:S(2)}) collective-permute-start(f32[16,128]{1,0:T(8,128)S(1)} %get-tuple-element.57), channel_id=1, source_target_pairs={{64,128},{192,193},{129,65},{1,2},{66,130},{194,195},{131,67},{3,4... | collective-permute-start | bytes 24584 | tf_op jit(solution)/shard_map/ppermute | solution.py:462
  45.1 0.9 %apply_second.1.partial = f32[4,16,128]{2,1,0:T(8,128)S(1)} custom-call(bf16[4,2048,128]{2,1,0:T(8,128)(2,1)S(1)} %get-tuple-element.47.blocks, bf16[4,1024,128]{2,1,0:T(8,128)(2,1)S(1)} %unpack_second_2.1.diagonals, f32[4,16,128]{2,1,0:T(8,128)S(1)} %get-tuple-element.55.vector.s, f32[5,16,128]{2,1,0:T(8,128)S(1)} %get-tuple-element.52.weights), custom_call_target="tpu_custom_call" | custom-call | tf_op jit(solution)/shard_map/apply_second/pallas_call | solution.py:434
  46.4 1.5 %solve_last.1 = (f32[88,128]{1,0:T(8,128)S(1)}, f32[88,128]{1,0:T(8,128)S(1)}, f32[88,128]{1,0:T(8,128)S(1)}, f32[88,128]{1,0:T(8,128)S(1)}) custom-call(bf16[4,2048,128]{2,1,0:T(8,128)(2,1)S(1)} %get-tuple-element.47.blocks, f32[4,16,128]{2,1,0:T(8,128)S(1)} %apply_second.1.partial, f32[16,128]{1,0:T(8,128)S(1)} %collective-permute-done.8.inner, ...), custom_call_target="tpu_custom_call" | custom-call | tf_op jit(solution)/shard_map/solve_last/pallas_call | solution.py:434
  48.0 0.7 collective-permute-start.10
  49.1 2.1 %collective-permute-start.12 = (f32[88,128]{1,0:T(8,128)S(1)}, f32[88,128]{1,0:T(8,128)S(1)}, u32[]{:S(2)}, u32[]{:S(2)}) collective-permute-start(f32[88,128]{1,0:T(8,128)S(1)} %get-tuple-element.63), channel_id=1, source_target_pairs={{0,192},{64,0},{128,64},{192,128},{1,193},{65,1},{129,65},{193,129... | collective-permute-start | bytes 135176 | tf_op jit(solution)/shard_map/ppermute | solution.py:448
  51.2 1.0 %collective-permute-done.10.b1 = f32[88,128]{1,0:T(8,128)S(1)} collective-permute-done((f32[88,128]{1,0:T(8,128)S(1)}, f32[88,128]{1,0:T(8,128)S(1)}, u32[]{:S(2)}, u32[]{:S(2)}) %collective-permute-start.10) | collective-permute-done | bytes 45088 | tf_op jit(solution)/shard_map/ppermute | solution.py:448
  52.1 0.9 %collective-permute-done.11.b2 = f32[88,128]{1,0:T(8,128)S(1)} collective-permute-done((f32[88,128]{1,0:T(8,128)S(1)}, f32[88,128]{1,0:T(8,128)S(1)}, u32[]{:S(2)}, u32[]{:S(2)}) %collective-permute-start.11) | collective-permute-done | bytes 45088 | tf_op jit(solution)/shard_map/ppermute | solution.py:448
  53.1 0.6 collective-permute-done.12.b3
  53.7 23.1 %all_to_all.5.sums = f32[64,1,128]{2,1,0:T(1,128)S(1)} all-to-all(f32[64,1,128]{2,1,0:T(1,128)S(1)} %broadcast_in_dim.18), channel_id=1, replica_groups=mesh['field'=4,'cross'=64] {'cross'}, dimensions={0} | all-to-all | bytes 65536 | tf_op jit(solution)/shard_map/all_to_all | solution.py:541
  76.8 1.1 %final.1 = (f32[64,128]{1,0:T(8,128)}, f32[64,128]{1,0:T(8,128)}, f32[64,128]{1,0:T(8,128)}) custom-call(f32[64,1,128]{2,1,0:T(1,128)S(1)} %all_to_all.5.sums, f32[64,128]{1,0:T(8,128)S(1)} %bitcast.12, f32[88,128]{1,0:T(8,128)S(1)} %get-tuple-element.60.b0, f32[88,128]{1,0:T(8,128)S(1)} %collective-permute-done.10.b1, ...), custom_call_target="tpu_custom_call" | custom-call | tf_op jit(solution)/shard_map/final/pallas_call | solution.py:434
  (22 shorter events, 5.3 us)
Async XLA Ops:
  3.8 10.9 %collective-permute-start = (bf16[1712,128]{1,0:T(8,128)(2,1)S(1)}, bf16[1712,128]{1,0:T(8,128)(2,1)S(1)}, u32[]{:S(2)}, u32[]{:S(2)}) collective-permute-start(bf16[1712,128]{1,0:T(8,128)(2,1)S(1)} %get-tuple-element.38), channel_id=1, source_target_pairs={{0,64},{64,128},{128,192},{192,0},{1,65},{65,129},{129,193},{193,1... | collective-permute-start | bytes 1314824 | tf_op jit(solution)/shard_map/ppermute | solution.py:448
  6.0 17.1 %collective-permute-start.1 = (bf16[1712,128]{1,0:T(8,128)(2,1)S(1)}, bf16[1712,128]{1,0:T(8,128)(2,1)S(1)}, u32[]{:S(2)}, u32[]{:S(2)}) collective-permute-start(bf16[1712,128]{1,0:T(8,128)(2,1)S(1)} %get-tuple-element.43), channel_id=1, source_target_pairs={{0,192},{64,0},{128,64},{192,128},{1,193},{65,1},{129,65},{193,129... | collective-permute-start | bytes 1314824 | tf_op jit(solution)/shard_map/ppermute | solution.py:448
  7.3 20.0 %collective-permute-start.2 = (bf16[1712,128]{1,0:T(8,128)(2,1)S(1)}, bf16[1712,128]{1,0:T(8,128)(2,1)S(1)}, u32[]{:S(2)}, u32[]{:S(2)}) collective-permute-start(bf16[1712,128]{1,0:T(8,128)(2,1)S(1)} %get-tuple-element.46), channel_id=1, source_target_pairs={{0,128},{64,192},{128,0},{192,64},{1,129},{65,193},{129,1},{193,65... | collective-permute-start | bytes 1314824 | tf_op jit(solution)/shard_map/ppermute | solution.py:448
  17.0 20.0 %collective-permute-start.3 = (bf16[400,128]{1,0:T(8,128)(2,1)S(1)}, bf16[400,128]{1,0:T(8,128)(2,1)S(1)}, u32[]{:S(2)}, u32[]{:S(2)}) collective-permute-start(bf16[400,128]{1,0:T(8,128)(2,1)S(1)} %get-tuple-element.48), channel_id=1, source_target_pairs={{0,64},{64,128},{128,192},{192,0},{1,65},{65,129},{129,193},{193,1... | collective-permute-start | bytes 307208 | tf_op jit(solution)/shard_map/ppermute | solution.py:448
  18.9 18.6 %collective-permute-start.4 = (bf16[400,128]{1,0:T(8,128)(2,1)S(1)}, bf16[400,128]{1,0:T(8,128)(2,1)S(1)}, u32[]{:S(2)}, u32[]{:S(2)}) collective-permute-start(bf16[400,128]{1,0:T(8,128)(2,1)S(1)} %get-tuple-element.49), channel_id=1, source_target_pairs={{0,192},{64,0},{128,64},{192,128},{1,193},{65,1},{129,65},{193,129... | collective-permute-start | bytes 307208 | tf_op jit(solution)/shard_map/ppermute | solution.py:448
  20.6 17.6 %collective-permute-start.5 = (bf16[400,128]{1,0:T(8,128)(2,1)S(1)}, bf16[400,128]{1,0:T(8,128)(2,1)S(1)}, u32[]{:S(2)}, u32[]{:S(2)}) collective-permute-start(bf16[400,128]{1,0:T(8,128)(2,1)S(1)} %get-tuple-element.50), channel_id=1, source_target_pairs={{0,128},{64,192},{128,0},{192,64},{1,129},{65,193},{129,1},{193,65... | collective-permute-start | bytes 307208 | tf_op jit(solution)/shard_map/ppermute | solution.py:448
  29.1 10.4 %collective-permute-start.6 = (f32[16,128]{1,0:T(8,128)S(1)}, f32[16,128]{1,0:T(8,128)S(1)}, u32[]{:S(2)}, u32[]{:S(2)}) collective-permute-start(f32[16,128]{1,0:T(8,128)S(1)} %get-tuple-element.53), channel_id=1, source_target_pairs={{0,64},{128,192},{193,129},{65,1},{2,66},{130,194},{195,131},{67,3... | collective-permute-start | bytes 24584 | tf_op jit(solution)/shard_map/ppermute | solution.py:462
  29.5 10.0 %collective-permute-start.7 = (f32[16,128]{1,0:T(8,128)S(1)}, f32[16,128]{1,0:T(8,128)S(1)}, u32[]{:S(2)}, u32[]{:S(2)}) collective-permute-start(f32[16,128]{1,0:T(8,128)S(1)} %get-tuple-element.54), channel_id=1, source_target_pairs={{64,128},{192,193},{129,65},{1,2},{66,130},{194,195},{131,67},{3,4... | collective-permute-start | bytes 24584 | tf_op jit(solution)/shard_map/ppermute | solution.py:462
  41.2 4.8 %collective-permute-start.8 = (f32[16,128]{1,0:T(8,128)S(1)}, f32[16,128]{1,0:T(8,128)S(1)}, u32[]{:S(2)}, u32[]{:S(2)}) collective-permute-start(f32[16,128]{1,0:T(8,128)S(1)} %get-tuple-element.56), channel_id=1, source_target_pairs={{0,64},{128,192},{193,129},{65,1},{2,66},{130,194},{195,131},{67,3... | collective-permute-start | bytes 24584 | tf_op jit(solution)/shard_map/ppermute | solution.py:462
  41.3 5.2 %collective-permute-start.9 = (f32[16,128]{1,0:T(8,128)S(1)}, f32[16,128]{1,0:T(8,128)S(1)}, u32[]{:S(2)}, u32[]{:S(2)}) collective-permute-start(f32[16,128]{1,0:T(8,128)S(1)} %get-tuple-element.57), channel_id=1, source_target_pairs={{64,128},{192,193},{129,65},{1,2},{66,130},{194,195},{131,67},{3,4... | collective-permute-start | bytes 24584 | tf_op jit(solution)/shard_map/ppermute | solution.py:462
  45.1 31.7 %copy-start = (f32[1,64,128]{2,1,0:T(8,128)S(1)}, f32[1,64,128]{2,1,0:T(8,128)}, u32[]{:S(2)}) copy-start(f32[1,64,128]{2,1,0:T(8,128)} %param.6) | copy-start | bytes 98308
  48.0 4.2 %collective-permute-start.10 = (f32[88,128]{1,0:T(8,128)S(1)}, f32[88,128]{1,0:T(8,128)S(1)}, u32[]{:S(2)}, u32[]{:S(2)}) collective-permute-start(f32[88,128]{1,0:T(8,128)S(1)} %get-tuple-element.61), channel_id=1, source_target_pairs={{0,64},{64,128},{128,192},{192,0},{1,65},{65,129},{129,193},{193,1... | collective-permute-start | bytes 135176 | tf_op jit(solution)/shard_map/ppermute | solution.py:448
  48.7 4.4 %collective-permute-start.11 = (f32[88,128]{1,0:T(8,128)S(1)}, f32[88,128]{1,0:T(8,128)S(1)}, u32[]{:S(2)}, u32[]{:S(2)}) collective-permute-start(f32[88,128]{1,0:T(8,128)S(1)} %get-tuple-element.62), channel_id=1, source_target_pairs={{0,128},{64,192},{128,0},{192,64},{1,129},{65,193},{129,1},{193,65... | collective-permute-start | bytes 135176 | tf_op jit(solution)/shard_map/ppermute | solution.py:448
  49.1 4.5 %collective-permute-start.12 = (f32[88,128]{1,0:T(8,128)S(1)}, f32[88,128]{1,0:T(8,128)S(1)}, u32[]{:S(2)}, u32[]{:S(2)}) collective-permute-start(f32[88,128]{1,0:T(8,128)S(1)} %get-tuple-element.63), channel_id=1, source_target_pairs={{0,192},{64,0},{128,64},{192,128},{1,193},{65,1},{129,65},{193,129... | collective-permute-start | bytes 135176 | tf_op jit(solution)/shard_map/ppermute | solution.py:448

commit v5 on v4

--- a/solution.py
+++ b/solution.py
@@ -9,10 +9,9 @@
 
 
 BLOCK_ROWS = 1024
-COUPLING, WIDE, SHORT, CORNER, RESIDUAL = (0, 1024, 1280, 1408, 1664)
-FIRST_ROWS = 1664 + 48
-SECOND_WIDE, SECOND_SHORT, SECOND_DIAGONAL = (0, 256, 384)
-SECOND_ROWS = 384 + 16
+COUPLING, WIDE, SHORT, CORNER, EDGE, RESIDUAL = (0, 1024, 1280, 1408, 1536, 1552)
+FIRST_ROWS = 1552 + 32
+SECOND_ROWS = RESIDUAL - WIDE
 PIVOT = 1024
 ELEMENT_ROWS = 2048
 VMEM_LIMIT = 24 * 1024 * 1024
@@ -44,12 +43,12 @@
     return lax.dot_general(left, right, (((1,), (1,)), ((), ())), preferred_element_type=f32)
 
 
-def three_parts(value):
-    high = value.astype(bf16)
-    rest = value - high.astype(f32)
-    middle = rest.astype(bf16)
-    low = (rest - middle.astype(f32)).astype(bf16)
-    return high, middle, low
+def bf16_parts(value, count):
+    parts = []
+    for _ in range(count):
+        parts.append(value.astype(bf16))
+        value = value - parts[-1].astype(f32)
+    return parts
 
 
 def start_fetch(sources, targets, sems):
@@ -65,33 +64,32 @@
         outs[d][start : start + rows, :] = result[:, d * 128 : (d + 1) * 128]
 
 
-def parts_below(block):
+def parts_of(block):
     def part(rows, column):
         return block[rows, 16 * column : 16 * column + 16, :].reshape(-1, 128)
 
     last, upper, lower = slice(48, 64), slice(32, 40), slice(40, 48)
     wide = [part(last, 0), part(last, 1), part(last, 2), part(slice(16, 32), 0)]
     short = [part(upper, 0), part(upper, 1), part(lower, 0), part(lower, 1)]
-    return [jnp.concatenate(wide, axis=1), jnp.concatenate(short, axis=1)]
-
-
-def corner_orders():
     shape = (16, 16, 128)
-    return lax.broadcasted_iota(jnp.int32, shape, 0), lax.broadcasted_iota(jnp.int32, shape, 1)
+    major, minor = lax.broadcasted_iota(jnp.int32, shape, 0), lax.broadcasted_iota(jnp.int32, shape, 1)
+    corner, edge = [], []
+    for q in (0, 2):
+        one, other = (
+            block[16 * k : 16 * k + 16, 16 * k : 16 * k + 16, :].astype(f32) for k in (q, q + 1)
+        )
+        pair = jnp.where(minor <= major, one, other).astype(bf16)
+        corner += [pair[0:8].reshape(128, 128), pair[8:16].reshape(128, 128)]
+        edge += [jnp.zeros((16, 128), bf16), jnp.sum(jnp.where(minor == major, other, 0.0), axis=0).astype(bf16)]
+    return [jnp.concatenate(parts, axis=1) for parts in (wide, short, corner, edge)]
 
 
 def pack_first_kernel(
-    neighbours, face_type, rhs, coupling, pivot, diagonal, out0, out1, out2, out3, weights, order, *scratch
+    neighbours, face_type, rhs, coupling, pivot, out0, out1, out2, out3, weights, order, *scratch
 ):
     *held, sems = scratch
-    sources = [neighbours, face_type, rhs, coupling, pivot]
-    targets = list(held[:5])
-    for q in range(4):
-        here = slice(16 * q, 16 * q + 16)
-        sources.append(diagonal.at[here, here, :])
-        targets.append(held[5].at[q])
-    copies = start_fetch(sources, targets, sems)
-    neighbours, face_type, rhs, coupling, pivot, corners = held
+    copies = start_fetch((neighbours, face_type, rhs, coupling, pivot), held, sems)
+    neighbours, face_type, rhs, coupling, pivot = held
     me, cross = lax.axis_index("field"), lax.axis_index("cross")
     square = (128, 128)
     lane = lax.broadcasted_iota(jnp.int32, square, 1)
@@ -129,16 +127,10 @@
     left = [coupling[:, 16 * q : 16 * q + 16, :].reshape(BLOCK_ROWS, 128) for q in range(4)]
     send(jnp.concatenate(left, axis=1), sorting, outs, COUPLING, BLOCK_ROWS)
 
-    for copy in (copies[2], *copies[4:]):
-        copy.wait()
-    major, minor = corner_orders()
-    shared = []
-    for q in range(4):
-        here = slice(16 * q, 16 * q + 16)
-        own, other = pivot[here, here, :].astype(f32), corners[q].astype(f32)
-        shared.append(jnp.where(minor <= major, own, other).astype(bf16).reshape(256, 128))
-    rows = parts_below(pivot) + [jnp.concatenate(shared, axis=1)]
-    for part in three_parts(rhs[...]):
+    copies[2].wait()
+    copies[4].wait()
+    rows = parts_of(pivot)
+    for part in bf16_parts(rhs[...], 2):
         rows.append(jnp.concatenate([part[16 * q : 16 * q + 16] for q in range(4)], axis=1))
     send(jnp.concatenate(rows, axis=0), sorting, outs, WIDE, FIRST_ROWS - WIDE)
 
@@ -160,13 +152,7 @@
 def pack_second_kernel(diagonal, order, after, out0, out1, out2, out3, held, sems):
     (copy,) = start_fetch([diagonal], [held], sems)
     copy.wait()
-    major, minor = corner_orders()
-    trail = []
-    for q in range(4):
-        here = slice(16 * q, 16 * q + 16)
-        trail.append(jnp.sum(jnp.where(minor == major, held[here, here, :].astype(f32), 0.0), axis=0).astype(bf16))
-    rows = parts_below(held) + [jnp.concatenate(trail, axis=1)]
-    send(jnp.concatenate(rows, axis=0), order[...], (out0, out1, out2, out3), 0, SECOND_ROWS)
+    send(jnp.concatenate(parts_of(held), axis=0), order[...], (out0, out1, out2, out3), 0, SECOND_ROWS)
 
 
 def in_hbm(*arrays):
@@ -222,49 +208,75 @@
     return rows
 
 
-def spread_parts(wide, parts, corner):
-    seg = segment_of((16, 128))
+def corner_row(parts, k):
+    odd = segment_of((16, 128)) % 2 == 1
+    start = CORNER - WIDE + 16 * (k % 8)
+    row = parts[start : start + 16, :].astype(f32)
+    if k < 8:
+        return jnp.where(odd, pltpu.roll(row, 32, 1), row)
+    return jnp.where(odd, row, pltpu.roll(row, 96, 1))
+
+
+def unpack(chunk, blocks, residual, elem, wide):
+    shape = (16, 128)
+    seg, m = segment_of(shape), row_of(shape)
+    blocks[elem, 0:BLOCK_ROWS, :] = chunk[COUPLING : COUPLING + BLOCK_ROWS, :]
+    residual[elem] = chunk[RESIDUAL : RESIDUAL + 16, :].astype(f32) + chunk[RESIDUAL + 16 : RESIDUAL + 32, :].astype(f32)
+    parts = chunk.at[WIDE:RESIDUAL, :]
     for k in range(16):
-        diagonal = corner[16 * k : 16 * k + 16, :].astype(f32)
+        corner = corner_row(parts, k)
         last = parts[16 * k : 16 * k + 16, :].astype(f32)
         third = parts[256 + 16 * (k % 8) : 272 + 16 * (k % 8), :].astype(f32)
         if k >= 8:
             third = pltpu.roll(third, 64, 1)
-        wide[16 * k : 16 * k + 16, :] = diagonal
-        wide[256 + 16 * k : 272 + 16 * k, :] = jnp.where(seg == 0, pltpu.roll(last, 32, 1), diagonal)
-        wide[512 + 16 * k : 528 + 16 * k, :] = jnp.where(seg == 2, diagonal, third)
-        wide[768 + 16 * k : 784 + 16 * k, :] = jnp.where(seg == 3, diagonal, last)
-
-
-def unpack_pivot(chunk, blocks, residual, elem, wide):
+        wide[16 * k : 16 * k + 16, :] = corner
+        wide[256 + 16 * k : 272 + 16 * k, :] = jnp.where(seg == 0, pltpu.roll(last, 32, 1), corner)
+        wide[512 + 16 * k : 528 + 16 * k, :] = jnp.where(seg == 2, corner, third)
+        wide[768 + 16 * k : 784 + 16 * k, :] = jnp.where(seg == 3, corner, last)
+    edge = chunk[EDGE : EDGE + 16, :].astype(f32)
+    for k in range(16):
+        turned = turn_segments([wide[pl.ds(256 * q + k, 16, stride=16), :] for q in range(4)])
+        for q in range(4):
+            a = 16 * q + k
+            here = (seg < q) | ((seg == q) & ((m <= k) if q % 2 == 0 else (m > k)))
+            value = jnp.where(here, wide[16 * a : 16 * a + 16, :], turned[q])
+            if q % 2 == 1:
+                value = jnp.where((seg == q) & (m == k), edge, value)
+            blocks[elem, PIVOT + 16 * a : PIVOT + 16 * a + 16, :] = value.astype(bf16)
+
+
+def diagonal_times(parts, packed):
     shape = (16, 128)
     seg, m = segment_of(shape), row_of(shape)
-    blocks[elem, 0:BLOCK_ROWS, :] = chunk[COUPLING : COUPLING + BLOCK_ROWS, :]
-    part = chunk[RESIDUAL : RESIDUAL + 48, :].astype(f32)
-    residual[elem] = (part[0:16] + part[16:32]) + part[32:48]
-    spread_parts(wide, chunk.at[WIDE:CORNER, :], chunk.at[CORNER:RESIDUAL, :])
+    spread = to_spread(packed)
+    v0, v1, v2, v3 = (spread[16 * q : 16 * q + 16] for q in range(4))
+
+    def both_ways(block, count, across, along):
+        down = [block[k] * across[k : k + 1] for k in range(count)]
+        while len(down) > 1:
+            down = [x + y for x, y in zip(down[::2], down[1::2], strict=True)]
+        return down[0], jnp.sum(block * along[None], axis=1)
+
+    odd = seg % 2 == 1
+    diagonal = parts[EDGE - WIDE : EDGE - WIDE + 16, :].astype(f32)
+    corner = []
     for k in range(16):
-        across = turn_segments([wide[pl.ds(256 * q + k, 16, stride=16), :] for q in range(4)])
-        for q in range(4):
-            a = 16 * q + k
-            below = (seg < q) | ((seg == q) & (m <= k))
-            value = jnp.where(below, wide[16 * a : 16 * a + 16, :], across[q])
-            blocks[elem, PIVOT + 16 * a : PIVOT + 16 * a + 16, :] = value.astype(bf16)
-
-
-def unpack_diagonal(first, second, diagonals, elem, wide):
-    shape = (16, 128)
-    seg, m = segment_of(shape), row_of(shape)
-    trail = second[SECOND_DIAGONAL:SECOND_ROWS, :].astype(f32)
-    spread_parts(wide, second.at[0:SECOND_DIAGONAL, :], first.at[CORNER:RESIDUAL, :])
-    for k in range(16):
-        across = turn_segments([wide[pl.ds(256 * q + k, 16, stride=16), :] for q in range(4)])
-        for q in range(4):
-            a = 16 * q + k
-            here = (seg < q) | ((seg == q) & (m > k))
-            value = jnp.where(here, wide[16 * a : 16 * a + 16, :], across[q])
-            value = jnp.where((seg == q) & (m == k), trail, value)
-            diagonals[elem, 16 * a : 16 * a + 16, :] = value.astype(bf16)
+        row = corner_row(parts, k)
+        diagonal = jnp.where((m == k) & ~odd, row, diagonal)
+        corner.append(jnp.where(jnp.where(odd, m - k, k - m) > 0, row, 0.0))
+    down, right = both_ways(jnp.concatenate(corner, axis=0).reshape(16, 16, 128), 16, packed, packed)
+    total = down + right + diagonal * packed
+    wide = parts[0 : SHORT - WIDE, :].astype(f32).reshape(16, 16, 128)
+    down, right = both_ways(wide, 16, jnp.where(seg == 3, v1, v3), jnp.where(seg == 3, v0, packed))
+    total = total + jnp.where(seg < 3, down, 0.0) + jnp.where(seg == 0, pltpu.roll(down, 32, 1), 0.0)
+    turned = [pltpu.roll(right, 32 * k, 1) for k in (1, 2, 3)]
+    total = total + jnp.where(seg == 3, (turned[0] + turned[1]) + turned[2], jnp.where(seg == 1, turned[1], 0.0))
+    short = parts[SHORT - WIDE : CORNER - WIDE, :].astype(f32).reshape(8, 16, 128)
+    down, right = both_ways(short, 8, jnp.where(seg[0:8] < 2, v2[0:8], v2[8:16]), jnp.where(odd, v1, v0))
+    total = total + jnp.where(seg < 2, down + pltpu.roll(down, 64, 1), 0.0)
+    upper = pltpu.roll(right, 64, 1) + pltpu.roll(right, 32, 1)
+    lower = right + pltpu.roll(right, 96, 1)
+    return total + jnp.where(seg == 2, jnp.concatenate([upper, lower], axis=0), 0.0)
 
 
 def line_solve(residual, blocks, row_ref):
@@ -301,12 +313,12 @@
     outer[...] = jnp.where(even, to_before, to_next)
 
 
-def line_apply(packed, blocks, diagonals, weights, row_ref):
+def line_apply(packed, blocks, products, weights, row_ref):
     spread = [to_spread(v) for v in packed]
     rows = []
     for elem in range(4):
         v = packed[elem]
-        total = transposed_times(diagonals, elem, 0, spread[elem], row_ref)
+        total = products[elem]
         if elem > 0:
             total = total + to_packed(times(blocks, elem, COUPLING, packed[elem - 1]))
         if elem < 3:
@@ -338,24 +350,23 @@
 
 def unpack_kernel(distance, *refs):
     *_, chunk, blocks, residual, wide = refs
-    unpack_pivot(chunk, blocks, residual, (lax.axis_index("field") - distance) & 3, wide)
+    unpack(chunk, blocks, residual, (lax.axis_index("field") - distance) & 3, wide)
 
 
 def solve_kernel(blocks_before, residual_before, chunk, blocks, residual, values, inner_out, outer_out, row_ref, wide):
-    unpack_pivot(chunk, blocks, residual, (lax.axis_index("field") - 2) & 3, wide)
+    unpack(chunk, blocks, residual, (lax.axis_index("field") - 2) & 3, wide)
     packed = [to_packed(v) for v in line_solve([residual[elem] for elem in range(4)], blocks, row_ref)]
     for elem in range(4):
         values[elem] = packed[elem]
     send_faces(packed, inner_out, outer_out)
 
 
-def unpack_second_kernel(distance, *refs):
-    *_, first, second, diagonals, wide = refs
-    unpack_diagonal(first, second, diagonals, (lax.axis_index("field") - distance) & 3, wide)
-
-
-def apply_kernel(blocks, diagonals, vector, weights, partial, row_ref):
-    rows = line_apply([vector[elem] for elem in range(4)], blocks, diagonals, weights, row_ref)
+def apply_kernel(blocks, p0, p1, p2, p3, vector, weights, partial, row_ref, products):
+    me = lax.axis_index("field")
+    for d, parts in enumerate((p0, p1, p2, p3)):
+        elem = (me - d) & 3
+        products[elem] = diagonal_times(parts, vector[elem])
+    rows = line_apply([vector[elem] for elem in range(4)], blocks, products, weights, row_ref)
     for elem in range(4):
         partial[elem] = rows[elem]
 
@@ -411,7 +422,7 @@
     first = alpha + alpha_next * grown
     other = alpha_next * alpha
     combos = [first * z - other * s, other * t - first * w, z - first * s + other * u]
-    parts = [part for combo in combos for part in three_parts(combo)]
+    parts = [part for combo in combos for part in bf16_parts(combo, 3)]
     moved = matmul(jnp.concatenate(parts, axis=0), order[...])
     for index, ref in enumerate((solution, residual, precond)):
         rows = moved[48 * index : 48 * index + 48]
@@ -427,7 +438,6 @@
 VECTOR = jax.ShapeDtypeStruct((4, 16, 128), f32)
 BACK = jax.ShapeDtypeStruct((88, 128), f32)
 BLOCKS = jax.ShapeDtypeStruct((4, ELEMENT_ROWS, 128), bf16)
-DIAGONALS = jax.ShapeDtypeStruct((4, BLOCK_ROWS, 128), bf16)
 
 
 def kernel(body, arrays, outs, name, spec=VMEM, scratch=(), aliases=None):
@@ -465,23 +475,21 @@
 def local(rhs, pivot_inverse, line_coupling, element_block, neighbours, face_type):
     matrix, small = pltpu.VMEM((64, 64, 128), bf16), pltpu.VMEM((4, 128), jnp.int32)
     spread, wide = pltpu.VMEM((64, 128), f32), pltpu.VMEM((BLOCK_ROWS, 128), f32)
-    fetches = 9
     *chunks, weights, order = kernel(
         pack_first_kernel,
-        in_hbm(neighbours.T, face_type.T, rhs[0], line_coupling[0], pivot_inverse[0], element_block[0]),
+        in_hbm(neighbours.T, face_type.T, rhs[0], line_coupling[0], pivot_inverse[0]),
         [jax.ShapeDtypeStruct((FIRST_ROWS, 128), bf16)] * 4
         + [jax.ShapeDtypeStruct((5, 16, 128), f32), jax.ShapeDtypeStruct((512, 512), bf16)],
         "pack_first",
         HBM,
-        [small, small, pltpu.VMEM((64, 128), f32), matrix, matrix, pltpu.VMEM((4, 16, 16, 128), bf16)]
-        + [pltpu.SemaphoreType.DMA((fetches,))],
+        [small, small, pltpu.VMEM((64, 128), f32), matrix, matrix, pltpu.SemaphoreType.DMA((5,))],
     )
     held = []
     first = {d: around(chunks[d], d) if d else chunks[0] for d in (0, 1, 3, 2)}
     for d in (0, 1, 3):
         held = kernel(
             functools.partial(unpack_kernel, d),
-            [*held, *(diagonals if d == 3 else []), first[d]],
+            [*held, first[d]],
             [BLOCKS, VECTOR],
             f"unpack_{d}",
             scratch=[wide],
@@ -497,9 +505,6 @@
                 [matrix, pltpu.SemaphoreType.DMA((1,))],
             )
             second = {d: around(chunks[d], d) if d else chunks[0] for d in (0, 1, 3, 2)}
-            diagonals = kernel(
-                functools.partial(unpack_second_kernel, 0), [first[0], second[0]], [DIAGONALS], "unpack_second_0", scratch=[wide]
-            )
     blocks, r, z, inner, outer = kernel(
         solve_kernel,
         [*held, first[2]],
@@ -509,16 +514,9 @@
         aliases={0: 0, 1: 1},
     )
     inner, outer = exchange(inner, outer)
-    for d in (1, 3, 2):
-        diagonals = kernel(
-            functools.partial(unpack_second_kernel, d),
-            [*diagonals, first[d], second[d]],
-            [DIAGONALS],
-            f"unpack_second_{d}",
-            scratch=[wide],
-            aliases={0: 0},
-        )
-    (partial,) = kernel(apply_kernel, [blocks, *diagonals, z, weights], [VECTOR], "apply_first", scratch=[spread])
+    parts = [second[d] for d in range(4)]
+    products = pltpu.VMEM((4, 16, 128), f32)
+    (partial,) = kernel(apply_kernel, [blocks, *parts, z, weights], [VECTOR], "apply_first", scratch=[spread, products])
     w, s, inner, outer = kernel(
         join_solve_kernel,
         [blocks, partial, inner, outer, weights],
@@ -527,7 +525,7 @@
         scratch=[spread],
     )
     inner, outer = exchange(inner, outer)
-    (partial,) = kernel(apply_kernel, [blocks, *diagonals, s, weights], [VECTOR], "apply_second", scratch=[spread])
+    (partial,) = kernel(apply_kernel, [blocks, *parts, s, weights], [VECTOR], "apply_second", scratch=[spread, products])
     backs = kernel(
         last_solve_kernel,
         [blocks, partial, inner, outer, weights, r, z, w, s],

time: 78.1 us -> 76.9 us (0.985)
  Pallas kernels: 16.5 us -> 14.6 us
  starting transfers between devices: 25.6 us -> 27.2 us
  waiting for transfers between devices: 11.8 us -> 10.9 us
    pallas_call x15 -> x11, Pallas kernels: 16.5 us -> 14.6 us  [kernel(): pl.pallas_call(body, out_shape=outs, in_specs=spec if isinstance(spec, li...]
    ppermute x4, starting transfers between devices: 11.8 us -> 13.2 us  [exchange(): lax.ppermute(faces, ('field', 'cross'), column_swaps(first))]
    ppermute x9, waiting for transfers between devices: 11.4 us -> 10.5 us  [around(): lax.ppermute(value, 'field', [(i, (i + distance) % count) for i in range(...]
  transfers between devices with their start and end apart: 13 -> 13, of which waited for: 6 -> 7; matrix products, arithmetic and copies ran while one was open for 0% -> 0% of each run, Pallas kernels for 12% -> 9%
where the time goes in v5:
time: 76.9 us; the launch traced here: 76.6 us
  starting transfers between devices  27.2 us (35%)
  blocking collectives  23.2 us (30%)
  Pallas kernels  14.6 us (19%)
  waiting for transfers between devices  10.9 us (14%)
  between operations  0.78 us (1%)
    all_to_all x1, blocking collectives, local(): sums = lax.all_to_all(rows, 'cross', 0, 0)  23.2 us
    pallas_call x11, Pallas kernels, kernel(): pl.pallas_call(body, out_shape=outs, in_specs=spec if isinstance(spec, li...  14.6 us
    ppermute x9, starting transfers between devices, around(): lax.ppermute(value, 'field', [(i, (i + distance) % count) for i in range(...  14 us
    ppermute x4, starting transfers between devices, exchange(): lax.ppermute(faces, ('field', 'cross'), column_swaps(first))  13.2 us
    ppermute x9, waiting for transfers between devices, around(): lax.ppermute(value, 'field', [(i, (i + distance) % count) for i in range(...  10.5 us
  transfers between devices with their start and end apart: 13, of which 7 were waited for; matrix products, arithmetic and copies ran while one was open for 0% of the time, Pallas kernels for 9%

profile of v5, /device:TPU:1, one launch (start us, length us, event | category | flops | bytes accessed | tf_op | source)
XLA Modules:
  0.0 76.6 jit_solution(16391865491918433098)
XLA Ops:
  0.6 3.1 %pack_first.1 = (bf16[1584,128]{1,0:T(8,128)(2,1)S(1)}, bf16[1584,128]{1,0:T(8,128)(2,1)S(1)}, bf16[1584,128]{1,0:T(8,128)(2,1)S(1)}, bf16[1584,128]{1,0:T(8,128...) custom-call(s32[4,128]{1,0:T(4,128)} %bitcast.16, s32[4,128]{1,0:T(4,128)} %bitcast.17, ...), custom_call_target="tpu_custom_call" | custom-call | tf_op jit(solution)/shard_map/pack_first/pallas_call | solution.py:444
  3.8 2.1 %collective-permute-start = (bf16[1584,128]{1,0:T(8,128)(2,1)S(1)}, bf16[1584,128]{1,0:T(8,128)(2,1)S(1)}, u32[]{:S(2)}, u32[]{:S(2)}) collective-permute-start(bf16[1584,128]{1,0:T(8,128)(2,1)S(1)} %get-tuple-element.38), channel_id=1, source_target_pairs={{0,64},{64,128},{128,192},{192,0},{1,65},{65,129},{129,193},{193,1... | collective-permute-start | bytes 1216520 | tf_op jit(solution)/shard_map/ppermute | solution.py:458
  5.9 1.4 %collective-permute-start.1 = (bf16[1584,128]{1,0:T(8,128)(2,1)S(1)}, bf16[1584,128]{1,0:T(8,128)(2,1)S(1)}, u32[]{:S(2)}, u32[]{:S(2)}) collective-permute-start(bf16[1584,128]{1,0:T(8,128)(2,1)S(1)} %get-tuple-element.41), channel_id=1, source_target_pairs={{0,192},{64,0},{128,64},{192,128},{1,193},{65,1},{129,65},{193,129... | collective-permute-start | bytes 1216520 | tf_op jit(solution)/shard_map/ppermute | solution.py:458
  7.2 1.6 %collective-permute-start.2 = (bf16[1584,128]{1,0:T(8,128)(2,1)S(1)}, bf16[1584,128]{1,0:T(8,128)(2,1)S(1)}, u32[]{:S(2)}, u32[]{:S(2)}) collective-permute-start(bf16[1584,128]{1,0:T(8,128)(2,1)S(1)} %get-tuple-element.44), channel_id=1, source_target_pairs={{0,128},{64,192},{128,0},{192,64},{1,129},{65,193},{129,1},{193,65... | collective-permute-start | bytes 1216520 | tf_op jit(solution)/shard_map/ppermute | solution.py:458
  9.4 4.6 %collective-permute-done.refs_2_ = bf16[1584,128]{1,0:T(8,128)(2,1)S(1)} collective-permute-done((bf16[1584,128]{1,0:T(8,128)(2,1)S(1)}, bf16[1584,128]{1,0:T(8,128)(2,1)S(1)}, u32[]{:S(2)}, u32[]{:S(2)}) %collective-permute-start) | collective-permute-done | bytes 405536 | tf_op jit(solution)/shard_map/ppermute | solution.py:458
  13.9 0.5 unpack_1.1
  14.4 1.7 %pack_second.1 = (bf16[528,128]{1,0:T(8,128)(2,1)S(1)}, bf16[528,128]{1,0:T(8,128)(2,1)S(1)}, bf16[528,128]{1,0:T(8,128)(2,1)S(1)}, bf16[528,128]{1,0:T(8,128)(2,1)S(1)}) custom-call(bf16[64,64,128]{2,1,0:T(8,128)(2,1)} %bitcast.15, bf16[512,512]{1,0:T(8,128)(2,1)S(1)} %get-tuple-element.46.order, f32[4,16,128]{2,1,0:T(8,128)S(1)} %get-tuple-element.40.refs_1_.after), custom_call_target="tpu_custom_call" | custom-call | tf_op jit(solution)/shard_map/pack_second/pallas_call | solution.py:444
  16.2 2.0 %collective-permute-start.3 = (bf16[528,128]{1,0:T(8,128)(2,1)S(1)}, bf16[528,128]{1,0:T(8,128)(2,1)S(1)}, u32[]{:S(2)}, u32[]{:S(2)}) collective-permute-start(bf16[528,128]{1,0:T(8,128)(2,1)S(1)} %get-tuple-element.48), channel_id=1, source_target_pairs={{0,64},{64,128},{128,192},{192,0},{1,65},{65,129},{129,193},{193,1... | collective-permute-start | bytes 405512 | tf_op jit(solution)/shard_map/ppermute | solution.py:458
  18.1 2.7 %collective-permute-start.4 = (bf16[528,128]{1,0:T(8,128)(2,1)S(1)}, bf16[528,128]{1,0:T(8,128)(2,1)S(1)}, u32[]{:S(2)}, u32[]{:S(2)}) collective-permute-start(bf16[528,128]{1,0:T(8,128)(2,1)S(1)} %get-tuple-element.49), channel_id=1, source_target_pairs={{0,128},{64,192},{128,0},{192,64},{1,129},{65,193},{129,1},{193,65... | collective-permute-start | bytes 405512 | tf_op jit(solution)/shard_map/ppermute | solution.py:458
  20.9 1.5 %collective-permute-start.5 = (bf16[528,128]{1,0:T(8,128)(2,1)S(1)}, bf16[528,128]{1,0:T(8,128)(2,1)S(1)}, u32[]{:S(2)}, u32[]{:S(2)}) collective-permute-start(bf16[528,128]{1,0:T(8,128)(2,1)S(1)} %get-tuple-element.50), channel_id=1, source_target_pairs={{0,192},{64,0},{128,64},{192,128},{1,193},{65,1},{129,65},{193,129... | collective-permute-start | bytes 405512 | tf_op jit(solution)/shard_map/ppermute | solution.py:458
  22.8 3.0 %collective-permute-done.2.chunk = bf16[1584,128]{1,0:T(8,128)(2,1)S(1)} collective-permute-done((bf16[1584,128]{1,0:T(8,128)(2,1)S(1)}, bf16[1584,128]{1,0:T(8,128)(2,1)S(1)}, u32[]{:S(2)}, u32[]{:S(2)}) %collective-permute-start.2) | collective-permute-done | bytes 405536 | tf_op jit(solution)/shard_map/ppermute | solution.py:458
  25.8 1.9 %solve_first.1 = (bf16[4,2048,128]{2,1,0:T(8,128)(2,1)S(1)}, f32[4,16,128]{2,1,0:T(8,128)S(1)}, f32[4,16,128]{2,1,0:T(8,128)S(1)}, f32[16,128]{1,0:T(8,128)S(1)}, f32[16,128]{1,0:T(8,128)S(1)}) custom-call(bf16[4,2048,128]{2,1,0:T(8,128)(2,1)S(1)} %get-tuple-element.42.blocks_before, ...), custom_call_target="tpu_custom_call", output_to_operand_aliasing={{0}: (0, {}), {1}: (1, {})} | custom-call | tf_op jit(solution)/shard_map/solve_first/pallas_call | solution.py:444
  28.1 7.3 %collective-permute-start.7 = (f32[16,128]{1,0:T(8,128)S(1)}, f32[16,128]{1,0:T(8,128)S(1)}, u32[]{:S(2)}, u32[]{:S(2)}) collective-permute-start(f32[16,128]{1,0:T(8,128)S(1)} %get-tuple-element.54), channel_id=1, source_target_pairs={{64,128},{192,193},{129,65},{1,2},{66,130},{194,195},{131,67},{3,4... | collective-permute-start | bytes 24584 | tf_op jit(solution)/shard_map/ppermute | solution.py:472
  35.4 1.1 %apply_first.1.partial = f32[4,16,128]{2,1,0:T(8,128)S(1)} custom-call(bf16[4,2048,128]{2,1,0:T(8,128)(2,1)S(1)} %get-tuple-element.45.blocks, bf16[528,128]{1,0:T(8,128)(2,1)S(1)} %get-tuple-element.47.p0, bf16[528,128]{1,0:T(8,128)(2,1)S(1)} %collective-permute-done.3.p1, bf16[528,128]{1,0:T(8,128)(2,1)S(1)} %collective-permute-done.4.p2, ...), custom_call_target="tpu_custom_call" | custom-call | tf_op jit(solution)/shard_map/apply_first/pallas_call | solution.py:444
  36.7 1.6 %solve_second.1 = (f32[4,16,128]{2,1,0:T(8,128)S(1)}, f32[4,16,128]{2,1,0:T(8,128)S(1)}, f32[16,128]{1,0:T(8,128)S(1)}, f32[16,128]{1,0:T(8,128)S(1)}) custom-call(bf16[4,2048,128]{2,1,0:T(8,128)(2,1)S(1)} %get-tuple-element.45.blocks, f32[4,16,128]{2,1,0:T(8,128)S(1)} %apply_first.1.partial, f32[16,128]{1,0:T(8,128)S(1)} %collective-permute-done.6.inner, ...), custom_call_target="tpu_custom_call" | custom-call | tf_op jit(solution)/shard_map/solve_second/pallas_call | solution.py:444
  38.6 5.3 %collective-permute-start.9 = (f32[16,128]{1,0:T(8,128)S(1)}, f32[16,128]{1,0:T(8,128)S(1)}, u32[]{:S(2)}, u32[]{:S(2)}) collective-permute-start(f32[16,128]{1,0:T(8,128)S(1)} %get-tuple-element.57), channel_id=1, source_target_pairs={{64,128},{192,193},{129,65},{1,2},{66,130},{194,195},{131,67},{3,4... | collective-permute-start | bytes 24584 | tf_op jit(solution)/shard_map/ppermute | solution.py:472
  43.9 1.1 %apply_second.1.partial = f32[4,16,128]{2,1,0:T(8,128)S(1)} custom-call(bf16[4,2048,128]{2,1,0:T(8,128)(2,1)S(1)} %get-tuple-element.45.blocks, bf16[528,128]{1,0:T(8,128)(2,1)S(1)} %get-tuple-element.47.p0, bf16[528,128]{1,0:T(8,128)(2,1)S(1)} %collective-permute-done.3.p1, bf16[528,128]{1,0:T(8,128)(2,1)S(1)} %collective-permute-done.4.p2, ...), custom_call_target="tpu_custom_call" | custom-call | tf_op jit(solution)/shard_map/apply_second/pallas_call | solution.py:444
  45.2 1.5 %solve_last.1 = (f32[88,128]{1,0:T(8,128)S(1)}, f32[88,128]{1,0:T(8,128)S(1)}, f32[88,128]{1,0:T(8,128)S(1)}, f32[88,128]{1,0:T(8,128)S(1)}) custom-call(bf16[4,2048,128]{2,1,0:T(8,128)(2,1)S(1)} %get-tuple-element.45.blocks, f32[4,16,128]{2,1,0:T(8,128)S(1)} %apply_second.1.partial, f32[16,128]{1,0:T(8,128)S(1)} %collective-permute-done.8.inner, ...), custom_call_target="tpu_custom_call" | custom-call | tf_op jit(solution)/shard_map/solve_last/pallas_call | solution.py:444
  46.8 1.0 %collective-permute-start.11 = (f32[88,128]{1,0:T(8,128)S(1)}, f32[88,128]{1,0:T(8,128)S(1)}, u32[]{:S(2)}, u32[]{:S(2)}) collective-permute-start(f32[88,128]{1,0:T(8,128)S(1)} %get-tuple-element.62), channel_id=1, source_target_pairs={{0,128},{64,192},{128,0},{192,64},{1,129},{65,193},{129,1},{193,65... | collective-permute-start | bytes 135176 | tf_op jit(solution)/shard_map/ppermute | solution.py:458
  47.8 1.6 %collective-permute-start.12 = (f32[88,128]{1,0:T(8,128)S(1)}, f32[88,128]{1,0:T(8,128)S(1)}, u32[]{:S(2)}, u32[]{:S(2)}) collective-permute-start(f32[88,128]{1,0:T(8,128)S(1)} %get-tuple-element.63), channel_id=1, source_target_pairs={{0,192},{64,0},{128,64},{192,128},{1,193},{65,1},{129,65},{193,129... | collective-permute-start | bytes 135176 | tf_op jit(solution)/shard_map/ppermute | solution.py:458
  49.4 1.4 %collective-permute-done.10.b1 = f32[88,128]{1,0:T(8,128)S(1)} collective-permute-done((f32[88,128]{1,0:T(8,128)S(1)}, f32[88,128]{1,0:T(8,128)S(1)}, u32[]{:S(2)}, u32[]{:S(2)}) %collective-permute-start.10) | collective-permute-done | bytes 45088 | tf_op jit(solution)/shard_map/ppermute | solution.py:458
  51.4 1.0 %collective-permute-done.12.b3 = f32[88,128]{1,0:T(8,128)S(1)} collective-permute-done((f32[88,128]{1,0:T(8,128)S(1)}, f32[88,128]{1,0:T(8,128)S(1)}, u32[]{:S(2)}, u32[]{:S(2)}) %collective-permute-start.12) | collective-permute-done | bytes 45088 | tf_op jit(solution)/shard_map/ppermute | solution.py:458
  52.4 23.2 %all_to_all.5.sums = f32[64,1,128]{2,1,0:T(1,128)S(1)} all-to-all(f32[64,1,128]{2,1,0:T(1,128)S(1)} %broadcast_in_dim.18), channel_id=1, replica_groups=mesh['field'=4,'cross'=64] {'cross'}, dimensions={0} | all-to-all | bytes 65536 | tf_op jit(solution)/shard_map/all_to_all | solution.py:539
  75.5 1.1 %final.1 = (f32[64,128]{1,0:T(8,128)}, f32[64,128]{1,0:T(8,128)}, f32[64,128]{1,0:T(8,128)}) custom-call(f32[64,1,128]{2,1,0:T(1,128)S(1)} %all_to_all.5.sums, f32[64,128]{1,0:T(8,128)S(1)} %bitcast.12, f32[88,128]{1,0:T(8,128)S(1)} %get-tuple-element.60.b0, f32[88,128]{1,0:T(8,128)S(1)} %collective-permute-done.10.b1, ...), custom_call_target="tpu_custom_call" | custom-call | tf_op jit(solution)/shard_map/final/pallas_call | solution.py:444
  (18 shorter events, 2.5 us)
Async XLA Ops:
  3.8 10.2 %collective-permute-start = (bf16[1584,128]{1,0:T(8,128)(2,1)S(1)}, bf16[1584,128]{1,0:T(8,128)(2,1)S(1)}, u32[]{:S(2)}, u32[]{:S(2)}) collective-permute-start(bf16[1584,128]{1,0:T(8,128)(2,1)S(1)} %get-tuple-element.38), channel_id=1, source_target_pairs={{0,64},{64,128},{128,192},{192,0},{1,65},{65,129},{129,193},{193,1... | collective-permute-start | bytes 1216520 | tf_op jit(solution)/shard_map/ppermute | solution.py:458
  5.9 16.5 %collective-permute-start.1 = (bf16[1584,128]{1,0:T(8,128)(2,1)S(1)}, bf16[1584,128]{1,0:T(8,128)(2,1)S(1)}, u32[]{:S(2)}, u32[]{:S(2)}) collective-permute-start(bf16[1584,128]{1,0:T(8,128)(2,1)S(1)} %get-tuple-element.41), channel_id=1, source_target_pairs={{0,192},{64,0},{128,64},{192,128},{1,193},{65,1},{129,65},{193,129... | collective-permute-start | bytes 1216520 | tf_op jit(solution)/shard_map/ppermute | solution.py:458
  7.2 18.6 %collective-permute-start.2 = (bf16[1584,128]{1,0:T(8,128)(2,1)S(1)}, bf16[1584,128]{1,0:T(8,128)(2,1)S(1)}, u32[]{:S(2)}, u32[]{:S(2)}) collective-permute-start(bf16[1584,128]{1,0:T(8,128)(2,1)S(1)} %get-tuple-element.44), channel_id=1, source_target_pairs={{0,128},{64,192},{128,0},{192,64},{1,129},{65,193},{129,1},{193,65... | collective-permute-start | bytes 1216520 | tf_op jit(solution)/shard_map/ppermute | solution.py:458
  16.2 19.3 %collective-permute-start.3 = (bf16[528,128]{1,0:T(8,128)(2,1)S(1)}, bf16[528,128]{1,0:T(8,128)(2,1)S(1)}, u32[]{:S(2)}, u32[]{:S(2)}) collective-permute-start(bf16[528,128]{1,0:T(8,128)(2,1)S(1)} %get-tuple-element.48), channel_id=1, source_target_pairs={{0,64},{64,128},{128,192},{192,0},{1,65},{65,129},{129,193},{193,1... | collective-permute-start | bytes 405512 | tf_op jit(solution)/shard_map/ppermute | solution.py:458
  18.1 17.3 %collective-permute-start.4 = (bf16[528,128]{1,0:T(8,128)(2,1)S(1)}, bf16[528,128]{1,0:T(8,128)(2,1)S(1)}, u32[]{:S(2)}, u32[]{:S(2)}) collective-permute-start(bf16[528,128]{1,0:T(8,128)(2,1)S(1)} %get-tuple-element.49), channel_id=1, source_target_pairs={{0,128},{64,192},{128,0},{192,64},{1,129},{65,193},{129,1},{193,65... | collective-permute-start | bytes 405512 | tf_op jit(solution)/shard_map/ppermute | solution.py:458
  20.9 14.6 %collective-permute-start.5 = (bf16[528,128]{1,0:T(8,128)(2,1)S(1)}, bf16[528,128]{1,0:T(8,128)(2,1)S(1)}, u32[]{:S(2)}, u32[]{:S(2)}) collective-permute-start(bf16[528,128]{1,0:T(8,128)(2,1)S(1)} %get-tuple-element.50), channel_id=1, source_target_pairs={{0,192},{64,0},{128,64},{192,128},{1,193},{65,1},{129,65},{193,129... | collective-permute-start | bytes 405512 | tf_op jit(solution)/shard_map/ppermute | solution.py:458
  27.7 8.8 %collective-permute-start.6 = (f32[16,128]{1,0:T(8,128)S(1)}, f32[16,128]{1,0:T(8,128)S(1)}, u32[]{:S(2)}, u32[]{:S(2)}) collective-permute-start(f32[16,128]{1,0:T(8,128)S(1)} %get-tuple-element.53), channel_id=1, source_target_pairs={{0,64},{128,192},{193,129},{65,1},{2,66},{130,194},{195,131},{67,3... | collective-permute-start | bytes 24584 | tf_op jit(solution)/shard_map/ppermute | solution.py:472
  28.1 8.6 %collective-permute-start.7 = (f32[16,128]{1,0:T(8,128)S(1)}, f32[16,128]{1,0:T(8,128)S(1)}, u32[]{:S(2)}, u32[]{:S(2)}) collective-permute-start(f32[16,128]{1,0:T(8,128)S(1)} %get-tuple-element.54), channel_id=1, source_target_pairs={{64,128},{192,193},{129,65},{1,2},{66,130},{194,195},{131,67},{3,4... | collective-permute-start | bytes 24584 | tf_op jit(solution)/shard_map/ppermute | solution.py:472
  38.3 6.7 %collective-permute-start.8 = (f32[16,128]{1,0:T(8,128)S(1)}, f32[16,128]{1,0:T(8,128)S(1)}, u32[]{:S(2)}, u32[]{:S(2)}) collective-permute-start(f32[16,128]{1,0:T(8,128)S(1)} %get-tuple-element.56), channel_id=1, source_target_pairs={{0,64},{128,192},{193,129},{65,1},{2,66},{130,194},{195,131},{67,3... | collective-permute-start | bytes 24584 | tf_op jit(solution)/shard_map/ppermute | solution.py:472
  38.6 6.6 %collective-permute-start.9 = (f32[16,128]{1,0:T(8,128)S(1)}, f32[16,128]{1,0:T(8,128)S(1)}, u32[]{:S(2)}, u32[]{:S(2)}) collective-permute-start(f32[16,128]{1,0:T(8,128)S(1)} %get-tuple-element.57), channel_id=1, source_target_pairs={{64,128},{192,193},{129,65},{1,2},{66,130},{194,195},{131,67},{3,4... | collective-permute-start | bytes 24584 | tf_op jit(solution)/shard_map/ppermute | solution.py:472
  43.8 31.7 %copy-start = (f32[1,64,128]{2,1,0:T(8,128)S(1)}, f32[1,64,128]{2,1,0:T(8,128)}, u32[]{:S(2)}) copy-start(f32[1,64,128]{2,1,0:T(8,128)} %param.6) | copy-start | bytes 98308
  46.7 4.2 %collective-permute-start.10 = (f32[88,128]{1,0:T(8,128)S(1)}, f32[88,128]{1,0:T(8,128)S(1)}, u32[]{:S(2)}, u32[]{:S(2)}) collective-permute-start(f32[88,128]{1,0:T(8,128)S(1)} %get-tuple-element.61), channel_id=1, source_target_pairs={{0,64},{64,128},{128,192},{192,0},{1,65},{65,129},{129,193},{193,1... | collective-permute-start | bytes 135176 | tf_op jit(solution)/shard_map/ppermute | solution.py:458
  46.8 4.6 %collective-permute-start.11 = (f32[88,128]{1,0:T(8,128)S(1)}, f32[88,128]{1,0:T(8,128)S(1)}, u32[]{:S(2)}, u32[]{:S(2)}) collective-permute-start(f32[88,128]{1,0:T(8,128)S(1)} %get-tuple-element.62), channel_id=1, source_target_pairs={{0,128},{64,192},{128,0},{192,64},{1,129},{65,193},{129,1},{193,65... | collective-permute-start | bytes 135176 | tf_op jit(solution)/shard_map/ppermute | solution.py:458
  47.8 4.5 %collective-permute-start.12 = (f32[88,128]{1,0:T(8,128)S(1)}, f32[88,128]{1,0:T(8,128)S(1)}, u32[]{:S(2)}, u32[]{:S(2)}) collective-permute-start(f32[88,128]{1,0:T(8,128)S(1)} %get-tuple-element.63), channel_id=1, source_target_pairs={{0,192},{64,0},{128,64},{192,128},{1,193},{65,1},{129,65},{193,129... | collective-permute-start | bytes 135176 | tf_op jit(solution)/shard_map/ppermute | solution.py:458

commit v6 on v5

--- a/solution.py
+++ b/solution.py
@@ -85,7 +85,7 @@
 
 
 def pack_first_kernel(
-    neighbours, face_type, rhs, coupling, pivot, out0, out1, out2, out3, weights, order, *scratch
+    neighbours, face_type, rhs, coupling, pivot, out0, out1, out2, out3, weights, order, rhs_out, *scratch
 ):
     *held, sems = scratch
     copies = start_fetch((neighbours, face_type, rhs, coupling, pivot), held, sems)
@@ -129,6 +129,7 @@
 
     copies[2].wait()
     copies[4].wait()
+    rhs_out[...] = rhs[...]
     rows = parts_of(pivot)
     for part in bf16_parts(rhs[...], 2):
         rows.append(jnp.concatenate([part[16 * q : 16 * q + 16] for q in range(4)], axis=1))
@@ -380,38 +381,43 @@
     send_faces(packed, inner_out, outer_out)
 
 
-def last_solve_kernel(blocks, partial, inner, outer, weights, r, z, w, s, back0, back1, back2, back3, row_ref, t, u):
+def sums_kernel(partial, inner, outer, weights, r, z, w, s, image, sums):
     rows = add_faces(partial, inner, outer, weights)
-    packed = [to_packed(v) for v in line_solve(rows, blocks, row_ref)]
-    for elem in range(4):
-        t[elem] = rows[elem]
-        u[elem] = packed[elem]
 
     def values(ref):
         return [ref[elem] for elem in range(4)]
 
     z_, w_, s_ = values(z), values(w), values(s)
     seg = segment_of((1, 128))
-    sums = jnp.zeros((1, 128), f32)
+    total = jnp.zeros((1, 128), f32)
     for index, pair in enumerate(((values(r), z_), (z_, w_), (w_, s_), (s_, rows))):
-        total = product_sum(*pair)
-        total = total + pltpu.roll(total, 32, 1)
-        total = total + pltpu.roll(total, 64, 1)
-        sums = jnp.where(seg == index, total, sums)
+        total = jnp.where(seg == index, over_segments(product_sum(*pair)), total)
+    for elem in range(4):
+        image[elem] = rows[elem]
+    sums[...] = jnp.broadcast_to(total, sums.shape)
+
+
+def fold_kernel(rows, total):
+    total[...] = jnp.broadcast_to(jnp.sum(rows[...], axis=0), total.shape)
+
+
+def last_solve_kernel(blocks, z, w, s, t, back0, back1, back2, back3, row_ref, u):
+    packed = [to_packed(v) for v in line_solve([t[elem] for elem in range(4)], blocks, row_ref)]
+    for elem in range(4):
+        u[elem] = packed[elem]
     me = lax.axis_index("field")
     for d, back in enumerate((back0, back1, back2, back3)):
         elem = (me + d) & 3
         for index, ref in enumerate((z, w, s, t, u)):
             back[16 * index : 16 * index + 16, :] = ref[elem]
-        back[80:88, :] = jnp.broadcast_to(sums, (8, 128))
-
-
-def final_kernel(sums, rhs, b0, b1, b2, b3, order, solution, residual, precond):
+
+
+def final_kernel(s0, s1, s2, s3, rhs, b0, b1, b2, b3, order, solution, residual, precond):
     backs = (b0, b3, b2, b1)
     z, w, s, t, u = (
         jnp.concatenate([b[16 * index : 16 * index + 16, :] for b in backs], axis=1) for index in range(5)
     )
-    total = jnp.sum(sums[...], axis=0)
+    total = ((s0[...] + s1[...]) + (s2[...] + s3[...]))[0:1]
     totals = [jnp.sum(total[:, 32 * k : 32 * k + 32], axis=1, keepdims=True) for k in range(4)]
     rho, curve, second, third = totals
     alpha = rho / curve
@@ -436,7 +442,7 @@
 
 FACE = jax.ShapeDtypeStruct((16, 128), f32)
 VECTOR = jax.ShapeDtypeStruct((4, 16, 128), f32)
-BACK = jax.ShapeDtypeStruct((88, 128), f32)
+BACK = jax.ShapeDtypeStruct((80, 128), f32)
 BLOCKS = jax.ShapeDtypeStruct((4, ELEMENT_ROWS, 128), bf16)
 
 
@@ -475,11 +481,12 @@
 def local(rhs, pivot_inverse, line_coupling, element_block, neighbours, face_type):
     matrix, small = pltpu.VMEM((64, 64, 128), bf16), pltpu.VMEM((4, 128), jnp.int32)
     spread, wide = pltpu.VMEM((64, 128), f32), pltpu.VMEM((BLOCK_ROWS, 128), f32)
-    *chunks, weights, order = kernel(
+    shape = jax.ShapeDtypeStruct((64, 128), f32)
+    *chunks, weights, order, rhs_here = kernel(
         pack_first_kernel,
         in_hbm(neighbours.T, face_type.T, rhs[0], line_coupling[0], pivot_inverse[0]),
         [jax.ShapeDtypeStruct((FIRST_ROWS, 128), bf16)] * 4
-        + [jax.ShapeDtypeStruct((5, 16, 128), f32), jax.ShapeDtypeStruct((512, 512), bf16)],
+        + [jax.ShapeDtypeStruct((5, 16, 128), f32), jax.ShapeDtypeStruct((512, 512), bf16), shape],
         "pack_first",
         HBM,
         [small, small, pltpu.VMEM((64, 128), f32), matrix, matrix, pltpu.SemaphoreType.DMA((5,))],
@@ -526,19 +533,21 @@
     )
     inner, outer = exchange(inner, outer)
     (partial,) = kernel(apply_kernel, [blocks, *parts, s, weights], [VECTOR], "apply_second", scratch=[spread, products])
+    count = lax.axis_size("cross")
+    t, rows = kernel(
+        sums_kernel,
+        [partial, inner, outer, weights, r, z, w, s],
+        [VECTOR, jax.ShapeDtypeStruct((count, 128), f32)],
+        "sums",
+    )
+    rows = lax.all_to_all(rows.reshape(count, 1, 128), "cross", 0, 0)
     backs = kernel(
-        last_solve_kernel,
-        [blocks, partial, inner, outer, weights, r, z, w, s],
-        [BACK] * 4,
-        "solve_last",
-        scratch=[spread, pltpu.VMEM((4, 16, 128), f32), pltpu.VMEM((4, 16, 128), f32)],
+        last_solve_kernel, [blocks, z, w, s, t], [BACK] * 4, "solve_last", scratch=[spread, pltpu.VMEM((4, 16, 128), f32)]
     )
     returned = [backs[0]] + [around(backs[d], d) for d in (1, 2, 3)]
-    row = (returned[0][80:81] + returned[1][80:81]) + (returned[2][80:81] + returned[3][80:81])
-    rows = jnp.broadcast_to(row[None], (lax.axis_size("cross"), 1, 128))
-    sums = lax.all_to_all(rows, "cross", 0, 0)
-    shape = jax.ShapeDtypeStruct((64, 128), f32)
-    outs = kernel(final_kernel, [sums, rhs[0], *returned, order], [shape] * 3, "final")
+    (total,) = kernel(fold_kernel, [rows], [jax.ShapeDtypeStruct((8, 128), f32)], "fold")
+    totals = [total] + [around(total, d) for d in (1, 2, 3)]
+    outs = kernel(final_kernel, [*totals, rhs_here, *returned, order], [shape] * 3, "final")
     return tuple(out[None] for out in outs)
 
 

time: 76.9 us -> 75.7 us (0.984)
  blocking collectives: 23.2 us -> 0 us
  starting transfers between devices: 27.2 us -> 43.4 us
  waiting for transfers between devices: 10.9 us -> 16.1 us
    all_to_all x1 -> x0, blocking collectives: 23.2 us -> none  [local(): sums = lax.all_to_all(rows, 'cross', 0, 0)]
    all_to_all x0 -> x1, starting transfers between devices: none -> 13.1 us  [local(): rows = lax.all_to_all(rows.reshape(count, 1, 128), 'cross', 0, 0)]
    all_to_all x0 -> x1, waiting for transfers between devices: none -> 4.49 us  [local(): rows = lax.all_to_all(rows.reshape(count, 1, 128), 'cross', 0, 0)]
    ppermute x9 -> x12, starting transfers between devices: 14 us -> 17.2 us  [around(): lax.ppermute(value, 'field', [(i, (i + distance) % count) for i in range(...]
    ppermute x9 -> x12, waiting for transfers between devices: 10.5 us -> 11.2 us  [around(): lax.ppermute(value, 'field', [(i, (i + distance) % count) for i in range(...]
    pallas_call x11 -> x13, Pallas kernels: 14.6 us -> 15.2 us  [kernel(): pl.pallas_call(body, out_shape=outs, in_specs=spec if isinstance(spec, li...]
  transfers between devices with their start and end apart: 13 -> 17, of which waited for: 7 -> 7; matrix products, arithmetic and copies ran while one was open for 0% -> 0% of each run, Pallas kernels for 9% -> 12%
where the time goes in v6:
time: 75.7 us; the launch traced here: 75.5 us
  starting transfers between devices  43.4 us (57%)
  waiting for transfers between devices  16.1 us (21%)
  Pallas kernels  15.2 us (20%)
  between operations  0.8 us (1%)
    ppermute x12, starting transfers between devices, around(): lax.ppermute(value, 'field', [(i, (i + distance) % count) for i in range(...  17.2 us
    pallas_call x13, Pallas kernels, kernel(): pl.pallas_call(body, out_shape=outs, in_specs=spec if isinstance(spec, li...  15.2 us
    ppermute x4, starting transfers between devices, exchange(): lax.ppermute(faces, ('field', 'cross'), column_swaps(first))  13.1 us
    all_to_all x1, starting transfers between devices, local(): rows = lax.all_to_all(rows.reshape(count, 1, 128), 'cross', 0, 0)  13.1 us
    ppermute x12, waiting for transfers between devices, around(): lax.ppermute(value, 'field', [(i, (i + distance) % count) for i in range(...  11.2 us
    all_to_all x1, waiting for transfers between devices, local(): rows = lax.all_to_all(rows.reshape(count, 1, 128), 'cross', 0, 0)  4.49 us
  transfers between devices with their start and end apart: 17, of which 7 were waited for; matrix products, arithmetic and copies ran while one was open for 0% of the time, Pallas kernels for 12%

profile of v6, /device:TPU:1, one launch (start us, length us, event | category | flops | bytes accessed | tf_op | source)
XLA Modules:
  0.0 75.5 jit_solution(12849329425562015445)
XLA Ops:
  0.6 3.1 %pack_first.1 = (bf16[1584,128]{1,0:T(8,128)(2,1)S(1)}, bf16[1584,128]{1,0:T(8,128)(2,1)S(1)}, bf16[1584,128]{1,0:T(8,128)(2,1)S(1)}, bf16[1584,128]{1,0:T(8,128...) custom-call(s32[4,128]{1,0:T(4,128)} %bitcast.14, s32[4,128]{1,0:T(4,128)} %bitcast.15, ...), custom_call_target="tpu_custom_call" | custom-call | tf_op jit(solution)/shard_map/pack_first/pallas_call | solution.py:450
  3.8 2.1 %collective-permute-start = (bf16[1584,128]{1,0:T(8,128)(2,1)S(1)}, bf16[1584,128]{1,0:T(8,128)(2,1)S(1)}, u32[]{:S(2)}, u32[]{:S(2)}) collective-permute-start(bf16[1584,128]{1,0:T(8,128)(2,1)S(1)} %get-tuple-element.41), channel_id=1, source_target_pairs={{0,64},{64,128},{128,192},{192,0},{1,65},{65,129},{129,193},{193,1... | collective-permute-start | bytes 1216520 | tf_op jit(solution)/shard_map/ppermute | solution.py:464
  5.9 1.4 %collective-permute-start.1 = (bf16[1584,128]{1,0:T(8,128)(2,1)S(1)}, bf16[1584,128]{1,0:T(8,128)(2,1)S(1)}, u32[]{:S(2)}, u32[]{:S(2)}) collective-permute-start(bf16[1584,128]{1,0:T(8,128)(2,1)S(1)} %get-tuple-element.44), channel_id=1, source_target_pairs={{0,192},{64,0},{128,64},{192,128},{1,193},{65,1},{129,65},{193,129... | collective-permute-start | bytes 1216520 | tf_op jit(solution)/shard_map/ppermute | solution.py:464
  7.2 1.6 %collective-permute-start.2 = (bf16[1584,128]{1,0:T(8,128)(2,1)S(1)}, bf16[1584,128]{1,0:T(8,128)(2,1)S(1)}, u32[]{:S(2)}, u32[]{:S(2)}) collective-permute-start(bf16[1584,128]{1,0:T(8,128)(2,1)S(1)} %get-tuple-element.47), channel_id=1, source_target_pairs={{0,128},{64,192},{128,0},{192,64},{1,129},{65,193},{129,1},{193,65... | collective-permute-start | bytes 1216520 | tf_op jit(solution)/shard_map/ppermute | solution.py:464
  9.4 4.6 %collective-permute-done.refs_2_ = bf16[1584,128]{1,0:T(8,128)(2,1)S(1)} collective-permute-done((bf16[1584,128]{1,0:T(8,128)(2,1)S(1)}, bf16[1584,128]{1,0:T(8,128)(2,1)S(1)}, u32[]{:S(2)}, u32[]{:S(2)}) %collective-permute-start) | collective-permute-done | bytes 405536 | tf_op jit(solution)/shard_map/ppermute | solution.py:464
  14.4 1.7 %pack_second.1 = (bf16[528,128]{1,0:T(8,128)(2,1)S(1)}, bf16[528,128]{1,0:T(8,128)(2,1)S(1)}, bf16[528,128]{1,0:T(8,128)(2,1)S(1)}, bf16[528,128]{1,0:T(8,128)(2,1)S(1)}) custom-call(bf16[64,64,128]{2,1,0:T(8,128)(2,1)} %bitcast.12, bf16[512,512]{1,0:T(8,128)(2,1)S(1)} %get-tuple-element.49.order, f32[4,16,128]{2,1,0:T(8,128)S(1)} %get-tuple-element.43.refs_1_.after), custom_call_target="tpu_custom_call" | custom-call | tf_op jit(solution)/shard_map/pack_second/pallas_call | solution.py:450
  16.2 1.9 %collective-permute-start.3 = (bf16[528,128]{1,0:T(8,128)(2,1)S(1)}, bf16[528,128]{1,0:T(8,128)(2,1)S(1)}, u32[]{:S(2)}, u32[]{:S(2)}) collective-permute-start(bf16[528,128]{1,0:T(8,128)(2,1)S(1)} %get-tuple-element.51), channel_id=1, source_target_pairs={{0,64},{64,128},{128,192},{192,0},{1,65},{65,129},{129,193},{193,1... | collective-permute-start | bytes 405512 | tf_op jit(solution)/shard_map/ppermute | solution.py:464
  18.1 2.8 %collective-permute-start.4 = (bf16[528,128]{1,0:T(8,128)(2,1)S(1)}, bf16[528,128]{1,0:T(8,128)(2,1)S(1)}, u32[]{:S(2)}, u32[]{:S(2)}) collective-permute-start(bf16[528,128]{1,0:T(8,128)(2,1)S(1)} %get-tuple-element.52), channel_id=1, source_target_pairs={{0,128},{64,192},{128,0},{192,64},{1,129},{65,193},{129,1},{193,65... | collective-permute-start | bytes 405512 | tf_op jit(solution)/shard_map/ppermute | solution.py:464
  20.9 1.5 %collective-permute-start.5 = (bf16[528,128]{1,0:T(8,128)(2,1)S(1)}, bf16[528,128]{1,0:T(8,128)(2,1)S(1)}, u32[]{:S(2)}, u32[]{:S(2)}) collective-permute-start(bf16[528,128]{1,0:T(8,128)(2,1)S(1)} %get-tuple-element.53), channel_id=1, source_target_pairs={{0,192},{64,0},{128,64},{192,128},{1,193},{65,1},{129,65},{193,129... | collective-permute-start | bytes 405512 | tf_op jit(solution)/shard_map/ppermute | solution.py:464
  22.8 3.0 %collective-permute-done.2.chunk = bf16[1584,128]{1,0:T(8,128)(2,1)S(1)} collective-permute-done((bf16[1584,128]{1,0:T(8,128)(2,1)S(1)}, bf16[1584,128]{1,0:T(8,128)(2,1)S(1)}, u32[]{:S(2)}, u32[]{:S(2)}) %collective-permute-start.2) | collective-permute-done | bytes 405536 | tf_op jit(solution)/shard_map/ppermute | solution.py:464
  25.8 1.9 %solve_first.1 = (bf16[4,2048,128]{2,1,0:T(8,128)(2,1)S(1)}, f32[4,16,128]{2,1,0:T(8,128)S(1)}, f32[4,16,128]{2,1,0:T(8,128)S(1)}, f32[16,128]{1,0:T(8,128)S(1)}, f32[16,128]{1,0:T(8,128)S(1)}) custom-call(bf16[4,2048,128]{2,1,0:T(8,128)(2,1)S(1)} %get-tuple-element.45.blocks_before, ...), custom_call_target="tpu_custom_call", output_to_operand_aliasing={{0}: (0, {}), {1}: (1, {})} | custom-call | tf_op jit(solution)/shard_map/solve_first/pallas_call | solution.py:450
  28.1 7.3 %collective-permute-start.7 = (f32[16,128]{1,0:T(8,128)S(1)}, f32[16,128]{1,0:T(8,128)S(1)}, u32[]{:S(2)}, u32[]{:S(2)}) collective-permute-start(f32[16,128]{1,0:T(8,128)S(1)} %get-tuple-element.57), channel_id=1, source_target_pairs={{64,128},{192,193},{129,65},{1,2},{66,130},{194,195},{131,67},{3,4... | collective-permute-start | bytes 24584 | tf_op jit(solution)/shard_map/ppermute | solution.py:478
  35.4 1.1 %apply_first.1.partial = f32[4,16,128]{2,1,0:T(8,128)S(1)} custom-call(bf16[4,2048,128]{2,1,0:T(8,128)(2,1)S(1)} %get-tuple-element.48.blocks, bf16[528,128]{1,0:T(8,128)(2,1)S(1)} %get-tuple-element.50.p0, bf16[528,128]{1,0:T(8,128)(2,1)S(1)} %collective-permute-done.3.p1, bf16[528,128]{1,0:T(8,128)(2,1)S(1)} %collective-permute-done.4.p2, ...), custom_call_target="tpu_custom_call" | custom-call | tf_op jit(solution)/shard_map/apply_first/pallas_call | solution.py:450
  36.7 1.6 %solve_second.1 = (f32[4,16,128]{2,1,0:T(8,128)S(1)}, f32[4,16,128]{2,1,0:T(8,128)S(1)}, f32[16,128]{1,0:T(8,128)S(1)}, f32[16,128]{1,0:T(8,128)S(1)}) custom-call(bf16[4,2048,128]{2,1,0:T(8,128)(2,1)S(1)} %get-tuple-element.48.blocks, f32[4,16,128]{2,1,0:T(8,128)S(1)} %apply_first.1.partial, f32[16,128]{1,0:T(8,128)S(1)} %collective-permute-done.6.inner, ...), custom_call_target="tpu_custom_call" | custom-call | tf_op jit(solution)/shard_map/solve_second/pallas_call | solution.py:450
  38.5 5.2 %collective-permute-start.9 = (f32[16,128]{1,0:T(8,128)S(1)}, f32[16,128]{1,0:T(8,128)S(1)}, u32[]{:S(2)}, u32[]{:S(2)}) collective-permute-start(f32[16,128]{1,0:T(8,128)S(1)} %get-tuple-element.60), channel_id=1, source_target_pairs={{64,128},{192,193},{129,65},{1,2},{66,130},{194,195},{131,67},{3,4... | collective-permute-start | bytes 24584 | tf_op jit(solution)/shard_map/ppermute | solution.py:478
  43.8 1.1 %apply_second.1.partial = f32[4,16,128]{2,1,0:T(8,128)S(1)} custom-call(bf16[4,2048,128]{2,1,0:T(8,128)(2,1)S(1)} %get-tuple-element.48.blocks, bf16[528,128]{1,0:T(8,128)(2,1)S(1)} %get-tuple-element.50.p0, bf16[528,128]{1,0:T(8,128)(2,1)S(1)} %collective-permute-done.3.p1, bf16[528,128]{1,0:T(8,128)(2,1)S(1)} %collective-permute-done.4.p2, ...), custom_call_target="tpu_custom_call" | custom-call | tf_op jit(solution)/shard_map/apply_second/pallas_call | solution.py:450
  45.9 13.1 %all-to-all-start = ((f32[64,1,128]{2,1,0:T(1,128)}), f32[64,1,128]{2,1,0:T(1,128)S(1)}, u32[]{:S(2)}, u32[]{:S(2)}) async-start(f32[64,1,128]{2,1,0:T(1,128)} %bitcast.6), calls=%async_computation | async-start | bytes 65536 | tf_op jit(solution)/shard_map/all_to_all | solution.py:543
  59.0 1.4 %solve_last.1 = (f32[80,128]{1,0:T(8,128)S(1)}, f32[80,128]{1,0:T(8,128)S(1)}, f32[80,128]{1,0:T(8,128)S(1)}, f32[80,128]{1,0:T(8,128)S(1)}) custom-call(bf16[4,2048,128]{2,1,0:T(8,128)(2,1)S(1)} %get-tuple-element.48.blocks, f32[4,16,128]{2,1,0:T(8,128)S(1)} %get-tuple-element.54.vector.z, f32[4,16,128]{2,1,0:T(8,128)S(1)} %get-tuple-element.62.w, ...), custom_call_target="tpu_custom_call" | custom-call | tf_op jit(solution)/shard_map/solve_last/pallas_call | solution.py:450
  61.7 2.0 %collective-permute-start.15 = (f32[80,128]{1,0:T(8,128)S(1)}, f32[80,128]{1,0:T(8,128)S(1)}, u32[]{:S(2)}, u32[]{:S(2)}) collective-permute-start(f32[80,128]{1,0:T(8,128)S(1)} %get-tuple-element.69), channel_id=1, source_target_pairs={{0,192},{64,0},{128,64},{192,128},{1,193},{65,1},{129,65},{193,129... | collective-permute-start | bytes 122888 | tf_op jit(solution)/shard_map/ppermute | solution.py:464
  63.7 4.5 %all-to-all-done.rows = f32[64,1,128]{2,1,0:T(1,128)S(1)} async-done(((f32[64,1,128]{2,1,0:T(1,128)}), f32[64,1,128]{2,1,0:T(1,128)S(1)}, u32[]{:S(2)}, u32[]{:S(2)}) %all-to-all-start) | async-done | bytes 32800 | tf_op jit(solution)/shard_map/all_to_all | solution.py:543
  68.4 2.5 %collective-permute-start.11 = (f32[8,128]{1,0:T(8,128)S(1)}, f32[8,128]{1,0:T(8,128)S(1)}, u32[]{:S(2)}, u32[]{:S(2)}) collective-permute-start(f32[8,128]{1,0:T(8,128)S(1)} %fold.1.s0), channel_id=1, source_target_pairs={{0,128},{64,192},{128,0},{192,64},{1,129},{65,193},{129,1},{193,65... | collective-permute-start | bytes 12296 | tf_op jit(solution)/shard_map/ppermute | solution.py:464
  70.9 1.6 %collective-permute-done.11.s2 = f32[8,128]{1,0:T(8,128)S(1)} collective-permute-done((f32[8,128]{1,0:T(8,128)S(1)}, f32[8,128]{1,0:T(8,128)S(1)}, u32[]{:S(2)}, u32[]{:S(2)}) %collective-permute-start.11) | collective-permute-done | bytes 4128 | tf_op jit(solution)/shard_map/ppermute | solution.py:464
  72.4 2.1 %collective-permute-done.10.s1 = f32[8,128]{1,0:T(8,128)S(1)} collective-permute-done((f32[8,128]{1,0:T(8,128)S(1)}, f32[8,128]{1,0:T(8,128)S(1)}, u32[]{:S(2)}, u32[]{:S(2)}) %collective-permute-start.10) | collective-permute-done | bytes 4128 | tf_op jit(solution)/shard_map/ppermute | solution.py:464
  74.5 1.0 %final.1 = (f32[64,128]{1,0:T(8,128)}, f32[64,128]{1,0:T(8,128)}, f32[64,128]{1,0:T(8,128)}) custom-call(f32[8,128]{1,0:T(8,128)S(1)} %fold.1.s0, f32[8,128]{1,0:T(8,128)S(1)} %collective-permute-done.10.s1, f32[8,128]{1,0:T(8,128)S(1)} %collective-permute-done.11.s2, f32[8,128]{1,0:T(8,128)S(1)} %collective-permute-done.12.s3, ...), custom_call_target="tpu_custom_call" | custom-call | tf_op jit(solution)/shard_map/final/pallas_call | solution.py:450
  (23 shorter events, 4.8 us)
Async XLA Ops:
  3.8 10.2 %collective-permute-start = (bf16[1584,128]{1,0:T(8,128)(2,1)S(1)}, bf16[1584,128]{1,0:T(8,128)(2,1)S(1)}, u32[]{:S(2)}, u32[]{:S(2)}) collective-permute-start(bf16[1584,128]{1,0:T(8,128)(2,1)S(1)} %get-tuple-element.41), channel_id=1, source_target_pairs={{0,64},{64,128},{128,192},{192,0},{1,65},{65,129},{129,193},{193,1... | collective-permute-start | bytes 1216520 | tf_op jit(solution)/shard_map/ppermute | solution.py:464
  5.9 16.5 %collective-permute-start.1 = (bf16[1584,128]{1,0:T(8,128)(2,1)S(1)}, bf16[1584,128]{1,0:T(8,128)(2,1)S(1)}, u32[]{:S(2)}, u32[]{:S(2)}) collective-permute-start(bf16[1584,128]{1,0:T(8,128)(2,1)S(1)} %get-tuple-element.44), channel_id=1, source_target_pairs={{0,192},{64,0},{128,64},{192,128},{1,193},{65,1},{129,65},{193,129... | collective-permute-start | bytes 1216520 | tf_op jit(solution)/shard_map/ppermute | solution.py:464
  7.2 18.6 %collective-permute-start.2 = (bf16[1584,128]{1,0:T(8,128)(2,1)S(1)}, bf16[1584,128]{1,0:T(8,128)(2,1)S(1)}, u32[]{:S(2)}, u32[]{:S(2)}) collective-permute-start(bf16[1584,128]{1,0:T(8,128)(2,1)S(1)} %get-tuple-element.47), channel_id=1, source_target_pairs={{0,128},{64,192},{128,0},{192,64},{1,129},{65,193},{129,1},{193,65... | collective-permute-start | bytes 1216520 | tf_op jit(solution)/shard_map/ppermute | solution.py:464
  16.2 19.2 %collective-permute-start.3 = (bf16[528,128]{1,0:T(8,128)(2,1)S(1)}, bf16[528,128]{1,0:T(8,128)(2,1)S(1)}, u32[]{:S(2)}, u32[]{:S(2)}) collective-permute-start(bf16[528,128]{1,0:T(8,128)(2,1)S(1)} %get-tuple-element.51), channel_id=1, source_target_pairs={{0,64},{64,128},{128,192},{192,0},{1,65},{65,129},{129,193},{193,1... | collective-permute-start | bytes 405512 | tf_op jit(solution)/shard_map/ppermute | solution.py:464
  18.1 17.3 %collective-permute-start.4 = (bf16[528,128]{1,0:T(8,128)(2,1)S(1)}, bf16[528,128]{1,0:T(8,128)(2,1)S(1)}, u32[]{:S(2)}, u32[]{:S(2)}) collective-permute-start(bf16[528,128]{1,0:T(8,128)(2,1)S(1)} %get-tuple-element.52), channel_id=1, source_target_pairs={{0,128},{64,192},{128,0},{192,64},{1,129},{65,193},{129,1},{193,65... | collective-permute-start | bytes 405512 | tf_op jit(solution)/shard_map/ppermute | solution.py:464
  20.9 14.6 %collective-permute-start.5 = (bf16[528,128]{1,0:T(8,128)(2,1)S(1)}, bf16[528,128]{1,0:T(8,128)(2,1)S(1)}, u32[]{:S(2)}, u32[]{:S(2)}) collective-permute-start(bf16[528,128]{1,0:T(8,128)(2,1)S(1)} %get-tuple-element.53), channel_id=1, source_target_pairs={{0,192},{64,0},{128,64},{192,128},{1,193},{65,1},{129,65},{193,129... | collective-permute-start | bytes 405512 | tf_op jit(solution)/shard_map/ppermute | solution.py:464
  27.7 8.8 %collective-permute-start.6 = (f32[16,128]{1,0:T(8,128)S(1)}, f32[16,128]{1,0:T(8,128)S(1)}, u32[]{:S(2)}, u32[]{:S(2)}) collective-permute-start(f32[16,128]{1,0:T(8,128)S(1)} %get-tuple-element.56), channel_id=1, source_target_pairs={{0,64},{128,192},{193,129},{65,1},{2,66},{130,194},{195,131},{67,3... | collective-permute-start | bytes 24584 | tf_op jit(solution)/shard_map/ppermute | solution.py:478
  28.1 8.6 %collective-permute-start.7 = (f32[16,128]{1,0:T(8,128)S(1)}, f32[16,128]{1,0:T(8,128)S(1)}, u32[]{:S(2)}, u32[]{:S(2)}) collective-permute-start(f32[16,128]{1,0:T(8,128)S(1)} %get-tuple-element.57), channel_id=1, source_target_pairs={{64,128},{192,193},{129,65},{1,2},{66,130},{194,195},{131,67},{3,4... | collective-permute-start | bytes 24584 | tf_op jit(solution)/shard_map/ppermute | solution.py:478
  38.3 6.6 %collective-permute-start.8 = (f32[16,128]{1,0:T(8,128)S(1)}, f32[16,128]{1,0:T(8,128)S(1)}, u32[]{:S(2)}, u32[]{:S(2)}) collective-permute-start(f32[16,128]{1,0:T(8,128)S(1)} %get-tuple-element.59), channel_id=1, source_target_pairs={{0,64},{128,192},{193,129},{65,1},{2,66},{130,194},{195,131},{67,3... | collective-permute-start | bytes 24584 | tf_op jit(solution)/shard_map/ppermute | solution.py:478
  38.5 6.6 %collective-permute-start.9 = (f32[16,128]{1,0:T(8,128)S(1)}, f32[16,128]{1,0:T(8,128)S(1)}, u32[]{:S(2)}, u32[]{:S(2)}) collective-permute-start(f32[16,128]{1,0:T(8,128)S(1)} %get-tuple-element.60), channel_id=1, source_target_pairs={{64,128},{192,193},{129,65},{1,2},{66,130},{194,195},{131,67},{3,4... | collective-permute-start | bytes 24584 | tf_op jit(solution)/shard_map/ppermute | solution.py:478
  45.9 22.3 %all-to-all-start = ((f32[64,1,128]{2,1,0:T(1,128)}), f32[64,1,128]{2,1,0:T(1,128)S(1)}, u32[]{:S(2)}, u32[]{:S(2)}) async-start(f32[64,1,128]{2,1,0:T(1,128)} %bitcast.6), calls=%async_computation | async-start | bytes 65536 | tf_op jit(solution)/shard_map/all_to_all | solution.py:543
  60.4 10.4 %collective-permute-start.13 = (f32[80,128]{1,0:T(8,128)S(1)}, f32[80,128]{1,0:T(8,128)S(1)}, u32[]{:S(2)}, u32[]{:S(2)}) collective-permute-start(f32[80,128]{1,0:T(8,128)S(1)} %get-tuple-element.67), channel_id=1, source_target_pairs={{0,64},{64,128},{128,192},{192,0},{1,65},{65,129},{129,193},{193,1... | collective-permute-start | bytes 122888 | tf_op jit(solution)/shard_map/ppermute | solution.py:464
  61.2 9.7 %collective-permute-start.14 = (f32[80,128]{1,0:T(8,128)S(1)}, f32[80,128]{1,0:T(8,128)S(1)}, u32[]{:S(2)}, u32[]{:S(2)}) collective-permute-start(f32[80,128]{1,0:T(8,128)S(1)} %get-tuple-element.68), channel_id=1, source_target_pairs={{0,128},{64,192},{128,0},{192,64},{1,129},{65,193},{129,1},{193,65... | collective-permute-start | bytes 122888 | tf_op jit(solution)/shard_map/ppermute | solution.py:464
  61.7 9.1 %collective-permute-start.15 = (f32[80,128]{1,0:T(8,128)S(1)}, f32[80,128]{1,0:T(8,128)S(1)}, u32[]{:S(2)}, u32[]{:S(2)}) collective-permute-start(f32[80,128]{1,0:T(8,128)S(1)} %get-tuple-element.69), channel_id=1, source_target_pairs={{0,192},{64,0},{128,64},{192,128},{1,193},{65,1},{129,65},{193,129... | collective-permute-start | bytes 122888 | tf_op jit(solution)/shard_map/ppermute | solution.py:464
  68.3 2.6 %collective-permute-start.12 = (f32[8,128]{1,0:T(8,128)S(1)}, f32[8,128]{1,0:T(8,128)S(1)}, u32[]{:S(2)}, u32[]{:S(2)}) collective-permute-start(f32[8,128]{1,0:T(8,128)S(1)} %fold.1.s0), channel_id=1, source_target_pairs={{0,192},{64,0},{128,64},{192,128},{1,193},{65,1},{129,65},{193,129... | collective-permute-start | bytes 12296 | tf_op jit(solution)/shard_map/ppermute | solution.py:464
  68.4 4.0 %collective-permute-start.11 = (f32[8,128]{1,0:T(8,128)S(1)}, f32[8,128]{1,0:T(8,128)S(1)}, u32[]{:S(2)}, u32[]{:S(2)}) collective-permute-start(f32[8,128]{1,0:T(8,128)S(1)} %fold.1.s0), channel_id=1, source_target_pairs={{0,128},{64,192},{128,0},{192,64},{1,129},{65,193},{129,1},{193,65... | collective-permute-start | bytes 12296 | tf_op jit(solution)/shard_map/ppermute | solution.py:464
  70.8 3.7 %collective-permute-start.10 = (f32[8,128]{1,0:T(8,128)S(1)}, f32[8,128]{1,0:T(8,128)S(1)}, u32[]{:S(2)}, u32[]{:S(2)}) collective-permute-start(f32[8,128]{1,0:T(8,128)S(1)} %fold.1.s0), channel_id=1, source_target_pairs={{0,64},{64,128},{128,192},{192,0},{1,65},{65,129},{129,193},{193,1... | collective-permute-start | bytes 12296 | tf_op jit(solution)/shard_map/ppermute | solution.py:464

commit v7 on v6

--- a/solution.py
+++ b/solution.py
@@ -1,5 +1,3 @@
-import functools
-
 import jax
 import jax.numpy as jnp
 from jax import lax
@@ -62,6 +60,19 @@
     result = matmul_nt(left, sorting).astype(bf16)
     for d in range(4):
         outs[d][start : start + rows, :] = result[:, d * 128 : (d + 1) * 128]
+
+
+def hits_of(position, distance, line):
+    return position == ((lax.axis_index("field") + distance) & 3) * 32 + line
+
+
+def sorting_matrix(position):
+    sub = row_of((128, 128))
+    rows = []
+    for d in range(4):
+        hit = hits_of(position, d, sub & 31)
+        rows.append(jnp.concatenate([jnp.where(hit & ((sub >> 5) == q), 1.0, 0.0) for q in range(4)], axis=1))
+    return jnp.concatenate(rows, axis=0).astype(bf16)
 
 
 def parts_of(block):
@@ -84,13 +95,11 @@
     return [jnp.concatenate(parts, axis=1) for parts in (wide, short, corner, edge)]
 
 
-def pack_first_kernel(
-    neighbours, face_type, rhs, coupling, pivot, out0, out1, out2, out3, weights, order, rhs_out, *scratch
-):
+def pack_first_kernel(neighbours, rhs, coupling, pivot, out0, out1, out2, out3, place, rhs_out, *scratch):
     *held, sems = scratch
-    copies = start_fetch((neighbours, face_type, rhs, coupling, pivot), held, sems)
-    neighbours, face_type, rhs, coupling, pivot = held
-    me, cross = lax.axis_index("field"), lax.axis_index("cross")
+    copies = start_fetch((neighbours, rhs, coupling, pivot), held, sems)
+    neighbours, rhs, coupling, pivot = held
+    cross = lax.axis_index("cross")
     square = (128, 128)
     lane = lax.broadcasted_iota(jnp.int32, square, 1)
     sub = row_of(square)
@@ -114,32 +123,36 @@
     owner = jnp.where(cross % 2 == 0, column, 3.0 - column)
     position = (owner * 32.0 + row).astype(jnp.int32)[0:1]
 
-    segment = sub >> 5
-    hits = [position == (((me + d) & 3) * 32 + (sub & 31)) for d in range(4)]
-    for q in range(4):
-        for d in range(4):
-            order[d * 128 : (d + 1) * 128, q * 128 : (q + 1) * 128] = jnp.where(
-                hits[d] & (segment == q), 1.0, 0.0
-            ).astype(bf16)
-
-    outs, sorting = (out0, out1, out2, out3), order[...]
-    copies[3].wait()
+    place[...] = jnp.broadcast_to(position, place.shape)
+
+    sorting = sorting_matrix(position)
+    outs = (out0, out1, out2, out3)
+    copies[2].wait()
     left = [coupling[:, 16 * q : 16 * q + 16, :].reshape(BLOCK_ROWS, 128) for q in range(4)]
     send(jnp.concatenate(left, axis=1), sorting, outs, COUPLING, BLOCK_ROWS)
 
-    copies[2].wait()
-    copies[4].wait()
+    copies[1].wait()
+    copies[3].wait()
     rhs_out[...] = rhs[...]
     rows = parts_of(pivot)
     for part in bf16_parts(rhs[...], 2):
         rows.append(jnp.concatenate([part[16 * q : 16 * q + 16] for q in range(4)], axis=1))
     send(jnp.concatenate(rows, axis=0), sorting, outs, WIDE, FIRST_ROWS - WIDE)
 
+
+def pack_second_kernel(diagonal, face_type, place, after, out0, out1, out2, out3, weights, order, held, faces, sems):
+    copies = start_fetch((diagonal, face_type), (held, faces), sems)
+    sub = row_of((128, 128))
+    position = place[0:1, :]
+    order[...] = sorting_matrix(position)
+    copies[0].wait()
+    send(jnp.concatenate(parts_of(held), axis=0), order[...], (out0, out1, out2, out3), 0, SECOND_ROWS)
+
     copies[1].wait()
-    interior = jnp.where(face_type[...] == 0, 2.0, 0.0)
-    own = interior + jnp.where(face_type[...] == 1, 4.0, 0.0)
+    interior = jnp.where(faces[...] == 0, 2.0, 0.0)
+    own = interior + jnp.where(faces[...] == 1, 4.0, 0.0)
     table = jnp.concatenate([own, interior, jnp.zeros((8, 128), f32)], axis=0).astype(bf16)
-    placed = matmul_nt(table, jnp.where(hits[0], 1.0, 0.0).astype(bf16))
+    placed = matmul_nt(table, jnp.where(hits_of(position, 0, sub & 31), 1.0, 0.0).astype(bf16))
     shape = (16, 128)
     seg, m = segment_of(shape), row_of(shape)
     masks = [seg == 0, seg == 3, m < 4, m >= 12]
@@ -148,12 +161,6 @@
         total = total + jnp.where(masks[face], placed[face : face + 1], 0.0)
         weights[1 + face] = jnp.where(masks[face], placed[4 + face : 5 + face], 0.0)
     weights[0] = total
-
-
-def pack_second_kernel(diagonal, order, after, out0, out1, out2, out3, held, sems):
-    (copy,) = start_fetch([diagonal], [held], sems)
-    copy.wait()
-    send(jnp.concatenate(parts_of(held), axis=0), order[...], (out0, out1, out2, out3), 0, SECOND_ROWS)
 
 
 def in_hbm(*arrays):
@@ -209,32 +216,34 @@
     return rows
 
 
-def corner_row(parts, k):
+def corner_row(read, k):
     odd = segment_of((16, 128)) % 2 == 1
     start = CORNER - WIDE + 16 * (k % 8)
-    row = parts[start : start + 16, :].astype(f32)
+    row = read(start, 16)
     if k < 8:
         return jnp.where(odd, pltpu.roll(row, 32, 1), row)
     return jnp.where(odd, row, pltpu.roll(row, 96, 1))
 
 
-def unpack(chunk, blocks, residual, elem, wide):
+def unpack(chunk, blocks, wide):
     shape = (16, 128)
     seg, m = segment_of(shape), row_of(shape)
-    blocks[elem, 0:BLOCK_ROWS, :] = chunk[COUPLING : COUPLING + BLOCK_ROWS, :]
-    residual[elem] = chunk[RESIDUAL : RESIDUAL + 16, :].astype(f32) + chunk[RESIDUAL + 16 : RESIDUAL + 32, :].astype(f32)
-    parts = chunk.at[WIDE:RESIDUAL, :]
+
+    def read(start, rows):
+        return chunk[start : start + rows, :].astype(f32)
+
+    blocks[0:BLOCK_ROWS, :] = chunk[COUPLING : COUPLING + BLOCK_ROWS, :]
     for k in range(16):
-        corner = corner_row(parts, k)
-        last = parts[16 * k : 16 * k + 16, :].astype(f32)
-        third = parts[256 + 16 * (k % 8) : 272 + 16 * (k % 8), :].astype(f32)
+        corner = corner_row(lambda start, rows: read(WIDE + start, rows), k)
+        last = read(WIDE + 16 * k, 16)
+        third = read(SHORT + 16 * (k % 8), 16)
         if k >= 8:
             third = pltpu.roll(third, 64, 1)
         wide[16 * k : 16 * k + 16, :] = corner
         wide[256 + 16 * k : 272 + 16 * k, :] = jnp.where(seg == 0, pltpu.roll(last, 32, 1), corner)
         wide[512 + 16 * k : 528 + 16 * k, :] = jnp.where(seg == 2, corner, third)
         wide[768 + 16 * k : 784 + 16 * k, :] = jnp.where(seg == 3, corner, last)
-    edge = chunk[EDGE : EDGE + 16, :].astype(f32)
+    edge = read(EDGE, 16)
     for k in range(16):
         turned = turn_segments([wide[pl.ds(256 * q + k, 16, stride=16), :] for q in range(4)])
         for q in range(4):
@@ -243,7 +252,8 @@
             value = jnp.where(here, wide[16 * a : 16 * a + 16, :], turned[q])
             if q % 2 == 1:
                 value = jnp.where((seg == q) & (m == k), edge, value)
-            blocks[elem, PIVOT + 16 * a : PIVOT + 16 * a + 16, :] = value.astype(bf16)
+            blocks[PIVOT + 16 * a : PIVOT + 16 * a + 16, :] = value.astype(bf16)
+    return read(RESIDUAL, 16) + read(RESIDUAL + 16, 16)
 
 
 def diagonal_times(parts, packed):
@@ -262,7 +272,7 @@
     diagonal = parts[EDGE - WIDE : EDGE - WIDE + 16, :].astype(f32)
     corner = []
     for k in range(16):
-        row = corner_row(parts, k)
+        row = corner_row(lambda start, rows: parts[start : start + rows, :].astype(f32), k)
         diagonal = jnp.where((m == k) & ~odd, row, diagonal)
         corner.append(jnp.where(jnp.where(odd, m - k, k - m) > 0, row, 0.0))
     down, right = both_ways(jnp.concatenate(corner, axis=0).reshape(16, 16, 128), 16, packed, packed)
@@ -349,13 +359,23 @@
     return jnp.sum(total, axis=0, keepdims=True)
 
 
-def unpack_kernel(distance, *refs):
-    *_, chunk, blocks, residual, wide = refs
-    unpack(chunk, blocks, residual, (lax.axis_index("field") - distance) & 3, wide)
-
-
-def solve_kernel(blocks_before, residual_before, chunk, blocks, residual, values, inner_out, outer_out, row_ref, wide):
-    unpack(chunk, blocks, residual, (lax.axis_index("field") - 2) & 3, wide)
+def unpack_kernel(chunk, blocks, residual, wide):
+    residual[...] = unpack(chunk, blocks, wide)
+
+
+def solve_kernel(b0, r0, b1, r1, b3, r3, chunk, blocks, residual, values, inner_out, outer_out, row_ref, wide, sems):
+    me = lax.axis_index("field")
+    copies = []
+    for d, source, part in ((0, b0, r0), (1, b1, r1), (3, b3, r3)):
+        elem = (me - d) & 3
+        residual[elem] = part[...]
+        copies.append(pltpu.make_async_copy(source, blocks.at[elem], sems.at[d]))
+    for copy in copies:
+        copy.start()
+    elem = (me - 2) & 3
+    residual[elem] = unpack(chunk, blocks.at[elem], wide)
+    for copy in copies:
+        copy.wait()
     packed = [to_packed(v) for v in line_solve([residual[elem] for elem in range(4)], blocks, row_ref)]
     for elem in range(4):
         values[elem] = packed[elem]
@@ -446,14 +466,13 @@
 BLOCKS = jax.ShapeDtypeStruct((4, ELEMENT_ROWS, 128), bf16)
 
 
-def kernel(body, arrays, outs, name, spec=VMEM, scratch=(), aliases=None):
+def kernel(body, arrays, outs, name, spec=VMEM, scratch=()):
     return pl.pallas_call(
         body,
         out_shape=outs,
         in_specs=spec if isinstance(spec, list) else [spec] * len(arrays),
         out_specs=[VMEM] * len(outs),
         scratch_shapes=list(scratch),
-        input_output_aliases=aliases or {},
         compiler_params=params(),
         name=name,
     )(*arrays)
@@ -480,36 +499,36 @@
 
 def local(rhs, pivot_inverse, line_coupling, element_block, neighbours, face_type):
     matrix, small = pltpu.VMEM((64, 64, 128), bf16), pltpu.VMEM((4, 128), jnp.int32)
-    spread, wide = pltpu.VMEM((64, 128), f32), pltpu.VMEM((BLOCK_ROWS, 128), f32)
+    spread, wide = pltpu.VMEM((64, 128), f32), pltpu.VMEM((BLOCK_ROWS + 16, 128), f32)
     shape = jax.ShapeDtypeStruct((64, 128), f32)
-    *chunks, weights, order, rhs_here = kernel(
+    *chunks, place, rhs_here = kernel(
         pack_first_kernel,
-        in_hbm(neighbours.T, face_type.T, rhs[0], line_coupling[0], pivot_inverse[0]),
-        [jax.ShapeDtypeStruct((FIRST_ROWS, 128), bf16)] * 4
-        + [jax.ShapeDtypeStruct((5, 16, 128), f32), jax.ShapeDtypeStruct((512, 512), bf16), shape],
+        in_hbm(neighbours.T, rhs[0], line_coupling[0], pivot_inverse[0]),
+        [jax.ShapeDtypeStruct((FIRST_ROWS, 128), bf16)] * 4 + [jax.ShapeDtypeStruct((8, 128), jnp.int32), shape],
         "pack_first",
         HBM,
-        [small, small, pltpu.VMEM((64, 128), f32), matrix, matrix, pltpu.SemaphoreType.DMA((5,))],
+        [small, pltpu.VMEM((64, 128), f32), matrix, matrix, pltpu.SemaphoreType.DMA((4,))],
     )
     held = []
     first = {d: around(chunks[d], d) if d else chunks[0] for d in (0, 1, 3, 2)}
     for d in (0, 1, 3):
-        held = kernel(
-            functools.partial(unpack_kernel, d),
-            [*held, first[d]],
-            [BLOCKS, VECTOR],
+        last = kernel(
+            unpack_kernel,
+            [first[d]],
+            [jax.ShapeDtypeStruct((ELEMENT_ROWS, 128), bf16), FACE],
             f"unpack_{d}",
             scratch=[wide],
-            aliases={0: 0, 1: 1} if held else None,
         )
+        held += last
         if d == 1:
-            chunks = kernel(
+            *chunks, weights, order = kernel(
                 pack_second_kernel,
-                in_hbm(element_block[0]) + [order, held[1]],
-                [jax.ShapeDtypeStruct((SECOND_ROWS, 128), bf16)] * 4,
+                in_hbm(element_block[0], face_type.T) + [place, last[1]],
+                [jax.ShapeDtypeStruct((SECOND_ROWS, 128), bf16)] * 4
+                + [jax.ShapeDtypeStruct((5, 16, 128), f32), jax.ShapeDtypeStruct((512, 512), bf16)],
                 "pack_second",
-                [HBM, VMEM, VMEM],
-                [matrix, pltpu.SemaphoreType.DMA((1,))],
+                [HBM, HBM, VMEM, VMEM],
+                [matrix, small, pltpu.SemaphoreType.DMA((2,))],
             )
             second = {d: around(chunks[d], d) if d else chunks[0] for d in (0, 1, 3, 2)}
     blocks, r, z, inner, outer = kernel(
@@ -517,8 +536,7 @@
         [*held, first[2]],
         [BLOCKS, VECTOR, VECTOR, FACE, FACE],
         "solve_first",
-        scratch=[spread, wide],
-        aliases={0: 0, 1: 1},
+        scratch=[spread, wide, pltpu.SemaphoreType.DMA((4,))],
     )
     inner, outer = exchange(inner, outer)
     parts = [second[d] for d in range(4)]

time: 75.7 us -> 75.7 us (level)
  no operation moved by 1% of the time
where the time goes in v7:
time: 75.7 us; the launch traced here: 75.5 us
  starting transfers between devices  43.3 us (57%)
  waiting for transfers between devices  16 us (21%)
  Pallas kernels  15.3 us (20%)
  between operations  0.81 us (1%)
    ppermute x12, starting transfers between devices, around(): lax.ppermute(value, 'field', [(i, (i + distance) % count) for i in range(...  17.1 us
    pallas_call x13, Pallas kernels, kernel(): pl.pallas_call(body, out_shape=outs, in_specs=spec if isinstance(spec, li...  15.3 us
    ppermute x4, starting transfers between devices, exchange(): lax.ppermute(faces, ('field', 'cross'), column_swaps(first))  13.3 us
    all_to_all x1, starting transfers between devices, local(): rows = lax.all_to_all(rows.reshape(count, 1, 128), 'cross', 0, 0)  13 us
    ppermute x12, waiting for transfers between devices, around(): lax.ppermute(value, 'field', [(i, (i + distance) % count) for i in range(...  11.2 us
    all_to_all x1, waiting for transfers between devices, local(): rows = lax.all_to_all(rows.reshape(count, 1, 128), 'cross', 0, 0)  4.49 us
  transfers between devices with their start and end apart: 17, of which 7 were waited for; matrix products, arithmetic and copies ran while one was open for 0% of the time, Pallas kernels for 12%

profile of v7, /device:TPU:1, one launch (start us, length us, event | category | flops | bytes accessed | tf_op | source)
XLA Modules:
  0.0 75.5 jit_solution(12424704566937018260)
XLA Ops:
  0.6 2.8 %pack_first.1 = (bf16[1584,128]{1,0:T(8,128)(2,1)S(1)}, bf16[1584,128]{1,0:T(8,128)(2,1)S(1)}, bf16[1584,128]{1,0:T(8,128)(2,1)S(1)}, bf16[1584,128]{1,0:T(8,128...) custom-call(s32[4,128]{1,0:T(4,128)} %bitcast.14, f32[64,128]{1,0:T(8,128)} %bitcast.13, ...), custom_call_target="tpu_custom_call" | custom-call | tf_op jit(solution)/shard_map/pack_first/pallas_call | solution.py:470
  3.5 2.1 %collective-permute-start = (bf16[1584,128]{1,0:T(8,128)(2,1)S(1)}, bf16[1584,128]{1,0:T(8,128)(2,1)S(1)}, u32[]{:S(2)}, u32[]{:S(2)}) collective-permute-start(bf16[1584,128]{1,0:T(8,128)(2,1)S(1)} %get-tuple-element.42), channel_id=1, source_target_pairs={{0,64},{64,128},{128,192},{192,0},{1,65},{65,129},{129,193},{193,1... | collective-permute-start | bytes 1216520 | tf_op jit(solution)/shard_map/ppermute | solution.py:483
  5.6 1.4 %collective-permute-start.1 = (bf16[1584,128]{1,0:T(8,128)(2,1)S(1)}, bf16[1584,128]{1,0:T(8,128)(2,1)S(1)}, u32[]{:S(2)}, u32[]{:S(2)}) collective-permute-start(bf16[1584,128]{1,0:T(8,128)(2,1)S(1)} %get-tuple-element.45), channel_id=1, source_target_pairs={{0,192},{64,0},{128,64},{192,128},{1,193},{65,1},{129,65},{193,129... | collective-permute-start | bytes 1216520 | tf_op jit(solution)/shard_map/ppermute | solution.py:483
  6.9 1.6 %collective-permute-start.2 = (bf16[1584,128]{1,0:T(8,128)(2,1)S(1)}, bf16[1584,128]{1,0:T(8,128)(2,1)S(1)}, u32[]{:S(2)}, u32[]{:S(2)}) collective-permute-start(bf16[1584,128]{1,0:T(8,128)(2,1)S(1)} %get-tuple-element.48), channel_id=1, source_target_pairs={{0,128},{64,192},{128,0},{192,64},{1,129},{65,193},{129,1},{193,65... | collective-permute-start | bytes 1216520 | tf_op jit(solution)/shard_map/ppermute | solution.py:483
  8.6 5.1 %collective-permute-done.chunk = bf16[1584,128]{1,0:T(8,128)(2,1)S(1)} collective-permute-done((bf16[1584,128]{1,0:T(8,128)(2,1)S(1)}, bf16[1584,128]{1,0:T(8,128)(2,1)S(1)}, u32[]{:S(2)}, u32[]{:S(2)}) %collective-permute-start) | collective-permute-done | bytes 405536 | tf_op jit(solution)/shard_map/ppermute | solution.py:483
  14.2 1.9 %pack_second.1 = (bf16[528,128]{1,0:T(8,128)(2,1)S(1)}, bf16[528,128]{1,0:T(8,128)(2,1)S(1)}, bf16[528,128]{1,0:T(8,128)(2,1)S(1)}, bf16[528,128]{1,0:T(8,128)(2...) custom-call(bf16[64,64,128]{2,1,0:T(8,128)(2,1)} %bitcast.12, s32[4,128]{1,0:T(4,128)} %bitcast.15, ...), custom_call_target="tpu_custom_call" | custom-call | tf_op jit(solution)/shard_map/pack_second/pallas_call | solution.py:470
  16.0 1.9 %collective-permute-start.3 = (bf16[528,128]{1,0:T(8,128)(2,1)S(1)}, bf16[528,128]{1,0:T(8,128)(2,1)S(1)}, u32[]{:S(2)}, u32[]{:S(2)}) collective-permute-start(bf16[528,128]{1,0:T(8,128)(2,1)S(1)} %get-tuple-element.52), channel_id=1, source_target_pairs={{0,64},{64,128},{128,192},{192,0},{1,65},{65,129},{129,193},{193,1... | collective-permute-start | bytes 405512 | tf_op jit(solution)/shard_map/ppermute | solution.py:483
  18.0 2.8 %collective-permute-start.4 = (bf16[528,128]{1,0:T(8,128)(2,1)S(1)}, bf16[528,128]{1,0:T(8,128)(2,1)S(1)}, u32[]{:S(2)}, u32[]{:S(2)}) collective-permute-start(bf16[528,128]{1,0:T(8,128)(2,1)S(1)} %get-tuple-element.53), channel_id=1, source_target_pairs={{0,128},{64,192},{128,0},{192,64},{1,129},{65,193},{129,1},{193,65... | collective-permute-start | bytes 405512 | tf_op jit(solution)/shard_map/ppermute | solution.py:483
  20.7 1.4 %collective-permute-start.5 = (bf16[528,128]{1,0:T(8,128)(2,1)S(1)}, bf16[528,128]{1,0:T(8,128)(2,1)S(1)}, u32[]{:S(2)}, u32[]{:S(2)}) collective-permute-start(bf16[528,128]{1,0:T(8,128)(2,1)S(1)} %get-tuple-element.54), channel_id=1, source_target_pairs={{0,192},{64,0},{128,64},{192,128},{1,193},{65,1},{129,65},{193,129... | collective-permute-start | bytes 405512 | tf_op jit(solution)/shard_map/ppermute | solution.py:483
  23.1 2.4 %collective-permute-done.2.chunk = bf16[1584,128]{1,0:T(8,128)(2,1)S(1)} collective-permute-done((bf16[1584,128]{1,0:T(8,128)(2,1)S(1)}, bf16[1584,128]{1,0:T(8,128)(2,1)S(1)}, u32[]{:S(2)}, u32[]{:S(2)}) %collective-permute-start.2) | collective-permute-done | bytes 405536 | tf_op jit(solution)/shard_map/ppermute | solution.py:483
  25.6 2.1 %solve_first.1 = (bf16[4,2048,128]{2,1,0:T(8,128)(2,1)S(1)}, f32[4,16,128]{2,1,0:T(8,128)S(1)}, f32[4,16,128]{2,1,0:T(8,128)S(1)}, f32[16,128]{1,0:T(8,128)S(1)}, f32[16,128]{1,0:T(8,128)S(1)}) custom-call(bf16[2048,128]{1,0:T(8,128)(2,1)S(1)} %get-tuple-element.40.b0, f32[16,128]{1,0:T(8,128)S(1)} %get-tuple-element.41.r0, ...), custom_call_target="tpu_custom_call" | custom-call | tf_op jit(solution)/shard_map/solve_first/pallas_call | solution.py:470
  28.1 7.3 %collective-permute-start.7 = (f32[16,128]{1,0:T(8,128)S(1)}, f32[16,128]{1,0:T(8,128)S(1)}, u32[]{:S(2)}, u32[]{:S(2)}) collective-permute-start(f32[16,128]{1,0:T(8,128)S(1)} %get-tuple-element.58), channel_id=1, source_target_pairs={{64,128},{192,193},{129,65},{1,2},{66,130},{194,195},{131,67},{3,4... | collective-permute-start | bytes 24584 | tf_op jit(solution)/shard_map/ppermute | solution.py:497
  35.4 1.1 %apply_first.1.partial = f32[4,16,128]{2,1,0:T(8,128)S(1)} custom-call(bf16[4,2048,128]{2,1,0:T(8,128)(2,1)S(1)} %get-tuple-element.49.blocks, bf16[528,128]{1,0:T(8,128)(2,1)S(1)} %get-tuple-element.51.p0, bf16[528,128]{1,0:T(8,128)(2,1)S(1)} %collective-permute-done.3.p1, bf16[528,128]{1,0:T(8,128)(2,1)S(1)} %collective-permute-done.4.p2, ...), custom_call_target="tpu_custom_call" | custom-call | tf_op jit(solution)/shard_map/apply_first/pallas_call | solution.py:470
  36.7 1.6 %solve_second.1 = (f32[4,16,128]{2,1,0:T(8,128)S(1)}, f32[4,16,128]{2,1,0:T(8,128)S(1)}, f32[16,128]{1,0:T(8,128)S(1)}, f32[16,128]{1,0:T(8,128)S(1)}) custom-call(bf16[4,2048,128]{2,1,0:T(8,128)(2,1)S(1)} %get-tuple-element.49.blocks, f32[4,16,128]{2,1,0:T(8,128)S(1)} %apply_first.1.partial, f32[16,128]{1,0:T(8,128)S(1)} %collective-permute-done.6.inner, ...), custom_call_target="tpu_custom_call" | custom-call | tf_op jit(solution)/shard_map/solve_second/pallas_call | solution.py:470
  38.5 5.3 %collective-permute-start.9 = (f32[16,128]{1,0:T(8,128)S(1)}, f32[16,128]{1,0:T(8,128)S(1)}, u32[]{:S(2)}, u32[]{:S(2)}) collective-permute-start(f32[16,128]{1,0:T(8,128)S(1)} %get-tuple-element.61), channel_id=1, source_target_pairs={{64,128},{192,193},{129,65},{1,2},{66,130},{194,195},{131,67},{3,4... | collective-permute-start | bytes 24584 | tf_op jit(solution)/shard_map/ppermute | solution.py:497
  43.8 1.1 %apply_second.1.partial = f32[4,16,128]{2,1,0:T(8,128)S(1)} custom-call(bf16[4,2048,128]{2,1,0:T(8,128)(2,1)S(1)} %get-tuple-element.49.blocks, bf16[528,128]{1,0:T(8,128)(2,1)S(1)} %get-tuple-element.51.p0, bf16[528,128]{1,0:T(8,128)(2,1)S(1)} %collective-permute-done.3.p1, bf16[528,128]{1,0:T(8,128)(2,1)S(1)} %collective-permute-done.4.p2, ...), custom_call_target="tpu_custom_call" | custom-call | tf_op jit(solution)/shard_map/apply_second/pallas_call | solution.py:470
  45.9 13.0 %all-to-all-start = ((f32[64,1,128]{2,1,0:T(1,128)}), f32[64,1,128]{2,1,0:T(1,128)S(1)}, u32[]{:S(2)}, u32[]{:S(2)}) async-start(f32[64,1,128]{2,1,0:T(1,128)} %bitcast.6), calls=%async_computation | async-start | bytes 65536 | tf_op jit(solution)/shard_map/all_to_all | solution.py:561
  59.0 1.4 %solve_last.1 = (f32[80,128]{1,0:T(8,128)S(1)}, f32[80,128]{1,0:T(8,128)S(1)}, f32[80,128]{1,0:T(8,128)S(1)}, f32[80,128]{1,0:T(8,128)S(1)}) custom-call(bf16[4,2048,128]{2,1,0:T(8,128)(2,1)S(1)} %get-tuple-element.49.blocks, f32[4,16,128]{2,1,0:T(8,128)S(1)} %get-tuple-element.55.vector.z, f32[4,16,128]{2,1,0:T(8,128)S(1)} %get-tuple-element.63.w, ...), custom_call_target="tpu_custom_call" | custom-call | tf_op jit(solution)/shard_map/solve_last/pallas_call | solution.py:470
  61.7 2.0 %collective-permute-start.15 = (f32[80,128]{1,0:T(8,128)S(1)}, f32[80,128]{1,0:T(8,128)S(1)}, u32[]{:S(2)}, u32[]{:S(2)}) collective-permute-start(f32[80,128]{1,0:T(8,128)S(1)} %get-tuple-element.70), channel_id=1, source_target_pairs={{0,192},{64,0},{128,64},{192,128},{1,193},{65,1},{129,65},{193,129... | collective-permute-start | bytes 122888 | tf_op jit(solution)/shard_map/ppermute | solution.py:483
  63.7 4.5 %all-to-all-done.rows = f32[64,1,128]{2,1,0:T(1,128)S(1)} async-done(((f32[64,1,128]{2,1,0:T(1,128)}), f32[64,1,128]{2,1,0:T(1,128)S(1)}, u32[]{:S(2)}, u32[]{:S(2)}) %all-to-all-start) | async-done | bytes 32800 | tf_op jit(solution)/shard_map/all_to_all | solution.py:561
  68.3 2.4 %collective-permute-start.11 = (f32[8,128]{1,0:T(8,128)S(1)}, f32[8,128]{1,0:T(8,128)S(1)}, u32[]{:S(2)}, u32[]{:S(2)}) collective-permute-start(f32[8,128]{1,0:T(8,128)S(1)} %fold.1.s0), channel_id=1, source_target_pairs={{0,128},{64,192},{128,0},{192,64},{1,129},{65,193},{129,1},{193,65... | collective-permute-start | bytes 12296 | tf_op jit(solution)/shard_map/ppermute | solution.py:483
  70.8 1.6 %collective-permute-done.11.s2 = f32[8,128]{1,0:T(8,128)S(1)} collective-permute-done((f32[8,128]{1,0:T(8,128)S(1)}, f32[8,128]{1,0:T(8,128)S(1)}, u32[]{:S(2)}, u32[]{:S(2)}) %collective-permute-start.11) | collective-permute-done | bytes 4128 | tf_op jit(solution)/shard_map/ppermute | solution.py:483
  72.4 2.1 %collective-permute-done.10.s1 = f32[8,128]{1,0:T(8,128)S(1)} collective-permute-done((f32[8,128]{1,0:T(8,128)S(1)}, f32[8,128]{1,0:T(8,128)S(1)}, u32[]{:S(2)}, u32[]{:S(2)}) %collective-permute-start.10) | collective-permute-done | bytes 4128 | tf_op jit(solution)/shard_map/ppermute | solution.py:483
  74.4 1.0 %final.1 = (f32[64,128]{1,0:T(8,128)}, f32[64,128]{1,0:T(8,128)}, f32[64,128]{1,0:T(8,128)}) custom-call(f32[8,128]{1,0:T(8,128)S(1)} %fold.1.s0, f32[8,128]{1,0:T(8,128)S(1)} %collective-permute-done.10.s1, f32[8,128]{1,0:T(8,128)S(1)} %collective-permute-done.11.s2, f32[8,128]{1,0:T(8,128)S(1)} %collective-permute-done.12.s3, ...), custom_call_target="tpu_custom_call" | custom-call | tf_op jit(solution)/shard_map/final/pallas_call | solution.py:470
  (23 shorter events, 4.8 us)
Async XLA Ops:
  3.5 10.2 %collective-permute-start = (bf16[1584,128]{1,0:T(8,128)(2,1)S(1)}, bf16[1584,128]{1,0:T(8,128)(2,1)S(1)}, u32[]{:S(2)}, u32[]{:S(2)}) collective-permute-start(bf16[1584,128]{1,0:T(8,128)(2,1)S(1)} %get-tuple-element.42), channel_id=1, source_target_pairs={{0,64},{64,128},{128,192},{192,0},{1,65},{65,129},{129,193},{193,1... | collective-permute-start | bytes 1216520 | tf_op jit(solution)/shard_map/ppermute | solution.py:483
  5.6 17.1 %collective-permute-start.1 = (bf16[1584,128]{1,0:T(8,128)(2,1)S(1)}, bf16[1584,128]{1,0:T(8,128)(2,1)S(1)}, u32[]{:S(2)}, u32[]{:S(2)}) collective-permute-start(bf16[1584,128]{1,0:T(8,128)(2,1)S(1)} %get-tuple-element.45), channel_id=1, source_target_pairs={{0,192},{64,0},{128,64},{192,128},{1,193},{65,1},{129,65},{193,129... | collective-permute-start | bytes 1216520 | tf_op jit(solution)/shard_map/ppermute | solution.py:483
  6.9 18.6 %collective-permute-start.2 = (bf16[1584,128]{1,0:T(8,128)(2,1)S(1)}, bf16[1584,128]{1,0:T(8,128)(2,1)S(1)}, u32[]{:S(2)}, u32[]{:S(2)}) collective-permute-start(bf16[1584,128]{1,0:T(8,128)(2,1)S(1)} %get-tuple-element.48), channel_id=1, source_target_pairs={{0,128},{64,192},{128,0},{192,64},{1,129},{65,193},{129,1},{193,65... | collective-permute-start | bytes 1216520 | tf_op jit(solution)/shard_map/ppermute | solution.py:483
  16.0 19.3 %collective-permute-start.3 = (bf16[528,128]{1,0:T(8,128)(2,1)S(1)}, bf16[528,128]{1,0:T(8,128)(2,1)S(1)}, u32[]{:S(2)}, u32[]{:S(2)}) collective-permute-start(bf16[528,128]{1,0:T(8,128)(2,1)S(1)} %get-tuple-element.52), channel_id=1, source_target_pairs={{0,64},{64,128},{128,192},{192,0},{1,65},{65,129},{129,193},{193,1... | collective-permute-start | bytes 405512 | tf_op jit(solution)/shard_map/ppermute | solution.py:483
  18.0 17.4 %collective-permute-start.4 = (bf16[528,128]{1,0:T(8,128)(2,1)S(1)}, bf16[528,128]{1,0:T(8,128)(2,1)S(1)}, u32[]{:S(2)}, u32[]{:S(2)}) collective-permute-start(bf16[528,128]{1,0:T(8,128)(2,1)S(1)} %get-tuple-element.53), channel_id=1, source_target_pairs={{0,128},{64,192},{128,0},{192,64},{1,129},{65,193},{129,1},{193,65... | collective-permute-start | bytes 405512 | tf_op jit(solution)/shard_map/ppermute | solution.py:483
  20.7 14.7 %collective-permute-start.5 = (bf16[528,128]{1,0:T(8,128)(2,1)S(1)}, bf16[528,128]{1,0:T(8,128)(2,1)S(1)}, u32[]{:S(2)}, u32[]{:S(2)}) collective-permute-start(bf16[528,128]{1,0:T(8,128)(2,1)S(1)} %get-tuple-element.54), channel_id=1, source_target_pairs={{0,192},{64,0},{128,64},{192,128},{1,193},{65,1},{129,65},{193,129... | collective-permute-start | bytes 405512 | tf_op jit(solution)/shard_map/ppermute | solution.py:483
  27.7 8.8 %collective-permute-start.6 = (f32[16,128]{1,0:T(8,128)S(1)}, f32[16,128]{1,0:T(8,128)S(1)}, u32[]{:S(2)}, u32[]{:S(2)}) collective-permute-start(f32[16,128]{1,0:T(8,128)S(1)} %get-tuple-element.57), channel_id=1, source_target_pairs={{0,64},{128,192},{193,129},{65,1},{2,66},{130,194},{195,131},{67,3... | collective-permute-start | bytes 24584 | tf_op jit(solution)/shard_map/ppermute | solution.py:497
  28.1 8.6 %collective-permute-start.7 = (f32[16,128]{1,0:T(8,128)S(1)}, f32[16,128]{1,0:T(8,128)S(1)}, u32[]{:S(2)}, u32[]{:S(2)}) collective-permute-start(f32[16,128]{1,0:T(8,128)S(1)} %get-tuple-element.58), channel_id=1, source_target_pairs={{64,128},{192,193},{129,65},{1,2},{66,130},{194,195},{131,67},{3,4... | collective-permute-start | bytes 24584 | tf_op jit(solution)/shard_map/ppermute | solution.py:497
  38.2 6.7 %collective-permute-start.8 = (f32[16,128]{1,0:T(8,128)S(1)}, f32[16,128]{1,0:T(8,128)S(1)}, u32[]{:S(2)}, u32[]{:S(2)}) collective-permute-start(f32[16,128]{1,0:T(8,128)S(1)} %get-tuple-element.60), channel_id=1, source_target_pairs={{0,64},{128,192},{193,129},{65,1},{2,66},{130,194},{195,131},{67,3... | collective-permute-start | bytes 24584 | tf_op jit(solution)/shard_map/ppermute | solution.py:497
  38.5 6.6 %collective-permute-start.9 = (f32[16,128]{1,0:T(8,128)S(1)}, f32[16,128]{1,0:T(8,128)S(1)}, u32[]{:S(2)}, u32[]{:S(2)}) collective-permute-start(f32[16,128]{1,0:T(8,128)S(1)} %get-tuple-element.61), channel_id=1, source_target_pairs={{64,128},{192,193},{129,65},{1,2},{66,130},{194,195},{131,67},{3,4... | collective-permute-start | bytes 24584 | tf_op jit(solution)/shard_map/ppermute | solution.py:497
  45.9 22.3 %all-to-all-start = ((f32[64,1,128]{2,1,0:T(1,128)}), f32[64,1,128]{2,1,0:T(1,128)S(1)}, u32[]{:S(2)}, u32[]{:S(2)}) async-start(f32[64,1,128]{2,1,0:T(1,128)} %bitcast.6), calls=%async_computation | async-start | bytes 65536 | tf_op jit(solution)/shard_map/all_to_all | solution.py:561
  60.4 10.4 %collective-permute-start.13 = (f32[80,128]{1,0:T(8,128)S(1)}, f32[80,128]{1,0:T(8,128)S(1)}, u32[]{:S(2)}, u32[]{:S(2)}) collective-permute-start(f32[80,128]{1,0:T(8,128)S(1)} %get-tuple-element.68), channel_id=1, source_target_pairs={{0,64},{64,128},{128,192},{192,0},{1,65},{65,129},{129,193},{193,1... | collective-permute-start | bytes 122888 | tf_op jit(solution)/shard_map/ppermute | solution.py:483
  61.1 9.7 %collective-permute-start.14 = (f32[80,128]{1,0:T(8,128)S(1)}, f32[80,128]{1,0:T(8,128)S(1)}, u32[]{:S(2)}, u32[]{:S(2)}) collective-permute-start(f32[80,128]{1,0:T(8,128)S(1)} %get-tuple-element.69), channel_id=1, source_target_pairs={{0,128},{64,192},{128,0},{192,64},{1,129},{65,193},{129,1},{193,65... | collective-permute-start | bytes 122888 | tf_op jit(solution)/shard_map/ppermute | solution.py:483
  61.7 9.1 %collective-permute-start.15 = (f32[80,128]{1,0:T(8,128)S(1)}, f32[80,128]{1,0:T(8,128)S(1)}, u32[]{:S(2)}, u32[]{:S(2)}) collective-permute-start(f32[80,128]{1,0:T(8,128)S(1)} %get-tuple-element.70), channel_id=1, source_target_pairs={{0,192},{64,0},{128,64},{192,128},{1,193},{65,1},{129,65},{193,129... | collective-permute-start | bytes 122888 | tf_op jit(solution)/shard_map/ppermute | solution.py:483
  68.3 2.5 %collective-permute-start.12 = (f32[8,128]{1,0:T(8,128)S(1)}, f32[8,128]{1,0:T(8,128)S(1)}, u32[]{:S(2)}, u32[]{:S(2)}) collective-permute-start(f32[8,128]{1,0:T(8,128)S(1)} %fold.1.s0), channel_id=1, source_target_pairs={{0,192},{64,0},{128,64},{192,128},{1,193},{65,1},{129,65},{193,129... | collective-permute-start | bytes 12296 | tf_op jit(solution)/shard_map/ppermute | solution.py:483
  68.3 4.0 %collective-permute-start.11 = (f32[8,128]{1,0:T(8,128)S(1)}, f32[8,128]{1,0:T(8,128)S(1)}, u32[]{:S(2)}, u32[]{:S(2)}) collective-permute-start(f32[8,128]{1,0:T(8,128)S(1)} %fold.1.s0), channel_id=1, source_target_pairs={{0,128},{64,192},{128,0},{192,64},{1,129},{65,193},{129,1},{193,65... | collective-permute-start | bytes 12296 | tf_op jit(solution)/shard_map/ppermute | solution.py:483
  70.8 3.7 %collective-permute-start.10 = (f32[8,128]{1,0:T(8,128)S(1)}, f32[8,128]{1,0:T(8,128)S(1)}, u32[]{:S(2)}, u32[]{:S(2)}) collective-permute-start(f32[8,128]{1,0:T(8,128)S(1)} %fold.1.s0), channel_id=1, source_target_pairs={{0,64},{64,128},{128,192},{192,0},{1,65},{65,129},{129,193},{193,1... | collective-permute-start | bytes 12296 | tf_op jit(solution)/shard_map/ppermute | solution.py:483

commit v8 on v7

--- a/solution.py
+++ b/solution.py
@@ -432,11 +432,18 @@
             back[16 * index : 16 * index + 16, :] = ref[elem]
 
 
-def final_kernel(s0, s1, s2, s3, rhs, b0, b1, b2, b3, order, solution, residual, precond):
-    backs = (b0, b3, b2, b1)
-    z, w, s, t, u = (
-        jnp.concatenate([b[16 * index : 16 * index + 16, :] for b in backs], axis=1) for index in range(5)
-    )
+def place_kernel(b0, b1, b2, b3, order, placed):
+    vectors = jnp.concatenate([b[...] for b in (b0, b3, b2, b1)], axis=1)
+    moved = matmul(jnp.concatenate(bf16_parts(vectors, 3), axis=0), order[...])
+    value = (moved[0:80] + moved[80:160]) + moved[160:240]
+    for index in range(5):
+        for q in range(4):
+            start = 64 * index + 16 * q
+            placed[start : start + 16, :] = value[16 * index : 16 * index + 16, 128 * q : 128 * q + 128]
+
+
+def final_kernel(s0, s1, s2, s3, rhs, placed, solution, residual, precond):
+    z, w, s, t, u = (placed[64 * index : 64 * index + 64, :] for index in range(5))
     total = ((s0[...] + s1[...]) + (s2[...] + s3[...]))[0:1]
     totals = [jnp.sum(total[:, 32 * k : 32 * k + 32], axis=1, keepdims=True) for k in range(4)]
     rho, curve, second, third = totals
@@ -447,17 +454,9 @@
     alpha_next = rho_next / curve_next
     first = alpha + alpha_next * grown
     other = alpha_next * alpha
-    combos = [first * z - other * s, other * t - first * w, z - first * s + other * u]
-    parts = [part for combo in combos for part in bf16_parts(combo, 3)]
-    moved = matmul(jnp.concatenate(parts, axis=0), order[...])
-    for index, ref in enumerate((solution, residual, precond)):
-        rows = moved[48 * index : 48 * index + 48]
-        value = (rows[0:16] + rows[16:32]) + rows[32:48]
-        for q in range(4):
-            part = value[:, 128 * q : 128 * q + 128]
-            if index == 1:
-                part = part + rhs[16 * q : 16 * q + 16, :]
-            ref[16 * q : 16 * q + 16, :] = part
+    solution[...] = first * z - other * s
+    residual[...] = rhs[...] + (other * t - first * w)
+    precond[...] = z - first * s + other * u
 
 
 FACE = jax.ShapeDtypeStruct((16, 128), f32)
@@ -565,7 +564,8 @@
     returned = [backs[0]] + [around(backs[d], d) for d in (1, 2, 3)]
     (total,) = kernel(fold_kernel, [rows], [jax.ShapeDtypeStruct((8, 128), f32)], "fold")
     totals = [total] + [around(total, d) for d in (1, 2, 3)]
-    outs = kernel(final_kernel, [*totals, rhs_here, *returned, order], [shape] * 3, "final")
+    (placed,) = kernel(place_kernel, [*returned, order], [jax.ShapeDtypeStruct((320, 128), f32)], "place")
+    outs = kernel(final_kernel, [*totals, rhs_here, placed], [shape] * 3, "final")
     return tuple(out[None] for out in outs)
 
 

time: 75.7 us -> 75.5 us (level)
    pallas_call x13 -> x14, Pallas kernels: 15.3 us -> 15.4 us  [kernel(): pl.pallas_call(body, out_shape=outs, in_specs=spec if isinstance(spec, li...]
where the time goes in v8:
time: 75.5 us; the launch traced here: 75.3 us
  starting transfers between devices  43.3 us (57%)
  waiting for transfers between devices  15.7 us (21%)
  Pallas kernels  15.4 us (20%)
  between operations  0.82 us (1%)
    ppermute x12, starting transfers between devices, around(): lax.ppermute(value, 'field', [(i, (i + distance) % count) for i in range(...  17.1 us
    pallas_call x14, Pallas kernels, kernel(): pl.pallas_call(body, out_shape=outs, in_specs=spec if isinstance(spec, li...  15.4 us
    ppermute x4, starting transfers between devices, exchange(): lax.ppermute(faces, ('field', 'cross'), column_swaps(first))  13.3 us
    all_to_all x1, starting transfers between devices, local(): rows = lax.all_to_all(rows.reshape(count, 1, 128), 'cross', 0, 0)  13 us
    ppermute x12, waiting for transfers between devices, around(): lax.ppermute(value, 'field', [(i, (i + distance) % count) for i in range(...  10.9 us
    all_to_all x1, waiting for transfers between devices, local(): rows = lax.all_to_all(rows.reshape(count, 1, 128), 'cross', 0, 0)  4.49 us
  transfers between devices with their start and end apart: 17, of which 7 were waited for; matrix products, arithmetic and copies ran while one was open for 0% of the time, Pallas kernels for 12%

profile of v8, /device:TPU:1, one launch (start us, length us, event | category | flops | bytes accessed | tf_op | source)
XLA Modules:
  0.0 75.3 jit_solution(7091792117072794402)
XLA Ops:
  0.6 2.8 %pack_first.1 = (bf16[1584,128]{1,0:T(8,128)(2,1)S(1)}, bf16[1584,128]{1,0:T(8,128)(2,1)S(1)}, bf16[1584,128]{1,0:T(8,128)(2,1)S(1)}, bf16[1584,128]{1,0:T(8,128...) custom-call(s32[4,128]{1,0:T(4,128)} %bitcast.14, f32[64,128]{1,0:T(8,128)} %bitcast.13, ...), custom_call_target="tpu_custom_call" | custom-call | tf_op jit(solution)/shard_map/pack_first/pallas_call | solution.py:469
  3.5 2.1 %collective-permute-start = (bf16[1584,128]{1,0:T(8,128)(2,1)S(1)}, bf16[1584,128]{1,0:T(8,128)(2,1)S(1)}, u32[]{:S(2)}, u32[]{:S(2)}) collective-permute-start(bf16[1584,128]{1,0:T(8,128)(2,1)S(1)} %get-tuple-element.42), channel_id=1, source_target_pairs={{0,64},{64,128},{128,192},{192,0},{1,65},{65,129},{129,193},{193,1... | collective-permute-start | bytes 1216520 | tf_op jit(solution)/shard_map/ppermute | solution.py:482
  5.6 1.4 %collective-permute-start.1 = (bf16[1584,128]{1,0:T(8,128)(2,1)S(1)}, bf16[1584,128]{1,0:T(8,128)(2,1)S(1)}, u32[]{:S(2)}, u32[]{:S(2)}) collective-permute-start(bf16[1584,128]{1,0:T(8,128)(2,1)S(1)} %get-tuple-element.45), channel_id=1, source_target_pairs={{0,192},{64,0},{128,64},{192,128},{1,193},{65,1},{129,65},{193,129... | collective-permute-start | bytes 1216520 | tf_op jit(solution)/shard_map/ppermute | solution.py:482
  6.9 1.6 %collective-permute-start.2 = (bf16[1584,128]{1,0:T(8,128)(2,1)S(1)}, bf16[1584,128]{1,0:T(8,128)(2,1)S(1)}, u32[]{:S(2)}, u32[]{:S(2)}) collective-permute-start(bf16[1584,128]{1,0:T(8,128)(2,1)S(1)} %get-tuple-element.48), channel_id=1, source_target_pairs={{0,128},{64,192},{128,0},{192,64},{1,129},{65,193},{129,1},{193,65... | collective-permute-start | bytes 1216520 | tf_op jit(solution)/shard_map/ppermute | solution.py:482
  8.6 5.1 %collective-permute-done.chunk = bf16[1584,128]{1,0:T(8,128)(2,1)S(1)} collective-permute-done((bf16[1584,128]{1,0:T(8,128)(2,1)S(1)}, bf16[1584,128]{1,0:T(8,128)(2,1)S(1)}, u32[]{:S(2)}, u32[]{:S(2)}) %collective-permute-start) | collective-permute-done | bytes 405536 | tf_op jit(solution)/shard_map/ppermute | solution.py:482
  14.2 1.9 %pack_second.1 = (bf16[528,128]{1,0:T(8,128)(2,1)S(1)}, bf16[528,128]{1,0:T(8,128)(2,1)S(1)}, bf16[528,128]{1,0:T(8,128)(2,1)S(1)}, bf16[528,128]{1,0:T(8,128)(2...) custom-call(bf16[64,64,128]{2,1,0:T(8,128)(2,1)} %bitcast.12, s32[4,128]{1,0:T(4,128)} %bitcast.15, ...), custom_call_target="tpu_custom_call" | custom-call | tf_op jit(solution)/shard_map/pack_second/pallas_call | solution.py:469
  16.0 1.9 %collective-permute-start.3 = (bf16[528,128]{1,0:T(8,128)(2,1)S(1)}, bf16[528,128]{1,0:T(8,128)(2,1)S(1)}, u32[]{:S(2)}, u32[]{:S(2)}) collective-permute-start(bf16[528,128]{1,0:T(8,128)(2,1)S(1)} %get-tuple-element.52), channel_id=1, source_target_pairs={{0,64},{64,128},{128,192},{192,0},{1,65},{65,129},{129,193},{193,1... | collective-permute-start | bytes 405512 | tf_op jit(solution)/shard_map/ppermute | solution.py:482
  18.0 2.8 %collective-permute-start.4 = (bf16[528,128]{1,0:T(8,128)(2,1)S(1)}, bf16[528,128]{1,0:T(8,128)(2,1)S(1)}, u32[]{:S(2)}, u32[]{:S(2)}) collective-permute-start(bf16[528,128]{1,0:T(8,128)(2,1)S(1)} %get-tuple-element.53), channel_id=1, source_target_pairs={{0,128},{64,192},{128,0},{192,64},{1,129},{65,193},{129,1},{193,65... | collective-permute-start | bytes 405512 | tf_op jit(solution)/shard_map/ppermute | solution.py:482
  20.7 1.4 %collective-permute-start.5 = (bf16[528,128]{1,0:T(8,128)(2,1)S(1)}, bf16[528,128]{1,0:T(8,128)(2,1)S(1)}, u32[]{:S(2)}, u32[]{:S(2)}) collective-permute-start(bf16[528,128]{1,0:T(8,128)(2,1)S(1)} %get-tuple-element.54), channel_id=1, source_target_pairs={{0,192},{64,0},{128,64},{192,128},{1,193},{65,1},{129,65},{193,129... | collective-permute-start | bytes 405512 | tf_op jit(solution)/shard_map/ppermute | solution.py:482
  23.1 2.4 %collective-permute-done.2.chunk = bf16[1584,128]{1,0:T(8,128)(2,1)S(1)} collective-permute-done((bf16[1584,128]{1,0:T(8,128)(2,1)S(1)}, bf16[1584,128]{1,0:T(8,128)(2,1)S(1)}, u32[]{:S(2)}, u32[]{:S(2)}) %collective-permute-start.2) | collective-permute-done | bytes 405536 | tf_op jit(solution)/shard_map/ppermute | solution.py:482
  25.6 2.1 %solve_first.1 = (bf16[4,2048,128]{2,1,0:T(8,128)(2,1)S(1)}, f32[4,16,128]{2,1,0:T(8,128)S(1)}, f32[4,16,128]{2,1,0:T(8,128)S(1)}, f32[16,128]{1,0:T(8,128)S(1)}, f32[16,128]{1,0:T(8,128)S(1)}) custom-call(bf16[2048,128]{1,0:T(8,128)(2,1)S(1)} %get-tuple-element.40.b0, f32[16,128]{1,0:T(8,128)S(1)} %get-tuple-element.41.r0, ...), custom_call_target="tpu_custom_call" | custom-call | tf_op jit(solution)/shard_map/solve_first/pallas_call | solution.py:469
  28.1 7.3 %collective-permute-start.7 = (f32[16,128]{1,0:T(8,128)S(1)}, f32[16,128]{1,0:T(8,128)S(1)}, u32[]{:S(2)}, u32[]{:S(2)}) collective-permute-start(f32[16,128]{1,0:T(8,128)S(1)} %get-tuple-element.58), channel_id=1, source_target_pairs={{64,128},{192,193},{129,65},{1,2},{66,130},{194,195},{131,67},{3,4... | collective-permute-start | bytes 24584 | tf_op jit(solution)/shard_map/ppermute | solution.py:496
  35.4 1.1 %apply_first.1.partial = f32[4,16,128]{2,1,0:T(8,128)S(1)} custom-call(bf16[4,2048,128]{2,1,0:T(8,128)(2,1)S(1)} %get-tuple-element.49.blocks, bf16[528,128]{1,0:T(8,128)(2,1)S(1)} %get-tuple-element.51.p0, bf16[528,128]{1,0:T(8,128)(2,1)S(1)} %collective-permute-done.3.p1, bf16[528,128]{1,0:T(8,128)(2,1)S(1)} %collective-permute-done.4.p2, ...), custom_call_target="tpu_custom_call" | custom-call | tf_op jit(solution)/shard_map/apply_first/pallas_call | solution.py:469
  36.7 1.6 %solve_second.1 = (f32[4,16,128]{2,1,0:T(8,128)S(1)}, f32[4,16,128]{2,1,0:T(8,128)S(1)}, f32[16,128]{1,0:T(8,128)S(1)}, f32[16,128]{1,0:T(8,128)S(1)}) custom-call(bf16[4,2048,128]{2,1,0:T(8,128)(2,1)S(1)} %get-tuple-element.49.blocks, f32[4,16,128]{2,1,0:T(8,128)S(1)} %apply_first.1.partial, f32[16,128]{1,0:T(8,128)S(1)} %collective-permute-done.6.inner, ...), custom_call_target="tpu_custom_call" | custom-call | tf_op jit(solution)/shard_map/solve_second/pallas_call | solution.py:469
  38.5 5.3 %collective-permute-start.9 = (f32[16,128]{1,0:T(8,128)S(1)}, f32[16,128]{1,0:T(8,128)S(1)}, u32[]{:S(2)}, u32[]{:S(2)}) collective-permute-start(f32[16,128]{1,0:T(8,128)S(1)} %get-tuple-element.61), channel_id=1, source_target_pairs={{64,128},{192,193},{129,65},{1,2},{66,130},{194,195},{131,67},{3,4... | collective-permute-start | bytes 24584 | tf_op jit(solution)/shard_map/ppermute | solution.py:496
  43.8 1.1 %apply_second.1.partial = f32[4,16,128]{2,1,0:T(8,128)S(1)} custom-call(bf16[4,2048,128]{2,1,0:T(8,128)(2,1)S(1)} %get-tuple-element.49.blocks, bf16[528,128]{1,0:T(8,128)(2,1)S(1)} %get-tuple-element.51.p0, bf16[528,128]{1,0:T(8,128)(2,1)S(1)} %collective-permute-done.3.p1, bf16[528,128]{1,0:T(8,128)(2,1)S(1)} %collective-permute-done.4.p2, ...), custom_call_target="tpu_custom_call" | custom-call | tf_op jit(solution)/shard_map/apply_second/pallas_call | solution.py:469
  45.9 13.0 %all-to-all-start = ((f32[64,1,128]{2,1,0:T(1,128)}), f32[64,1,128]{2,1,0:T(1,128)S(1)}, u32[]{:S(2)}, u32[]{:S(2)}) async-start(f32[64,1,128]{2,1,0:T(1,128)} %bitcast.6), calls=%async_computation | async-start | bytes 65536 | tf_op jit(solution)/shard_map/all_to_all | solution.py:560
  59.0 1.4 %solve_last.1 = (f32[80,128]{1,0:T(8,128)S(1)}, f32[80,128]{1,0:T(8,128)S(1)}, f32[80,128]{1,0:T(8,128)S(1)}, f32[80,128]{1,0:T(8,128)S(1)}) custom-call(bf16[4,2048,128]{2,1,0:T(8,128)(2,1)S(1)} %get-tuple-element.49.blocks, f32[4,16,128]{2,1,0:T(8,128)S(1)} %get-tuple-element.55.vector.z, f32[4,16,128]{2,1,0:T(8,128)S(1)} %get-tuple-element.63.w, ...), custom_call_target="tpu_custom_call" | custom-call | tf_op jit(solution)/shard_map/solve_last/pallas_call | solution.py:469
  61.7 2.0 %collective-permute-start.15 = (f32[80,128]{1,0:T(8,128)S(1)}, f32[80,128]{1,0:T(8,128)S(1)}, u32[]{:S(2)}, u32[]{:S(2)}) collective-permute-start(f32[80,128]{1,0:T(8,128)S(1)} %get-tuple-element.70), channel_id=1, source_target_pairs={{0,192},{64,0},{128,64},{192,128},{1,193},{65,1},{129,65},{193,129... | collective-permute-start | bytes 122888 | tf_op jit(solution)/shard_map/ppermute | solution.py:482
  63.7 4.5 %all-to-all-done.rows = f32[64,1,128]{2,1,0:T(1,128)S(1)} async-done(((f32[64,1,128]{2,1,0:T(1,128)}), f32[64,1,128]{2,1,0:T(1,128)S(1)}, u32[]{:S(2)}, u32[]{:S(2)}) %all-to-all-start) | async-done | bytes 32800 | tf_op jit(solution)/shard_map/all_to_all | solution.py:560
  68.3 2.4 %collective-permute-start.11 = (f32[8,128]{1,0:T(8,128)S(1)}, f32[8,128]{1,0:T(8,128)S(1)}, u32[]{:S(2)}, u32[]{:S(2)}) collective-permute-start(f32[8,128]{1,0:T(8,128)S(1)} %fold.1.s0), channel_id=1, source_target_pairs={{0,128},{64,192},{128,0},{192,64},{1,129},{65,193},{129,1},{193,65... | collective-permute-start | bytes 12296 | tf_op jit(solution)/shard_map/ppermute | solution.py:482
  71.1 1.3 %collective-permute-done.11.s2 = f32[8,128]{1,0:T(8,128)S(1)} collective-permute-done((f32[8,128]{1,0:T(8,128)S(1)}, f32[8,128]{1,0:T(8,128)S(1)}, u32[]{:S(2)}, u32[]{:S(2)}) %collective-permute-start.11) | collective-permute-done | bytes 4128 | tf_op jit(solution)/shard_map/ppermute | solution.py:482
  72.4 2.1 %collective-permute-done.10.s1 = f32[8,128]{1,0:T(8,128)S(1)} collective-permute-done((f32[8,128]{1,0:T(8,128)S(1)}, f32[8,128]{1,0:T(8,128)S(1)}, u32[]{:S(2)}, u32[]{:S(2)}) %collective-permute-start.10) | collective-permute-done | bytes 4128 | tf_op jit(solution)/shard_map/ppermute | solution.py:482
  74.4 0.8 %final.1 = (f32[64,128]{1,0:T(8,128)}, f32[64,128]{1,0:T(8,128)}, f32[64,128]{1,0:T(8,128)}) custom-call(f32[8,128]{1,0:T(8,128)S(1)} %fold.1.s0, f32[8,128]{1,0:T(8,128)S(1)} %collective-permute-done.10.s1, f32[8,128]{1,0:T(8,128)S(1)} %collective-permute-done.11.s2, f32[8,128]{1,0:T(8,128)S(1)} %collective-permute-done.12.s3, ...), custom_call_target="tpu_custom_call" | custom-call | tf_op jit(solution)/shard_map/final/pallas_call | solution.py:469
  (24 shorter events, 5.1 us)
Async XLA Ops:
  3.5 10.2 %collective-permute-start = (bf16[1584,128]{1,0:T(8,128)(2,1)S(1)}, bf16[1584,128]{1,0:T(8,128)(2,1)S(1)}, u32[]{:S(2)}, u32[]{:S(2)}) collective-permute-start(bf16[1584,128]{1,0:T(8,128)(2,1)S(1)} %get-tuple-element.42), channel_id=1, source_target_pairs={{0,64},{64,128},{128,192},{192,0},{1,65},{65,129},{129,193},{193,1... | collective-permute-start | bytes 1216520 | tf_op jit(solution)/shard_map/ppermute | solution.py:482
  5.6 17.1 %collective-permute-start.1 = (bf16[1584,128]{1,0:T(8,128)(2,1)S(1)}, bf16[1584,128]{1,0:T(8,128)(2,1)S(1)}, u32[]{:S(2)}, u32[]{:S(2)}) collective-permute-start(bf16[1584,128]{1,0:T(8,128)(2,1)S(1)} %get-tuple-element.45), channel_id=1, source_target_pairs={{0,192},{64,0},{128,64},{192,128},{1,193},{65,1},{129,65},{193,129... | collective-permute-start | bytes 1216520 | tf_op jit(solution)/shard_map/ppermute | solution.py:482
  6.9 18.6 %collective-permute-start.2 = (bf16[1584,128]{1,0:T(8,128)(2,1)S(1)}, bf16[1584,128]{1,0:T(8,128)(2,1)S(1)}, u32[]{:S(2)}, u32[]{:S(2)}) collective-permute-start(bf16[1584,128]{1,0:T(8,128)(2,1)S(1)} %get-tuple-element.48), channel_id=1, source_target_pairs={{0,128},{64,192},{128,0},{192,64},{1,129},{65,193},{129,1},{193,65... | collective-permute-start | bytes 1216520 | tf_op jit(solution)/shard_map/ppermute | solution.py:482
  16.0 19.3 %collective-permute-start.3 = (bf16[528,128]{1,0:T(8,128)(2,1)S(1)}, bf16[528,128]{1,0:T(8,128)(2,1)S(1)}, u32[]{:S(2)}, u32[]{:S(2)}) collective-permute-start(bf16[528,128]{1,0:T(8,128)(2,1)S(1)} %get-tuple-element.52), channel_id=1, source_target_pairs={{0,64},{64,128},{128,192},{192,0},{1,65},{65,129},{129,193},{193,1... | collective-permute-start | bytes 405512 | tf_op jit(solution)/shard_map/ppermute | solution.py:482
  18.0 17.4 %collective-permute-start.4 = (bf16[528,128]{1,0:T(8,128)(2,1)S(1)}, bf16[528,128]{1,0:T(8,128)(2,1)S(1)}, u32[]{:S(2)}, u32[]{:S(2)}) collective-permute-start(bf16[528,128]{1,0:T(8,128)(2,1)S(1)} %get-tuple-element.53), channel_id=1, source_target_pairs={{0,128},{64,192},{128,0},{192,64},{1,129},{65,193},{129,1},{193,65... | collective-permute-start | bytes 405512 | tf_op jit(solution)/shard_map/ppermute | solution.py:482
  20.7 14.7 %collective-permute-start.5 = (bf16[528,128]{1,0:T(8,128)(2,1)S(1)}, bf16[528,128]{1,0:T(8,128)(2,1)S(1)}, u32[]{:S(2)}, u32[]{:S(2)}) collective-permute-start(bf16[528,128]{1,0:T(8,128)(2,1)S(1)} %get-tuple-element.54), channel_id=1, source_target_pairs={{0,192},{64,0},{128,64},{192,128},{1,193},{65,1},{129,65},{193,129... | collective-permute-start | bytes 405512 | tf_op jit(solution)/shard_map/ppermute | solution.py:482
  27.7 8.8 %collective-permute-start.6 = (f32[16,128]{1,0:T(8,128)S(1)}, f32[16,128]{1,0:T(8,128)S(1)}, u32[]{:S(2)}, u32[]{:S(2)}) collective-permute-start(f32[16,128]{1,0:T(8,128)S(1)} %get-tuple-element.57), channel_id=1, source_target_pairs={{0,64},{128,192},{193,129},{65,1},{2,66},{130,194},{195,131},{67,3... | collective-permute-start | bytes 24584 | tf_op jit(solution)/shard_map/ppermute | solution.py:496
  28.1 8.6 %collective-permute-start.7 = (f32[16,128]{1,0:T(8,128)S(1)}, f32[16,128]{1,0:T(8,128)S(1)}, u32[]{:S(2)}, u32[]{:S(2)}) collective-permute-start(f32[16,128]{1,0:T(8,128)S(1)} %get-tuple-element.58), channel_id=1, source_target_pairs={{64,128},{192,193},{129,65},{1,2},{66,130},{194,195},{131,67},{3,4... | collective-permute-start | bytes 24584 | tf_op jit(solution)/shard_map/ppermute | solution.py:496
  38.2 6.7 %collective-permute-start.8 = (f32[16,128]{1,0:T(8,128)S(1)}, f32[16,128]{1,0:T(8,128)S(1)}, u32[]{:S(2)}, u32[]{:S(2)}) collective-permute-start(f32[16,128]{1,0:T(8,128)S(1)} %get-tuple-element.60), channel_id=1, source_target_pairs={{0,64},{128,192},{193,129},{65,1},{2,66},{130,194},{195,131},{67,3... | collective-permute-start | bytes 24584 | tf_op jit(solution)/shard_map/ppermute | solution.py:496
  38.5 6.6 %collective-permute-start.9 = (f32[16,128]{1,0:T(8,128)S(1)}, f32[16,128]{1,0:T(8,128)S(1)}, u32[]{:S(2)}, u32[]{:S(2)}) collective-permute-start(f32[16,128]{1,0:T(8,128)S(1)} %get-tuple-element.61), channel_id=1, source_target_pairs={{64,128},{192,193},{129,65},{1,2},{66,130},{194,195},{131,67},{3,4... | collective-permute-start | bytes 24584 | tf_op jit(solution)/shard_map/ppermute | solution.py:496
  45.9 22.3 %all-to-all-start = ((f32[64,1,128]{2,1,0:T(1,128)}), f32[64,1,128]{2,1,0:T(1,128)S(1)}, u32[]{:S(2)}, u32[]{:S(2)}) async-start(f32[64,1,128]{2,1,0:T(1,128)} %bitcast.6), calls=%async_computation | async-start | bytes 65536 | tf_op jit(solution)/shard_map/all_to_all | solution.py:560
  60.4 10.4 %collective-permute-start.13 = (f32[80,128]{1,0:T(8,128)S(1)}, f32[80,128]{1,0:T(8,128)S(1)}, u32[]{:S(2)}, u32[]{:S(2)}) collective-permute-start(f32[80,128]{1,0:T(8,128)S(1)} %get-tuple-element.68), channel_id=1, source_target_pairs={{0,64},{64,128},{128,192},{192,0},{1,65},{65,129},{129,193},{193,1... | collective-permute-start | bytes 122888 | tf_op jit(solution)/shard_map/ppermute | solution.py:482
  61.1 9.7 %collective-permute-start.14 = (f32[80,128]{1,0:T(8,128)S(1)}, f32[80,128]{1,0:T(8,128)S(1)}, u32[]{:S(2)}, u32[]{:S(2)}) collective-permute-start(f32[80,128]{1,0:T(8,128)S(1)} %get-tuple-element.69), channel_id=1, source_target_pairs={{0,128},{64,192},{128,0},{192,64},{1,129},{65,193},{129,1},{193,65... | collective-permute-start | bytes 122888 | tf_op jit(solution)/shard_map/ppermute | solution.py:482
  61.7 9.1 %collective-permute-start.15 = (f32[80,128]{1,0:T(8,128)S(1)}, f32[80,128]{1,0:T(8,128)S(1)}, u32[]{:S(2)}, u32[]{:S(2)}) collective-permute-start(f32[80,128]{1,0:T(8,128)S(1)} %get-tuple-element.70), channel_id=1, source_target_pairs={{0,192},{64,0},{128,64},{192,128},{1,193},{65,1},{129,65},{193,129... | collective-permute-start | bytes 122888 | tf_op jit(solution)/shard_map/ppermute | solution.py:482
  68.3 2.8 %collective-permute-start.12 = (f32[8,128]{1,0:T(8,128)S(1)}, f32[8,128]{1,0:T(8,128)S(1)}, u32[]{:S(2)}, u32[]{:S(2)}) collective-permute-start(f32[8,128]{1,0:T(8,128)S(1)} %fold.1.s0), channel_id=1, source_target_pairs={{0,192},{64,0},{128,64},{192,128},{1,193},{65,1},{129,65},{193,129... | collective-permute-start | bytes 12296 | tf_op jit(solution)/shard_map/ppermute | solution.py:482
  68.3 4.0 %collective-permute-start.11 = (f32[8,128]{1,0:T(8,128)S(1)}, f32[8,128]{1,0:T(8,128)S(1)}, u32[]{:S(2)}, u32[]{:S(2)}) collective-permute-start(f32[8,128]{1,0:T(8,128)S(1)} %fold.1.s0), channel_id=1, source_target_pairs={{0,128},{64,192},{128,0},{192,64},{1,129},{65,193},{129,1},{193,65... | collective-permute-start | bytes 12296 | tf_op jit(solution)/shard_map/ppermute | solution.py:482
  70.8 3.7 %collective-permute-start.10 = (f32[8,128]{1,0:T(8,128)S(1)}, f32[8,128]{1,0:T(8,128)S(1)}, u32[]{:S(2)}, u32[]{:S(2)}) collective-permute-start(f32[8,128]{1,0:T(8,128)S(1)} %fold.1.s0), channel_id=1, source_target_pairs={{0,64},{64,128},{128,192},{192,0},{1,65},{65,129},{129,193},{193,1... | collective-permute-start | bytes 12296 | tf_op jit(solution)/shard_map/ppermute | solution.py:482

commit v9 on v8

--- a/solution.py
+++ b/solution.py
@@ -114,12 +114,16 @@
     once = matmul(ones, across)
     twice = matmul(once.astype(bf16), across)
     column = once + twice + matmul(twice.astype(bf16), across)
-    jump = step_down(2)
-    row = matmul(ones, jump)
-    for turn in range(5):
-        row = row + matmul(row.astype(bf16), jump)
-        if turn < 4:
-            jump = matmul(jump, jump).astype(bf16)
+    steps = []
+    for face in (2, 3):
+        jump = step_down(face)
+        row = matmul(ones, jump)
+        for turn in range(4):
+            row = row + matmul(row.astype(bf16), jump)
+            if turn < 3:
+                jump = matmul(jump, jump).astype(bf16)
+        steps.append(row)
+    row = jnp.where(steps[0] < 16.0, steps[0], 31.0 - steps[1])
     owner = jnp.where(cross % 2 == 0, column, 3.0 - column)
     position = (owner * 32.0 + row).astype(jnp.int32)[0:1]
 

time: 75.5 us -> 75.7 us (level)
  no operation moved by 1% of the time
where the time goes in v9:
time: 75.7 us; the launch traced here: 75.5 us
  starting transfers between devices  43.4 us (57%)
  waiting for transfers between devices  15.7 us (21%)
  Pallas kernels  15.6 us (21%)
  between operations  0.82 us (1%)
    ppermute x12, starting transfers between devices, around(): lax.ppermute(value, 'field', [(i, (i + distance) % count) for i in range(...  17 us
    pallas_call x14, Pallas kernels, kernel(): pl.pallas_call(body, out_shape=outs, in_specs=spec if isinstance(spec, li...  15.6 us
    ppermute x4, starting transfers between devices, exchange(): lax.ppermute(faces, ('field', 'cross'), column_swaps(first))  13.2 us
    all_to_all x1, starting transfers between devices, local(): rows = lax.all_to_all(rows.reshape(count, 1, 128), 'cross', 0, 0)  13.1 us
    ppermute x12, waiting for transfers between devices, around(): lax.ppermute(value, 'field', [(i, (i + distance) % count) for i in range(...  10.8 us
    all_to_all x1, waiting for transfers between devices, local(): rows = lax.all_to_all(rows.reshape(count, 1, 128), 'cross', 0, 0)  4.49 us
  transfers between devices with their start and end apart: 17, of which 7 were waited for; matrix products, arithmetic and copies ran while one was open for 0% of the time, Pallas kernels for 12%

profile of v9, /device:TPU:1, one launch (start us, length us, event | category | flops | bytes accessed | tf_op | source)
XLA Modules:
  0.0 75.5 jit_solution(12949521210395952303)
XLA Ops:
  0.6 3.1 %pack_first.1 = (bf16[1584,128]{1,0:T(8,128)(2,1)S(1)}, bf16[1584,128]{1,0:T(8,128)(2,1)S(1)}, bf16[1584,128]{1,0:T(8,128)(2,1)S(1)}, bf16[1584,128]{1,0:T(8,128...) custom-call(s32[4,128]{1,0:T(4,128)} %bitcast.14, f32[64,128]{1,0:T(8,128)} %bitcast.13, ...), custom_call_target="tpu_custom_call" | custom-call | tf_op jit(solution)/shard_map/pack_first/pallas_call | solution.py:473
  3.7 2.1 %collective-permute-start = (bf16[1584,128]{1,0:T(8,128)(2,1)S(1)}, bf16[1584,128]{1,0:T(8,128)(2,1)S(1)}, u32[]{:S(2)}, u32[]{:S(2)}) collective-permute-start(bf16[1584,128]{1,0:T(8,128)(2,1)S(1)} %get-tuple-element.42), channel_id=1, source_target_pairs={{0,64},{64,128},{128,192},{192,0},{1,65},{65,129},{129,193},{193,1... | collective-permute-start | bytes 1216520 | tf_op jit(solution)/shard_map/ppermute | solution.py:486
  5.8 1.3 %collective-permute-start.1 = (bf16[1584,128]{1,0:T(8,128)(2,1)S(1)}, bf16[1584,128]{1,0:T(8,128)(2,1)S(1)}, u32[]{:S(2)}, u32[]{:S(2)}) collective-permute-start(bf16[1584,128]{1,0:T(8,128)(2,1)S(1)} %get-tuple-element.45), channel_id=1, source_target_pairs={{0,192},{64,0},{128,64},{192,128},{1,193},{65,1},{129,65},{193,129... | collective-permute-start | bytes 1216520 | tf_op jit(solution)/shard_map/ppermute | solution.py:486
  7.2 1.6 %collective-permute-start.2 = (bf16[1584,128]{1,0:T(8,128)(2,1)S(1)}, bf16[1584,128]{1,0:T(8,128)(2,1)S(1)}, u32[]{:S(2)}, u32[]{:S(2)}) collective-permute-start(bf16[1584,128]{1,0:T(8,128)(2,1)S(1)} %get-tuple-element.48), channel_id=1, source_target_pairs={{0,128},{64,192},{128,0},{192,64},{1,129},{65,193},{129,1},{193,65... | collective-permute-start | bytes 1216520 | tf_op jit(solution)/shard_map/ppermute | solution.py:486
  8.8 5.1 %collective-permute-done.chunk = bf16[1584,128]{1,0:T(8,128)(2,1)S(1)} collective-permute-done((bf16[1584,128]{1,0:T(8,128)(2,1)S(1)}, bf16[1584,128]{1,0:T(8,128)(2,1)S(1)}, u32[]{:S(2)}, u32[]{:S(2)}) %collective-permute-start) | collective-permute-done | bytes 405536 | tf_op jit(solution)/shard_map/ppermute | solution.py:486
  14.4 1.9 %pack_second.1 = (bf16[528,128]{1,0:T(8,128)(2,1)S(1)}, bf16[528,128]{1,0:T(8,128)(2,1)S(1)}, bf16[528,128]{1,0:T(8,128)(2,1)S(1)}, bf16[528,128]{1,0:T(8,128)(2...) custom-call(bf16[64,64,128]{2,1,0:T(8,128)(2,1)} %bitcast.12, s32[4,128]{1,0:T(4,128)} %bitcast.15, ...), custom_call_target="tpu_custom_call" | custom-call | tf_op jit(solution)/shard_map/pack_second/pallas_call | solution.py:473
  16.3 2.0 %collective-permute-start.3 = (bf16[528,128]{1,0:T(8,128)(2,1)S(1)}, bf16[528,128]{1,0:T(8,128)(2,1)S(1)}, u32[]{:S(2)}, u32[]{:S(2)}) collective-permute-start(bf16[528,128]{1,0:T(8,128)(2,1)S(1)} %get-tuple-element.52), channel_id=1, source_target_pairs={{0,64},{64,128},{128,192},{192,0},{1,65},{65,129},{129,193},{193,1... | collective-permute-start | bytes 405512 | tf_op jit(solution)/shard_map/ppermute | solution.py:486
  18.3 2.7 %collective-permute-start.4 = (bf16[528,128]{1,0:T(8,128)(2,1)S(1)}, bf16[528,128]{1,0:T(8,128)(2,1)S(1)}, u32[]{:S(2)}, u32[]{:S(2)}) collective-permute-start(bf16[528,128]{1,0:T(8,128)(2,1)S(1)} %get-tuple-element.53), channel_id=1, source_target_pairs={{0,128},{64,192},{128,0},{192,64},{1,129},{65,193},{129,1},{193,65... | collective-permute-start | bytes 405512 | tf_op jit(solution)/shard_map/ppermute | solution.py:486
  21.0 1.4 %collective-permute-start.5 = (bf16[528,128]{1,0:T(8,128)(2,1)S(1)}, bf16[528,128]{1,0:T(8,128)(2,1)S(1)}, u32[]{:S(2)}, u32[]{:S(2)}) collective-permute-start(bf16[528,128]{1,0:T(8,128)(2,1)S(1)} %get-tuple-element.54), channel_id=1, source_target_pairs={{0,192},{64,0},{128,64},{192,128},{1,193},{65,1},{129,65},{193,129... | collective-permute-start | bytes 405512 | tf_op jit(solution)/shard_map/ppermute | solution.py:486
  23.4 2.4 %collective-permute-done.2.chunk = bf16[1584,128]{1,0:T(8,128)(2,1)S(1)} collective-permute-done((bf16[1584,128]{1,0:T(8,128)(2,1)S(1)}, bf16[1584,128]{1,0:T(8,128)(2,1)S(1)}, u32[]{:S(2)}, u32[]{:S(2)}) %collective-permute-start.2) | collective-permute-done | bytes 405536 | tf_op jit(solution)/shard_map/ppermute | solution.py:486
  25.8 2.1 %solve_first.1 = (bf16[4,2048,128]{2,1,0:T(8,128)(2,1)S(1)}, f32[4,16,128]{2,1,0:T(8,128)S(1)}, f32[4,16,128]{2,1,0:T(8,128)S(1)}, f32[16,128]{1,0:T(8,128)S(1)}, f32[16,128]{1,0:T(8,128)S(1)}) custom-call(bf16[2048,128]{1,0:T(8,128)(2,1)S(1)} %get-tuple-element.40.b0, f32[16,128]{1,0:T(8,128)S(1)} %get-tuple-element.41.r0, ...), custom_call_target="tpu_custom_call" | custom-call | tf_op jit(solution)/shard_map/solve_first/pallas_call | solution.py:473
  28.3 7.3 %collective-permute-start.7 = (f32[16,128]{1,0:T(8,128)S(1)}, f32[16,128]{1,0:T(8,128)S(1)}, u32[]{:S(2)}, u32[]{:S(2)}) collective-permute-start(f32[16,128]{1,0:T(8,128)S(1)} %get-tuple-element.58), channel_id=1, source_target_pairs={{64,128},{192,193},{129,65},{1,2},{66,130},{194,195},{131,67},{3,4... | collective-permute-start | bytes 24584 | tf_op jit(solution)/shard_map/ppermute | solution.py:500
  35.7 1.1 %apply_first.1.partial = f32[4,16,128]{2,1,0:T(8,128)S(1)} custom-call(bf16[4,2048,128]{2,1,0:T(8,128)(2,1)S(1)} %get-tuple-element.49.blocks, bf16[528,128]{1,0:T(8,128)(2,1)S(1)} %get-tuple-element.51.p0, bf16[528,128]{1,0:T(8,128)(2,1)S(1)} %collective-permute-done.3.p1, bf16[528,128]{1,0:T(8,128)(2,1)S(1)} %collective-permute-done.4.p2, ...), custom_call_target="tpu_custom_call" | custom-call | tf_op jit(solution)/shard_map/apply_first/pallas_call | solution.py:473
  37.0 1.6 %solve_second.1 = (f32[4,16,128]{2,1,0:T(8,128)S(1)}, f32[4,16,128]{2,1,0:T(8,128)S(1)}, f32[16,128]{1,0:T(8,128)S(1)}, f32[16,128]{1,0:T(8,128)S(1)}) custom-call(bf16[4,2048,128]{2,1,0:T(8,128)(2,1)S(1)} %get-tuple-element.49.blocks, f32[4,16,128]{2,1,0:T(8,128)S(1)} %apply_first.1.partial, f32[16,128]{1,0:T(8,128)S(1)} %collective-permute-done.6.inner, ...), custom_call_target="tpu_custom_call" | custom-call | tf_op jit(solution)/shard_map/solve_second/pallas_call | solution.py:473
  38.8 5.3 %collective-permute-start.9 = (f32[16,128]{1,0:T(8,128)S(1)}, f32[16,128]{1,0:T(8,128)S(1)}, u32[]{:S(2)}, u32[]{:S(2)}) collective-permute-start(f32[16,128]{1,0:T(8,128)S(1)} %get-tuple-element.61), channel_id=1, source_target_pairs={{64,128},{192,193},{129,65},{1,2},{66,130},{194,195},{131,67},{3,4... | collective-permute-start | bytes 24584 | tf_op jit(solution)/shard_map/ppermute | solution.py:500
  44.0 1.1 %apply_second.1.partial = f32[4,16,128]{2,1,0:T(8,128)S(1)} custom-call(bf16[4,2048,128]{2,1,0:T(8,128)(2,1)S(1)} %get-tuple-element.49.blocks, bf16[528,128]{1,0:T(8,128)(2,1)S(1)} %get-tuple-element.51.p0, bf16[528,128]{1,0:T(8,128)(2,1)S(1)} %collective-permute-done.3.p1, bf16[528,128]{1,0:T(8,128)(2,1)S(1)} %collective-permute-done.4.p2, ...), custom_call_target="tpu_custom_call" | custom-call | tf_op jit(solution)/shard_map/apply_second/pallas_call | solution.py:473
  46.1 13.1 %all-to-all-start = ((f32[64,1,128]{2,1,0:T(1,128)}), f32[64,1,128]{2,1,0:T(1,128)S(1)}, u32[]{:S(2)}, u32[]{:S(2)}) async-start(f32[64,1,128]{2,1,0:T(1,128)} %bitcast.6), calls=%async_computation | async-start | bytes 65536 | tf_op jit(solution)/shard_map/all_to_all | solution.py:564
  59.3 1.4 %solve_last.1 = (f32[80,128]{1,0:T(8,128)S(1)}, f32[80,128]{1,0:T(8,128)S(1)}, f32[80,128]{1,0:T(8,128)S(1)}, f32[80,128]{1,0:T(8,128)S(1)}) custom-call(bf16[4,2048,128]{2,1,0:T(8,128)(2,1)S(1)} %get-tuple-element.49.blocks, f32[4,16,128]{2,1,0:T(8,128)S(1)} %get-tuple-element.55.vector.z, f32[4,16,128]{2,1,0:T(8,128)S(1)} %get-tuple-element.63.w, ...), custom_call_target="tpu_custom_call" | custom-call | tf_op jit(solution)/shard_map/solve_last/pallas_call | solution.py:473
  62.1 2.0 %collective-permute-start.15 = (f32[80,128]{1,0:T(8,128)S(1)}, f32[80,128]{1,0:T(8,128)S(1)}, u32[]{:S(2)}, u32[]{:S(2)}) collective-permute-start(f32[80,128]{1,0:T(8,128)S(1)} %get-tuple-element.70), channel_id=1, source_target_pairs={{0,192},{64,0},{128,64},{192,128},{1,193},{65,1},{129,65},{193,129... | collective-permute-start | bytes 122888 | tf_op jit(solution)/shard_map/ppermute | solution.py:486
  64.0 4.5 %all-to-all-done.rows = f32[64,1,128]{2,1,0:T(1,128)S(1)} async-done(((f32[64,1,128]{2,1,0:T(1,128)}), f32[64,1,128]{2,1,0:T(1,128)S(1)}, u32[]{:S(2)}, u32[]{:S(2)}) %all-to-all-start) | async-done | bytes 32800 | tf_op jit(solution)/shard_map/all_to_all | solution.py:564
  68.7 2.4 %collective-permute-start.11 = (f32[8,128]{1,0:T(8,128)S(1)}, f32[8,128]{1,0:T(8,128)S(1)}, u32[]{:S(2)}, u32[]{:S(2)}) collective-permute-start(f32[8,128]{1,0:T(8,128)S(1)} %fold.1.s0), channel_id=1, source_target_pairs={{0,128},{64,192},{128,0},{192,64},{1,129},{65,193},{129,1},{193,65... | collective-permute-start | bytes 12296 | tf_op jit(solution)/shard_map/ppermute | solution.py:486
  71.4 1.4 %collective-permute-done.11.s2 = f32[8,128]{1,0:T(8,128)S(1)} collective-permute-done((f32[8,128]{1,0:T(8,128)S(1)}, f32[8,128]{1,0:T(8,128)S(1)}, u32[]{:S(2)}, u32[]{:S(2)}) %collective-permute-start.11) | collective-permute-done | bytes 4128 | tf_op jit(solution)/shard_map/ppermute | solution.py:486
  72.7 2.0 %collective-permute-done.10.s1 = f32[8,128]{1,0:T(8,128)S(1)} collective-permute-done((f32[8,128]{1,0:T(8,128)S(1)}, f32[8,128]{1,0:T(8,128)S(1)}, u32[]{:S(2)}, u32[]{:S(2)}) %collective-permute-start.10) | collective-permute-done | bytes 4128 | tf_op jit(solution)/shard_map/ppermute | solution.py:486
  74.7 0.8 %final.1 = (f32[64,128]{1,0:T(8,128)}, f32[64,128]{1,0:T(8,128)}, f32[64,128]{1,0:T(8,128)}) custom-call(f32[8,128]{1,0:T(8,128)S(1)} %fold.1.s0, f32[8,128]{1,0:T(8,128)S(1)} %collective-permute-done.10.s1, f32[8,128]{1,0:T(8,128)S(1)} %collective-permute-done.11.s2, f32[8,128]{1,0:T(8,128)S(1)} %collective-permute-done.12.s3, ...), custom_call_target="tpu_custom_call" | custom-call | tf_op jit(solution)/shard_map/final/pallas_call | solution.py:473
  (24 shorter events, 5.1 us)
Async XLA Ops:
  3.7 10.2 %collective-permute-start = (bf16[1584,128]{1,0:T(8,128)(2,1)S(1)}, bf16[1584,128]{1,0:T(8,128)(2,1)S(1)}, u32[]{:S(2)}, u32[]{:S(2)}) collective-permute-start(bf16[1584,128]{1,0:T(8,128)(2,1)S(1)} %get-tuple-element.42), channel_id=1, source_target_pairs={{0,64},{64,128},{128,192},{192,0},{1,65},{65,129},{129,193},{193,1... | collective-permute-start | bytes 1216520 | tf_op jit(solution)/shard_map/ppermute | solution.py:486
  5.8 17.1 %collective-permute-start.1 = (bf16[1584,128]{1,0:T(8,128)(2,1)S(1)}, bf16[1584,128]{1,0:T(8,128)(2,1)S(1)}, u32[]{:S(2)}, u32[]{:S(2)}) collective-permute-start(bf16[1584,128]{1,0:T(8,128)(2,1)S(1)} %get-tuple-element.45), channel_id=1, source_target_pairs={{0,192},{64,0},{128,64},{192,128},{1,193},{65,1},{129,65},{193,129... | collective-permute-start | bytes 1216520 | tf_op jit(solution)/shard_map/ppermute | solution.py:486
  7.2 18.6 %collective-permute-start.2 = (bf16[1584,128]{1,0:T(8,128)(2,1)S(1)}, bf16[1584,128]{1,0:T(8,128)(2,1)S(1)}, u32[]{:S(2)}, u32[]{:S(2)}) collective-permute-start(bf16[1584,128]{1,0:T(8,128)(2,1)S(1)} %get-tuple-element.48), channel_id=1, source_target_pairs={{0,128},{64,192},{128,0},{192,64},{1,129},{65,193},{129,1},{193,65... | collective-permute-start | bytes 1216520 | tf_op jit(solution)/shard_map/ppermute | solution.py:486
  16.3 19.4 %collective-permute-start.3 = (bf16[528,128]{1,0:T(8,128)(2,1)S(1)}, bf16[528,128]{1,0:T(8,128)(2,1)S(1)}, u32[]{:S(2)}, u32[]{:S(2)}) collective-permute-start(bf16[528,128]{1,0:T(8,128)(2,1)S(1)} %get-tuple-element.52), channel_id=1, source_target_pairs={{0,64},{64,128},{128,192},{192,0},{1,65},{65,129},{129,193},{193,1... | collective-permute-start | bytes 405512 | tf_op jit(solution)/shard_map/ppermute | solution.py:486
  18.3 17.4 %collective-permute-start.4 = (bf16[528,128]{1,0:T(8,128)(2,1)S(1)}, bf16[528,128]{1,0:T(8,128)(2,1)S(1)}, u32[]{:S(2)}, u32[]{:S(2)}) collective-permute-start(bf16[528,128]{1,0:T(8,128)(2,1)S(1)} %get-tuple-element.53), channel_id=1, source_target_pairs={{0,128},{64,192},{128,0},{192,64},{1,129},{65,193},{129,1},{193,65... | collective-permute-start | bytes 405512 | tf_op jit(solution)/shard_map/ppermute | solution.py:486
  21.0 14.7 %collective-permute-start.5 = (bf16[528,128]{1,0:T(8,128)(2,1)S(1)}, bf16[528,128]{1,0:T(8,128)(2,1)S(1)}, u32[]{:S(2)}, u32[]{:S(2)}) collective-permute-start(bf16[528,128]{1,0:T(8,128)(2,1)S(1)} %get-tuple-element.54), channel_id=1, source_target_pairs={{0,192},{64,0},{128,64},{192,128},{1,193},{65,1},{129,65},{193,129... | collective-permute-start | bytes 405512 | tf_op jit(solution)/shard_map/ppermute | solution.py:486
  27.9 8.9 %collective-permute-start.6 = (f32[16,128]{1,0:T(8,128)S(1)}, f32[16,128]{1,0:T(8,128)S(1)}, u32[]{:S(2)}, u32[]{:S(2)}) collective-permute-start(f32[16,128]{1,0:T(8,128)S(1)} %get-tuple-element.57), channel_id=1, source_target_pairs={{0,64},{128,192},{193,129},{65,1},{2,66},{130,194},{195,131},{67,3... | collective-permute-start | bytes 24584 | tf_op jit(solution)/shard_map/ppermute | solution.py:500
  28.3 8.6 %collective-permute-start.7 = (f32[16,128]{1,0:T(8,128)S(1)}, f32[16,128]{1,0:T(8,128)S(1)}, u32[]{:S(2)}, u32[]{:S(2)}) collective-permute-start(f32[16,128]{1,0:T(8,128)S(1)} %get-tuple-element.58), channel_id=1, source_target_pairs={{64,128},{192,193},{129,65},{1,2},{66,130},{194,195},{131,67},{3,4... | collective-permute-start | bytes 24584 | tf_op jit(solution)/shard_map/ppermute | solution.py:500
  38.5 6.6 %collective-permute-start.8 = (f32[16,128]{1,0:T(8,128)S(1)}, f32[16,128]{1,0:T(8,128)S(1)}, u32[]{:S(2)}, u32[]{:S(2)}) collective-permute-start(f32[16,128]{1,0:T(8,128)S(1)} %get-tuple-element.60), channel_id=1, source_target_pairs={{0,64},{128,192},{193,129},{65,1},{2,66},{130,194},{195,131},{67,3... | collective-permute-start | bytes 24584 | tf_op jit(solution)/shard_map/ppermute | solution.py:500
  38.8 6.6 %collective-permute-start.9 = (f32[16,128]{1,0:T(8,128)S(1)}, f32[16,128]{1,0:T(8,128)S(1)}, u32[]{:S(2)}, u32[]{:S(2)}) collective-permute-start(f32[16,128]{1,0:T(8,128)S(1)} %get-tuple-element.61), channel_id=1, source_target_pairs={{64,128},{192,193},{129,65},{1,2},{66,130},{194,195},{131,67},{3,4... | collective-permute-start | bytes 24584 | tf_op jit(solution)/shard_map/ppermute | solution.py:500
  46.1 22.4 %all-to-all-start = ((f32[64,1,128]{2,1,0:T(1,128)}), f32[64,1,128]{2,1,0:T(1,128)S(1)}, u32[]{:S(2)}, u32[]{:S(2)}) async-start(f32[64,1,128]{2,1,0:T(1,128)} %bitcast.6), calls=%async_computation | async-start | bytes 65536 | tf_op jit(solution)/shard_map/all_to_all | solution.py:564
  60.7 10.3 %collective-permute-start.13 = (f32[80,128]{1,0:T(8,128)S(1)}, f32[80,128]{1,0:T(8,128)S(1)}, u32[]{:S(2)}, u32[]{:S(2)}) collective-permute-start(f32[80,128]{1,0:T(8,128)S(1)} %get-tuple-element.68), channel_id=1, source_target_pairs={{0,64},{64,128},{128,192},{192,0},{1,65},{65,129},{129,193},{193,1... | collective-permute-start | bytes 122888 | tf_op jit(solution)/shard_map/ppermute | solution.py:486
  61.4 9.7 %collective-permute-start.14 = (f32[80,128]{1,0:T(8,128)S(1)}, f32[80,128]{1,0:T(8,128)S(1)}, u32[]{:S(2)}, u32[]{:S(2)}) collective-permute-start(f32[80,128]{1,0:T(8,128)S(1)} %get-tuple-element.69), channel_id=1, source_target_pairs={{0,128},{64,192},{128,0},{192,64},{1,129},{65,193},{129,1},{193,65... | collective-permute-start | bytes 122888 | tf_op jit(solution)/shard_map/ppermute | solution.py:486
  62.1 9.0 %collective-permute-start.15 = (f32[80,128]{1,0:T(8,128)S(1)}, f32[80,128]{1,0:T(8,128)S(1)}, u32[]{:S(2)}, u32[]{:S(2)}) collective-permute-start(f32[80,128]{1,0:T(8,128)S(1)} %get-tuple-element.70), channel_id=1, source_target_pairs={{0,192},{64,0},{128,64},{192,128},{1,193},{65,1},{129,65},{193,129... | collective-permute-start | bytes 122888 | tf_op jit(solution)/shard_map/ppermute | solution.py:486
  68.6 2.8 %collective-permute-start.12 = (f32[8,128]{1,0:T(8,128)S(1)}, f32[8,128]{1,0:T(8,128)S(1)}, u32[]{:S(2)}, u32[]{:S(2)}) collective-permute-start(f32[8,128]{1,0:T(8,128)S(1)} %fold.1.s0), channel_id=1, source_target_pairs={{0,192},{64,0},{128,64},{192,128},{1,193},{65,1},{129,65},{193,129... | collective-permute-start | bytes 12296 | tf_op jit(solution)/shard_map/ppermute | solution.py:486
  68.7 4.0 %collective-permute-start.11 = (f32[8,128]{1,0:T(8,128)S(1)}, f32[8,128]{1,0:T(8,128)S(1)}, u32[]{:S(2)}, u32[]{:S(2)}) collective-permute-start(f32[8,128]{1,0:T(8,128)S(1)} %fold.1.s0), channel_id=1, source_target_pairs={{0,128},{64,192},{128,0},{192,64},{1,129},{65,193},{129,1},{193,65... | collective-permute-start | bytes 12296 | tf_op jit(solution)/shard_map/ppermute | solution.py:486
  71.0 3.7 %collective-permute-start.10 = (f32[8,128]{1,0:T(8,128)S(1)}, f32[8,128]{1,0:T(8,128)S(1)}, u32[]{:S(2)}, u32[]{:S(2)}) collective-permute-start(f32[8,128]{1,0:T(8,128)S(1)} %fold.1.s0), channel_id=1, source_target_pairs={{0,64},{64,128},{128,192},{192,0},{1,65},{65,129},{129,193},{193,1... | collective-permute-start | bytes 12296 | tf_op jit(solution)/shard_map/ppermute | solution.py:486
